TPU v7x, 32 devices: a whole 2x2x4 slice. The times are simulated.
32 devices in a mesh: rows: 8 (over y, x, core), feat: 4 (over z).
Axes of the slice: x: 2, y: 2, z: 4, core: 2. Of those that a mesh axis runs over, the one named last changes fastest.
Arguments:
- tokens: bfloat16 [8192, 1024], P(('rows', 'feat')), may hold values from -6 to 6
- cotangent: bfloat16 [8192, 1024], P(('rows', 'feat')), may hold values from -6 to 6
- image_length: int32 [32], replicated, may hold values from 0 to 7168, as said below
- image_start: int32 [32], replicated, may hold values from 0 to 8192, as said below
- norm_gain: float32 [2, 2, 1024], replicated, may hold values from 0.5 to 1.5
- norm_bias: float32 [2, 2, 1024], replicated, may hold values from -1 to 1
- weight_in: bfloat16 [2, 1024, 3, 1024], P(None, None, None, 'feat'), may hold values from -0.1875 to 0.1875
- weight_mix: bfloat16 [2, 1024, 1024], P(None, None, 'feat'), may hold values from -1.5 to 1.5
- weight_up: bfloat16 [2, 1024, 4096], P(None, None, 'feat'), may hold values from -0.1875 to 0.1875
- weight_down: bfloat16 [2, 1024, 4096], P(None, None, 'feat'), may hold values from -0.09375 to 0.09375
Outputs:
- output: bfloat16 [8192, 1024], P(('rows', 'feat'))
- grad_input: float32 [8192, 1024], P(('rows', 'feat'))
- grad_gain: float32 [2, 2, 1024], replicated
- grad_bias: float32 [2, 2, 1024], replicated
- grad_bias_top: float32 [1024], replicated
- grad_in: float32 [2, 1024, 3, 1024], P(None, 'rows', None, 'feat')
- grad_mix: float32 [2, 1024, 1024], P(None, 'rows', 'feat')
- grad_up: float32 [2, 1024, 4096], P(None, 'rows', 'feat')
- grad_down: float32 [2, 1024, 4096], P(None, 'rows', 'feat')
- log_max: float32 [], replicated
- log_mean: float32 [], replicated
Inputs may be any that keep to these rules, and one draw needn't show every extreme that they name: `image_length`: images lie end to end from pixel 0 in order: each image_start is the previous start plus the previous length. One image has 7168 pixels; every other live image has 256 pixels, at least one before the long image and at least one after it. Entries after the last image have length 0. `image_start`: entries after the last image start at 8192.
All inputs are finite; a program needn't handle non-finite values.
Results may differ from a plain program's by a relative error of at most 0.017.
Values may be sent and summed in bfloat16 or wider, within the bound.
A program may use at most 192 MiB of HBM per device.

v0:
```python
from functools import partial

import jax
import jax.numpy as jnp
from jax import lax
from jax.sharding import PartitionSpec as P

HEADS = 16
HD = 64
LAYERS = 2
BLK = 512


EPS_NORM = 1e-05
EPS_DEN = 1e-06
HIGHEST = lax.Precision.HIGHEST


def carried_in(array, axis, join, neutral):
    place = lax.axis_index(axis)
    gathered = jax.tree.map(
        lambda a, kind: lax.all_gather(a.astype(kind), axis),
        array,
        (jnp.bfloat16, jnp.bfloat16, jnp.bfloat16),
    )
    state = jax.tree.map(lambda a, e: jnp.zeros_like(a) + jnp.asarray(e, a.dtype), array, neutral)

    def one(step, state):
        return join(
            state,
            jax.tree.map(
                lambda a, own: lax.dynamic_index_in_dim(a, step, 0, False).astype(own.dtype),
                gathered,
                array,
            ),
        )

    return lax.fori_loop(0, place, one, state)


def entering(array, axis, combine, identity):
    peers, mine = (lax.axis_size(axis), lax.axis_index(axis))
    everything = jax.tree.map(
        lambda part, kind: lax.all_gather(part.astype(kind), axis),
        array,
        jax.tree.map(lambda a: jnp.bfloat16 if a.dtype == jnp.float32 else a.dtype, array),
    )
    start = jax.tree.map(
        lambda part, zero: jnp.broadcast_to(jnp.asarray(zero, part.dtype), part.shape),
        array,
        identity,
    )

    def step(k, before):
        at = peers - 1 - k
        reached = at > mine
        new = combine(
            before, jax.tree.map(lambda part, own: part[at].astype(own.dtype), everything, array)
        )
        return jax.tree.map(lambda a, b: jnp.where(reached, a, b), new, before)

    return lax.fori_loop(0, peers, step, start)


def layer_norm(values, gain, bias):
    center = jnp.mean(values, axis=-1, keepdims=True)
    shifted = values - center
    spread = jnp.mean(shifted * shifted, axis=-1, keepdims=True)
    return shifted * lax.rsqrt(spread + EPS_NORM) * gain + bias


def feature(values):
    return jax.nn.elu(values) + 1.0


def image_rows(image_length, image_start, first, count):
    positions = first + jnp.arange(count, dtype=jnp.int32)
    live = (image_length > 0)[None, :]
    begun = (image_start[None, :] <= positions[:, None]) & live
    segment = jnp.sum(begun.astype(jnp.int32), axis=1) - 1
    opening = jnp.any((image_start[None, :] == positions[:, None]) & live, axis=1)
    return (segment, opening)


def block_masks(segment, opening):
    order = jnp.arange(segment.shape[0])
    same = ((segment[:, None] == segment[None, :]) & (order[None, :] <= order[:, None])).astype(
        jnp.float32
    )
    carried = ((segment == segment[0]) & jnp.logical_not(opening[0])).astype(jnp.float32)
    last = (segment == segment[-1]).astype(jnp.float32)
    return (same, carried, last)


def in_blocks(array, blocks):
    return array.reshape((blocks, array.shape[0] // blocks) + array.shape[1:])


def block_forward(carry, block):
    state, total = carry
    query_block, key_block, value_block, segment, opening = block
    same, carried, last = block_masks(segment, opening)
    scores = (
        jnp.einsum("ihc,jhc->hij", query_block, key_block, preferred_element_type=jnp.float32)
        * same[None]
    )
    weights = scores.astype(jnp.bfloat16)
    query_wide = query_block.astype(jnp.float32)
    numerator = jnp.einsum("hij,jhe->ihe", weights, value_block, preferred_element_type=jnp.float32)
    numerator = numerator + carried[:, None, None] * jnp.einsum(
        "ihc,hce->ihe", query_wide, state, precision=HIGHEST
    )
    denominator = (
        jnp.sum(scores, axis=2).T
        + carried[:, None] * jnp.einsum("ihc,hc->ih", query_wide, total, precision=HIGHEST)
        + EPS_DEN
    )
    keep = carried[-1]
    masked = key_block * last[:, None, None].astype(jnp.bfloat16)
    state_next = keep * state + jnp.einsum(
        "jhc,jhe->hce", masked, value_block, preferred_element_type=jnp.float32
    )
    total_next = keep * total + jnp.sum(masked.astype(jnp.float32), axis=0)
    return (
        (state_next, total_next),
        (numerator / denominator[:, :, None], denominator, state, total),
    )


def block_backward(carry, block):
    state_grad, total_grad = carry
    (
        query_block,
        key_block,
        value_block,
        segment,
        opening,
        state,
        total,
        numerator_grad,
        denominator_grad,
    ) = block
    same, carried, last = block_masks(segment, opening)
    query_wide = query_block.astype(jnp.float32)
    key_wide = key_block.astype(jnp.float32)
    value_wide = value_block.astype(jnp.float32)
    numerator_wide = numerator_grad.astype(jnp.float32)
    scores = (
        jnp.einsum("ihc,jhc->hij", query_block, key_block, preferred_element_type=jnp.float32)
        * same[None]
    )
    weights = scores.astype(jnp.bfloat16)
    weight_grad = jnp.einsum(
        "ihe,jhe->hij", numerator_grad, value_block, preferred_element_type=jnp.float32
    )
    score_grad = ((weight_grad + denominator_grad.T[:, :, None]) * same[None]).astype(jnp.bfloat16)
    value_grad = jnp.einsum(
        "hij,ihe->jhe", weights, numerator_grad, preferred_element_type=jnp.float32
    )
    query_grad = jnp.einsum(
        "hij,jhc->ihc", score_grad, key_block, preferred_element_type=jnp.float32
    )
    query_grad = query_grad + carried[:, None, None] * (
        jnp.einsum("ihe,hce->ihc", numerator_wide, state, precision=HIGHEST)
        + denominator_grad[:, :, None] * total[None]
    )
    key_grad = jnp.einsum(
        "hij,ihc->jhc", score_grad, query_block, preferred_element_type=jnp.float32
    )
    last_wide = last[:, None, None]
    key_grad = key_grad + last_wide * (
        jnp.einsum("hce,jhe->jhc", state_grad, value_wide, precision=HIGHEST) + total_grad[None]
    )
    value_grad = value_grad + last_wide * jnp.einsum(
        "jhc,hce->jhe", key_wide, state_grad, precision=HIGHEST
    )
    keep = carried[-1]
    state_prior = keep * state_grad + jnp.einsum(
        "ihc,ihe->hce", query_wide * carried[:, None, None], numerator_wide, precision=HIGHEST
    )
    total_prior = keep * total_grad + jnp.einsum(
        "ih,ihc->hc", denominator_grad * carried[:, None], query_wide, precision=HIGHEST
    )
    return ((state_prior, total_prior), (query_grad, key_grad, value_grad))


def rows_times(left, weight):
    return jnp.einsum("te,de->td", left, weight, preferred_element_type=jnp.float32)


def gather_rows(normed):
    return lax.all_gather(normed, "feat", axis=0, tiled=True)


def sum_branch(left, weight):
    return lax.psum_scatter(
        rows_times(left, weight).astype(jnp.bfloat16), "feat", scatter_dimension=0, tiled=True
    ).astype(jnp.float32)


def gather_grads(gradient):
    return lax.all_gather(gradient, "feat", axis=0, tiled=True)


def sum_inputs(left, weight):
    return lax.psum_scatter(
        rows_times(left, weight).astype(jnp.bfloat16), "feat", scatter_dimension=0, tiled=True
    ).astype(jnp.float32)


def join_forward(earlier, later):
    return (
        jnp.maximum(earlier[0], later[0]),
        later[1] + (1.0 - later[0]) * earlier[1],
        later[2] + (1.0 - later[0]) * earlier[2],
    )


def join_backward(earlier, later):
    return (
        earlier[0] * later[0],
        later[1] + later[0] * earlier[1],
        later[2] + later[0] * earlier[2],
    )


def carry_in(reset, aggregate, aggregate_total):
    identity = (
        jnp.zeros((), jnp.float32),
        jnp.zeros_like(aggregate),
        jnp.zeros_like(aggregate_total),
    )
    _, state_in, total_in = carried_in(
        (reset, aggregate, aggregate_total), "rows", join_forward, identity
    )
    return (state_in, total_in)


def carry_back(keep, direct_state, direct_total):
    identity = (
        jnp.ones((), jnp.float32),
        jnp.zeros_like(direct_state),
        jnp.zeros_like(direct_total),
    )
    _, state_after, total_after = entering(
        (keep, direct_state, direct_total), "rows", join_backward, identity
    )
    return (state_after, total_after)


def local(
    tokens,
    cotangent,
    image_length,
    image_start,
    norm_gain,
    norm_bias,
    weight_in,
    weight_mix,
    weight_up,
    weight_down,
):
    local_rows = tokens.shape[0]
    shard_rows = local_rows * lax.axis_size("feat")
    all_rows = shard_rows * lax.axis_size("rows")
    width = weight_mix.shape[2]
    heads_here = width // HD
    blocks = shard_rows // BLK
    segment, opening = image_rows(
        image_length, image_start, lax.axis_index("rows") * shard_rows, shard_rows
    )
    reaching = ((segment == segment[0]) & jnp.logical_not(opening[0])).astype(jnp.float32)
    last_shard = (segment == segment[-1]).astype(jnp.bfloat16)
    keep_shard = reaching[-1]
    reset = 1.0 - keep_shard
    segment_blocks = in_blocks(segment, blocks)
    opening_blocks = in_blocks(opening, blocks)
    stream = tokens.astype(jnp.float32)
    kept = []
    log_total = jnp.zeros((), jnp.float32)
    log_top = jnp.full((), -jnp.inf, jnp.float32)
    for level in range(LAYERS):
        gain = norm_gain[level]
        bias = norm_bias[level]
        normed_all = gather_rows(layer_norm(stream, gain[0], bias[0]).astype(jnp.bfloat16))
        projected = jnp.einsum(
            "td,dke->tke", normed_all, weight_in[level], preferred_element_type=jnp.float32
        )
        query_feat = (
            feature(projected[:, 0]).astype(jnp.bfloat16).reshape(shard_rows, heads_here, HD)
        )
        key_feat = feature(projected[:, 1]).astype(jnp.bfloat16).reshape(shard_rows, heads_here, HD)
        values = projected[:, 2].astype(jnp.bfloat16).reshape(shard_rows, heads_here, HD)
        masked_keys = key_feat * last_shard[:, None, None]
        aggregate = jnp.einsum(
            "thc,the->hce", masked_keys, values, preferred_element_type=jnp.float32
        )
        aggregate_total = jnp.sum(masked_keys.astype(jnp.float32), axis=0)
        state_in, total_in = carry_in(reset, aggregate, aggregate_total)
        pieces = (
            in_blocks(query_feat, blocks),
            in_blocks(key_feat, blocks),
            in_blocks(values, blocks),
            segment_blocks,
            opening_blocks,
        )
        _, (ratio, denominator, states, totals) = lax.scan(
            block_forward, (state_in, total_in), pieces
        )
        ratio = ratio.reshape(shard_rows, heads_here, HD)
        denominator = denominator.reshape(shard_rows, heads_here)
        mixed = ratio.reshape(shard_rows, width).astype(jnp.bfloat16)
        middle = stream + sum_branch(mixed, weight_mix[level])
        normed_mid = gather_rows(layer_norm(middle, gain[1], bias[1]).astype(jnp.bfloat16))
        upward = jnp.dot(normed_mid, weight_up[level], preferred_element_type=jnp.float32)
        active = jax.nn.gelu(upward, approximate=False).astype(jnp.bfloat16)
        kept.append(
            (
                stream,
                normed_all,
                projected,
                query_feat,
                key_feat,
                values,
                ratio,
                denominator,
                states,
                totals,
                mixed,
                middle,
                normed_mid,
                upward,
                active,
            )
        )
        stream = middle + sum_branch(active, weight_down[level])
        logs = jnp.log(denominator)
        log_total = log_total + jnp.sum(logs)
        log_top = jnp.maximum(log_top, jnp.max(logs))
    output = stream.astype(jnp.bfloat16)
    gradient = cotangent.astype(jnp.float32)
    gain_parts = []
    bias_parts = []
    weight_parts = []
    for level in reversed(range(LAYERS)):
        (
            stream_in,
            normed_all,
            projected,
            query_feat,
            key_feat,
            values,
            ratio,
            denominator,
            states,
            totals,
            mixed,
            middle,
            normed_mid,
            upward,
            active,
        ) = kept[level]
        gain = norm_gain[level]
        bias = norm_bias[level]
        down_grad = gather_grads(gradient.astype(jnp.bfloat16))
        grad_down = jnp.einsum("td,tf->df", down_grad, active, preferred_element_type=jnp.float32)
        active_grad = jnp.dot(down_grad, weight_down[level], preferred_element_type=jnp.float32)
        _, gelu_back = jax.vjp(partial(jax.nn.gelu, approximate=False), upward)
        upward_grad = gelu_back(active_grad)[0].astype(jnp.bfloat16)
        grad_up = jnp.einsum(
            "td,tf->df", normed_mid, upward_grad, preferred_element_type=jnp.float32
        )
        _, norm_late = jax.vjp(layer_norm, middle, gain[1], bias[1])
        middle_part, gain_late, bias_late = norm_late(sum_inputs(upward_grad, weight_up[level]))
        middle_grad = gradient + middle_part
        mix_grad = gather_grads(middle_grad.astype(jnp.bfloat16))
        grad_mix = jnp.einsum("td,te->de", mix_grad, mixed, preferred_element_type=jnp.float32)
        ratio_grad = jnp.dot(
            mix_grad, weight_mix[level], preferred_element_type=jnp.float32
        ).astype(jnp.bfloat16)
        ratio_grad = ratio_grad.astype(jnp.float32).reshape(shard_rows, heads_here, HD)
        numerator_grad = (ratio_grad / denominator[:, :, None]).astype(jnp.bfloat16)
        numerator_wide = numerator_grad.astype(jnp.float32)
        denominator_grad = -jnp.sum(ratio_grad * ratio, axis=2) / denominator
        query_wide = query_feat.astype(jnp.float32)
        direct_state = jnp.einsum(
            "thc,the->hce", query_wide * reaching[:, None, None], numerator_wide, precision=HIGHEST
        )
        direct_total = jnp.einsum(
            "th,thc->hc", denominator_grad * reaching[:, None], query_wide, precision=HIGHEST
        )
        state_after, total_after = carry_back(keep_shard, direct_state, direct_total)
        pieces = (
            in_blocks(query_feat, blocks),
            in_blocks(key_feat, blocks),
            in_blocks(values, blocks),
            segment_blocks,
            opening_blocks,
            states,
            totals,
            in_blocks(numerator_grad, blocks),
            in_blocks(denominator_grad, blocks),
        )
        _, (query_grad, key_grad, value_grad) = lax.scan(
            block_backward, (state_after, total_after), pieces, reverse=True
        )
        query_grad = query_grad.reshape(shard_rows, width)
        key_grad = key_grad.reshape(shard_rows, width)
        value_grad = value_grad.reshape(shard_rows, 1, width)
        _, feature_back = jax.vjp(feature, projected[:, :2])
        front_grad = feature_back(jnp.stack([query_grad, key_grad], axis=1))[0]
        projected_grad = jnp.concatenate(
            [front_grad.astype(jnp.bfloat16), value_grad.astype(jnp.bfloat16)], axis=1
        )
        grad_in = jnp.einsum(
            "td,tke->dke", normed_all, projected_grad, preferred_element_type=jnp.float32
        )
        flat_weight = weight_in[level].reshape(weight_in.shape[1], 3 * width)
        _, norm_early = jax.vjp(layer_norm, stream_in, gain[0], bias[0])
        stream_part, gain_early, bias_early = norm_early(
            sum_inputs(projected_grad.reshape(shard_rows, 3 * width), flat_weight)
        )
        gradient = middle_grad + stream_part
        gain_parts.insert(0, jnp.stack([gain_early, gain_late]))
        bias_parts.insert(0, jnp.stack([bias_early, bias_late]))
        weight_parts.insert(0, (grad_in, grad_mix, grad_up, grad_down))
    first_layer, second_layer = weight_parts
    summed = (
        lax.psum_scatter(
            first_layer[0].astype(jnp.bfloat16), "rows", scatter_dimension=0, tiled=True
        ).astype(jnp.float32),
        lax.psum_scatter(
            first_layer[1].astype(jnp.bfloat16), "rows", scatter_dimension=0, tiled=True
        ).astype(jnp.float32),
        lax.psum_scatter(
            first_layer[2].astype(jnp.bfloat16), "rows", scatter_dimension=0, tiled=True
        ).astype(jnp.float32),
        lax.psum_scatter(
            first_layer[3].astype(jnp.bfloat16), "rows", scatter_dimension=0, tiled=True
        ).astype(jnp.float32),
        lax.psum_scatter(
            second_layer[0].astype(jnp.bfloat16), "rows", scatter_dimension=0, tiled=True
        ).astype(jnp.float32),
        lax.psum_scatter(
            second_layer[1].astype(jnp.bfloat16), "rows", scatter_dimension=0, tiled=True
        ).astype(jnp.float32),
        lax.psum_scatter(
            second_layer[2].astype(jnp.bfloat16), "rows", scatter_dimension=0, tiled=True
        ).astype(jnp.float32),
        lax.psum_scatter(
            second_layer[3].astype(jnp.bfloat16), "rows", scatter_dimension=0, tiled=True
        ).astype(jnp.float32),
    )
    weight_parts = [summed[0:4], summed[4:8]]
    gain_sum, bias_sum, log_sum = lax.psum(
        (jnp.stack(gain_parts), jnp.stack(bias_parts), log_total), ("rows", "feat")
    )
    log_max = lax.pmax(log_top, ("rows", "feat"))
    log_mean = log_sum / (all_rows * HEADS * LAYERS)
    return (
        output,
        gradient,
        gain_sum,
        bias_sum,
        bias_sum[LAYERS - 1, 1],
        jnp.stack([part[0] for part in weight_parts]),
        jnp.stack([part[1] for part in weight_parts]),
        jnp.stack([part[2] for part in weight_parts]),
        jnp.stack([part[3] for part in weight_parts]),
        log_max,
        log_mean,
    )


def solution(mesh):
    placed = (
        P(("rows", "feat"), None),
        P(("rows", "feat"), None),
        P(),
        P(),
        P(),
        P(),
        P(None, None, None, "feat"),
        P(None, None, "feat"),
        P(None, None, "feat"),
        P(None, None, "feat"),
    )
    return jax.shard_map(
        local,
        mesh=mesh,
        in_specs=placed,
        out_specs=(
            P(("rows", "feat"), None),
            P(("rows", "feat"), None),
            P(),
            P(),
            P(),
            P(None, "rows", None, "feat"),
            P(None, "rows", "feat"),
            P(None, "rows", "feat"),
            P(None, "rows", "feat"),
            P(),
            P(),
        ),
        check_vma=False,
    )
```

profile of v0, /device:TPU:0, one launch (start us, length us, event | category | flops | bytes accessed | tf_op | source)
XLA Modules:
  0.0 1490.3 jit_solution(3401779635067275458)
XLA Ops:
  24.6 16.5 %all-reduce.3 = (bf16[8]{0:T(256)(128)(2,1)S(1)}, bf16[8]{0:T(256)(128)(2,1)}) all-reduce(bf16[8]{0:T(256)(128)(2,1)S(1)} %dynamic-update-slice, bf16[8]{0:T(256)(128)(2,1)S(1)} %dynamic-update-slice.1), channel_id=1, replica_groups=mesh['rows'=8,'feat'=4] {'rows'}, use_global_device_ids=true, to_apply=%add | all-reduce | flops 16 | bytes 64
  41.7 21.0 %all-gather.17.cloned.1.call-done = bf16[1024,1024]{1,0:T(8,128)(2,1)} async-done(((bf16[256,1024]{1,0:T(8,128)(2,1)}), bf16[1024,1024]{1,0:T(8,128)(2,1)}) %all-gather.17.cloned.1.call-update) | async-done | bytes 2097168 | tf_op jit(solution)/shard_map/all_gather | solution.py:192
  62.7 3.9 fusion.238
  71.0 10.1 all-gather
  81.2 8.6 all_gather.89
  93.4 16.6 %while.149 = (s32[]{:T(128)}, f32[4,64,64]{2,1,0:T(8,128)S(1)}, f32[4,64]{1,0:T(4,128)S(1)}, f32[2,512,4,64]{1,3,2,0:T(8,128)S(1)}, f32[2,512,4]{1,2,0:T(4,128)S...) while((s32[]{:T(128)}, f32[4,64,64]{2,1,0:T(8,128)S(1)}, ...), condition=%wide.region_10.11_spmd, body=%wide.region_7.10_spmd.sunk | while | flops 393655552 | bytes 15901416 | solution.py:307
  115.6 51.2 %reduce-scatter.17.cloned.1.call-done = bf16[256,1024]{1,0:T(8,128)(2,1)} async-done(((bf16[1024,1024]{1,0:T(8,128)(2,1)}), bf16[256,1024]{1,0:T(8,128)(2,1)}) %reduce-scatter.17.cloned.1.call-update) | async-done | bytes 524304 | tf_op jit(solution)/shard_map/reduce_scatter | solution.py:196
  171.9 45.1 %all-gather.19.cloned.1.call-done = bf16[1024,1024]{1,0:T(8,128)(2,1)} async-done(((bf16[256,1024]{1,0:T(8,128)(2,1)}), bf16[1024,1024]{1,0:T(8,128)(2,1)}) %all-gather.19.cloned.1.call-update) | async-done | bytes 2097168 | tf_op jit(solution)/shard_map/all_gather | solution.py:192
  217.0 14.9 %multiply_convert_fusion.29 = (bf16[1024,1024]{1,0:T(8,128)(2,1)S(1)}, f32[1024,1024]{1,0:T(8,128)}, f32[1024,1024]{1,0:T(8,128)}) fusion(bf16[1024,1024]{1,0:T(8,128)(2,1)} %all-gather.19.cloned.1.call-done, bf16[2,1024,1024]{2,1,0:T(8,128)(2,1)} %param.34), kind=kOutput, calls=%fused_computation.289 | convolution fusion | flops 2215641088 | bytes 14680064 | tf_op jit(solution)/shard_map/dot_general | solution.py:315
  233.2 3.7 fusion.243
  237.0 42.7 %reduce-scatter.19.cloned.1.call-done = bf16[256,1024]{1,0:T(8,128)(2,1)} async-done(((bf16[1024,1024]{1,0:T(8,128)(2,1)}), bf16[256,1024]{1,0:T(8,128)(2,1)}) %reduce-scatter.19.cloned.1.call-update) | async-done | bytes 524304 | tf_op jit(solution)/shard_map/reduce_scatter | solution.py:196
  282.9 44.9 %all-gather.21.cloned.1.call-done = bf16[1024,1024]{1,0:T(8,128)(2,1)} async-done(((bf16[256,1024]{1,0:T(8,128)(2,1)}), bf16[1024,1024]{1,0:T(8,128)(2,1)}) %all-gather.21.cloned.1.call-update) | async-done | bytes 2097168 | tf_op jit(solution)/shard_map/all_gather | solution.py:192
  327.8 3.9 fusion.224
  343.6 9.8 all-gather.1
  353.5 8.8 all_gather.95
  363.4 28.3 %while.151 = (s32[]{:T(128)}, f32[4,64,64]{2,1,0:T(8,128)S(1)}, f32[4,64]{1,0:T(4,128)S(1)}, f32[2,512,4,64]{1,3,2,0:T(8,128)S(1)}, f32[2,512,4]{1,2,0:T(4,128)S...) while((s32[]{:T(128)}, f32[4,64,64]{2,1,0:T(8,128)S(1)}, ...), condition=%wide.region_23.24_spmd, body=%wide.region_20.23_spmd.sunk | while | flops 393655552 | bytes 15770336 | solution.py:307
  392.4 3.3 convolution_convert_fusion.3
  395.8 51.0 %reduce-scatter.21.cloned.1.call-done = bf16[256,1024]{1,0:T(8,128)(2,1)} async-done(((bf16[1024,1024]{1,0:T(8,128)(2,1)}), bf16[256,1024]{1,0:T(8,128)(2,1)}) %reduce-scatter.21.cloned.1.call-update) | async-done | bytes 524304 | tf_op jit(solution)/shard_map/reduce_scatter | solution.py:196
  450.4 44.5 %all-gather.23.cloned.1.call-done = bf16[1024,1024]{1,0:T(8,128)(2,1)} async-done(((bf16[256,1024]{1,0:T(8,128)(2,1)}), bf16[1024,1024]{1,0:T(8,128)(2,1)}) %all-gather.23.cloned.1.call-update) | async-done | bytes 2097168 | tf_op jit(solution)/shard_map/all_gather | solution.py:192
  494.9 14.8 multiply_convert_fusion.28
  509.6 31.5 %all-gather.25.cloned.1.call-done = bf16[1024,1024]{1,0:T(8,128)(2,1)} async-done(((bf16[256,1024]{1,0:T(8,128)(2,1)}), bf16[1024,1024]{1,0:T(8,128)(2,1)}) %all-gather.25.cloned.1.call-update) | async-done | bytes 2097168 | tf_op jit(solution)/shard_map/all_gather | solution.py:202
  541.1 8.1 add_convert_fusion.1
  550.6 3.8 fusion.246
  554.7 5.3 fusion.249
  560.0 37.2 %reduce-scatter.25.cloned.1.call-done = bf16[256,1024]{1,0:T(8,128)(2,1)} async-done(((bf16[1024,1024]{1,0:T(8,128)(2,1)}), bf16[256,1024]{1,0:T(8,128)(2,1)}) %reduce-scatter.25.cloned.1.call-update) | async-done | bytes 524304 | tf_op jit(solution)/shard_map/reduce_scatter | solution.py:206
  599.3 43.3 %reduce-scatter.23.cloned.1.call-done = bf16[256,1024]{1,0:T(8,128)(2,1)} async-done(((bf16[1024,1024]{1,0:T(8,128)(2,1)}), bf16[256,1024]{1,0:T(8,128)(2,1)}) %reduce-scatter.23.cloned.1.call-update) | async-done | bytes 524304 | tf_op jit(solution)/shard_map/reduce_scatter | solution.py:196
  648.7 3.3 fusion.392
  654.8 37.6 %all-gather.27.cloned.1.call-done = bf16[1024,1024]{1,0:T(8,128)(2,1)} async-done(((bf16[256,1024]{1,0:T(8,128)(2,1)}), bf16[1024,1024]{1,0:T(8,128)(2,1)}) %all-gather.27.cloned.1.call-update) | async-done | bytes 2097168 | tf_op jit(solution)/shard_map/all_gather | solution.py:202
  702.7 8.9 all-gather.6
  713.3 10.0 all-gather.2
  723.4 10.8 while.154
  736.7 92.8 %while.152 = (s32[]{:T(128)}, f32[4,64,64]{2,1,0:T(8,128)S(1)}, f32[4,64]{1,0:T(4,128)S(1)}, f32[2,512,4,64]{1,0,3,2:T(2,128)}, f32[2,512,4,64]{1,0,3,2:T(2,128)...) while((s32[]{:T(128)}, f32[4,64,64]{2,1,0:T(8,128)S(1)}, ...), condition=%wide.region_35.36_spmd, body=%wide.region_34.35_spmd.sunk | while | flops 1083085824 | bytes 24459148 | solution.py:404
  749.9 10.4 dynamic_update_slice.115
  763.6 10.4 dynamic_update_slice.116
  796.1 10.4 dynamic_update_slice.115
  809.8 10.4 dynamic_update_slice.116
  849.6 41.8 %reduce-scatter.27.cloned.1.call-done = bf16[256,1024]{1,0:T(8,128)(2,1)} async-done(((bf16[1024,1024]{1,0:T(8,128)(2,1)}), bf16[256,1024]{1,0:T(8,128)(2,1)}) %reduce-scatter.27.cloned.1.call-update) | async-done | bytes 524304 | tf_op jit(solution)/shard_map/reduce_scatter | solution.py:206
  898.4 45.2 %all-gather.29.cloned.1.call-done = bf16[1024,1024]{1,0:T(8,128)(2,1)} async-done(((bf16[256,1024]{1,0:T(8,128)(2,1)}), bf16[1024,1024]{1,0:T(8,128)(2,1)}) %all-gather.29.cloned.1.call-update) | async-done | bytes 2097168 | tf_op jit(solution)/shard_map/all_gather | solution.py:202
  943.6 8.1 add_convert_fusion
  953.1 3.8 fusion.240
  956.9 42.7 %reduce-scatter.29.cloned.1.call-done = bf16[256,1024]{1,0:T(8,128)(2,1)} async-done(((bf16[1024,1024]{1,0:T(8,128)(2,1)}), bf16[256,1024]{1,0:T(8,128)(2,1)}) %reduce-scatter.29.cloned.1.call-update) | async-done | bytes 524304 | tf_op jit(solution)/shard_map/reduce_scatter | solution.py:206
  1006.4 5.9 convert_bitcast_fusion
  1012.4 6.3 convolution_convert_fusion
  1019.0 5.3 convolution_convert_fusion.1
  1024.4 6.1 convolution_convert_fusion.2
  1032.2 19.5 %all-gather.31.cloned.1.call-done = bf16[1024,1024]{1,0:T(8,128)(2,1)} async-done(((bf16[256,1024]{1,0:T(8,128)(2,1)}), bf16[1024,1024]{1,0:T(8,128)(2,1)}) %all-gather.31.cloned.1.call-update) | async-done | bytes 2097168 | tf_op jit(solution)/shard_map/all_gather | solution.py:202
  1056.0 4.7 fusion.263
  1067.8 8.8 all-gather.7
  1078.5 10.2 all-gather.4
  1088.7 10.9 while.155
  1102.1 89.2 %while.153 = (s32[]{:T(128)}, f32[4,64,64]{2,1,0:T(8,128)S(1)}, f32[4,64]{1,0:T(4,128)S(1)}, f32[2,512,4,64]{1,0,3,2:T(2,128)}, f32[2,512,4,64]{1,0,3,2:T(2,128)...) while((s32[]{:T(128)}, f32[4,64,64]{2,1,0:T(8,128)S(1)}, ...), condition=%wide.region_46.47_spmd, body=%wide.region_45.46_spmd.sunk | while | flops 1083085824 | bytes 26555820 | solution.py:404
  1115.5 10.4 dynamic_update_slice.118
  1129.3 10.4 dynamic_update_slice.119
  1160.0 10.4 dynamic_update_slice.118
  1173.7 10.4 dynamic_update_slice.119
  1194.4 3.3 stack_reshape.15
  1211.7 4.6 convolution_convert_fusion.5
  1220.2 9.4 reduce-scatter.41.cloned.1.call-done
  1231.7 39.3 %pmax.7 = f32[]{:T(128)} all-reduce(f32[]{:T(128)S(6)} %max.5), channel_id=1, replica_groups=mesh['rows'=8,'feat'=4] {'rows','feat'}, use_global_device_ids=true, to_apply=%region_70.71 | all-reduce | flops 1 | bytes 8 | tf_op jit(solution)/shard_map/pmax | solution.py:458
  1272.2 32.1 %reduce-scatter.37.cloned.1.call-done = bf16[128,256]{1,0:T(8,128)(2,1)} async-done(((bf16[1024,256]{1,0:T(8,128)(2,1)}), bf16[128,256]{1,0:T(8,128)(2,1)}) %reduce-scatter.37.cloned.1.call-update) | async-done | bytes 65552 | tf_op jit(solution)/shard_map/reduce_scatter | solution.py:432
  1305.8 40.6 %reduce-scatter.35.cloned.1.call-done = bf16[128,3,256]{2,0,1:T(8,128)(2,1)} async-done(((bf16[1024,3,256]{2,0,1:T(8,128)(2,1)}), bf16[128,3,256]{2,0,1:T(8,128)(2,1)}) %reduce-scatter.35.cloned.1.call-update) | async-done | bytes 196624 | tf_op jit(solution)/shard_map/reduce_scatter | solution.py:441
  1346.4 42.1 %reduce-scatter.33.cloned.1.call-done = bf16[128,3,256]{2,0,1:T(8,128)(2,1)} async-done(((bf16[1024,3,256]{2,0,1:T(8,128)(2,1)}), bf16[128,3,256]{2,0,1:T(8,128)(2,1)}) %reduce-scatter.33.cloned.1.call-update) | async-done | bytes 196624 | tf_op jit(solution)/shard_map/reduce_scatter | solution.py:429
  1390.5 44.1 %reduce-scatter.31.cloned.1.call-done = bf16[256,1024]{1,0:T(8,128)(2,1)} async-done(((bf16[1024,1024]{1,0:T(8,128)(2,1)}), bf16[256,1024]{1,0:T(8,128)(2,1)}) %reduce-scatter.31.cloned.1.call-update) | async-done | bytes 524304 | tf_op jit(solution)/shard_map/reduce_scatter | solution.py:206
  1437.9 40.1 %all-reduce.2 = (f32[2,2,1024]{2,1,0:T(2,128)}, f32[2,2,1024]{2,1,0:T(2,128)S(1)}, f32[]{:T(128)}) all-reduce(f32[2,2,1024]{2,1,0:T(2,128)S(1)} %pad_maximum_fusion.2, f32[2,2,1024]{2,1,0:T(2,128)S(1)} %pad_maximum_fusion.3, f32[]{:T(128)S(6)} %add.652), channel_id=1, replica_groups=mesh['rows'=8,'feat'=4] {'rows','feat'}, use_global_device_ids=true, to_apply=%region_54.55 | all-reduce | flops 8193 | bytes 65544 | tf_op jit(solution)/shard_map/psum | solution.py:455
  (656 shorter events, 321.7 us)
Async XLA Ops:
  7.2 55.5 %all-gather.17.cloned.1.call-start = ((), (), s32[]{:S(2)}) async-start(), calls=%async_computation.16 | async-start | bytes 2621440 | tf_op jit(solution)/shard_map/all_gather | solution.py:192
  11.1 158.3 %copy-start.58 = (f32[1,1,1024]{2,1,0:T(1,128)}, f32[1,1,1024]{2,1,0:T(1,128)S(1)}, u32[]{:S(2)}) copy-start(f32[1,1,1024]{2,1,0:T(1,128)S(1)} %get-tuple-element.1733) | copy-start | bytes 12292
  11.1 270.2 %copy-start.63 = (f32[1,1,1024]{2,1,0:T(1,128)}, f32[1,1,1024]{2,1,0:T(1,128)S(1)}, u32[]{:S(2)}) copy-start(f32[1,1,1024]{2,1,0:T(1,128)S(1)} %get-tuple-element.1735) | copy-start | bytes 12292
  14.1 152.7 %reduce-scatter.17.cloned.1.call-start = ((), (), s32[]{:S(2)}) async-start(), calls=%async_computation.17 | async-start | bytes 2621440 | tf_op jit(solution)/shard_map/reduce_scatter | solution.py:196
  19.4 47.2 %copy-start.70 = (f32[1024]{0:T(1024)}, f32[1024]{0:T(1024)S(1)}, u32[]{:S(2)}) copy-start(f32[1024]{0:T(1024)S(1)} %get-tuple-element.1740) | copy-start | bytes 12292
  110.8 56.0 %copy-start.3 = (bf16[256,1024]{1,0:T(8,128)(2,1)S(1)}, bf16[256,1024]{1,0:T(8,128)(2,1)}, u32[]{:S(2)}) copy-start(bf16[256,1024]{1,0:T(8,128)(2,1)} %param.26) | copy-start | bytes 1572868
  115.5 101.5 %all-gather.19.cloned.1.call-start = ((), (), s32[]{:S(2)}) async-start(), calls=%async_computation.18 | async-start | bytes 2621440 | tf_op jit(solution)/shard_map/all_gather | solution.py:192
  168.0 63.9 %copy-start.67 = (f32[256]{0:T(256)}, f32[256]{0:T(256)S(1)}, u32[]{:S(2)}) copy-start(f32[256]{0:T(256)S(1)} %broadcast_multiply_fusion.2) | copy-start | bytes 3076
  169.4 62.5 %copy-start.94 = (f32[256]{0:T(256)}, f32[256]{0:T(256)S(1)}, u32[]{:S(2)}) copy-start(f32[256]{0:T(256)S(1)} %multiply_reduce_fusion.6) | copy-start | bytes 3076
  169.4 62.5 %copy-start.77 = (f32[256]{0:T(256)}, f32[256]{0:T(256)S(1)}, u32[]{:S(2)}) copy-start(f32[256]{0:T(256)S(1)} %fusion.365) | copy-start | bytes 3076
  171.6 108.1 %reduce-scatter.19.cloned.1.call-start = ((), (), s32[]{:S(2)}) async-start(), calls=%async_computation.19 | async-start | bytes 2621440 | tf_op jit(solution)/shard_map/reduce_scatter | solution.py:196
  236.9 90.9 %all-gather.21.cloned.1.call-start = ((), (), s32[]{:S(2)}) async-start(), calls=%async_computation.20 | async-start | bytes 2621440 | tf_op jit(solution)/shard_map/all_gather | solution.py:192
  281.0 165.9 %copy-start.9 = (f32[256,1024]{1,0:T(8,128)}, f32[256,1024]{1,0:T(8,128)S(1)}, u32[]{:S(2)}) copy-start(f32[256,1024]{1,0:T(8,128)S(1)} %get-tuple-element.1690) | copy-start | bytes 3145732
  281.0 50.7 %copy-start.73 = (f32[256]{0:T(256)}, f32[256]{0:T(256)S(1)}, u32[]{:S(2)}) copy-start(f32[256]{0:T(256)S(1)} %broadcast_multiply_fusion.1) | copy-start | bytes 3076
  281.3 50.4 %copy-start.96 = (f32[256]{0:T(256)}, f32[256]{0:T(256)S(1)}, u32[]{:S(2)}) copy-start(f32[256]{0:T(256)S(1)} %multiply_reduce_fusion.5) | copy-start | bytes 3076
  281.3 50.4 %copy-start.88 = (f32[256]{0:T(256)}, f32[256]{0:T(256)S(1)}, u32[]{:S(2)}) copy-start(f32[256]{0:T(256)S(1)} %fusion.366) | copy-start | bytes 3076
  282.4 164.5 %reduce-scatter.21.cloned.1.call-start = ((), (), s32[]{:S(2)}) async-start(), calls=%async_computation.21 | async-start | bytes 2621440 | tf_op jit(solution)/shard_map/reduce_scatter | solution.py:196
  392.4 56.0 %copy-start.42 = (bf16[32,8,2,512]{3,1,2,0:T(8,128)(2,1)}, bf16[32,8,2,512]{3,1,2,0:T(8,128)(2,1)S(1)}, u32[]{:S(2)}) copy-start(bf16[32,8,2,512]{3,1,2,0:T(8,128)(2,1)S(1)} %copy.247) | copy-start | bytes 1572868
  395.8 99.1 %all-gather.23.cloned.1.call-start = ((), (), s32[]{:S(2)}) async-start(), calls=%async_computation.22 | async-start | bytes 2621440 | tf_op jit(solution)/shard_map/all_gather | solution.py:192
  449.5 91.6 %all-gather.25.cloned.1.call-start = ((), (), s32[]{:S(2)}) async-start(), calls=%async_computation.24 | async-start | bytes 2621440 | tf_op jit(solution)/shard_map/all_gather | solution.py:202
  450.2 147.0 %reduce-scatter.25.cloned.1.call-start = ((), (), s32[]{:S(2)}) async-start(), calls=%async_computation.25 | async-start | bytes 2621440 | tf_op jit(solution)/shard_map/reduce_scatter | solution.py:206
  554.4 88.2 %reduce-scatter.23.cloned.1.call-start = ((), (), s32[]{:S(2)}) async-start(), calls=%async_computation.23 | async-start | bytes 2621440 | tf_op jit(solution)/shard_map/reduce_scatter | solution.py:196
  559.9 86.0 %copy-start.29 = (bf16[256,1024]{1,0:T(8,128)(2,1)S(1)}, bf16[256,1024]{1,0:T(8,128)(2,1)}, u32[]{:S(2)}) copy-start(bf16[256,1024]{1,0:T(8,128)(2,1)} %param.27) | copy-start | bytes 1572868
  560.0 132.4 %all-gather.27.cloned.1.call-start = ((), (), s32[]{:S(2)}) async-start(), calls=%async_computation.26 | async-start | bytes 2621440 | tf_op jit(solution)/shard_map/all_gather | solution.py:202
  647.0 244.4 %reduce-scatter.27.cloned.1.call-start = ((), (), s32[]{:S(2)}) async-start(), calls=%async_computation.27 | async-start | bytes 2621440 | tf_op jit(solution)/shard_map/reduce_scatter | solution.py:206
  846.3 47.1 %copy-start.97 = (f32[256]{0:T(256)S(1)}, f32[256]{0:T(256)}, u32[]{:S(2)}) copy-start(f32[256]{0:T(256)} %copy-done.96) | copy-start | bytes 3076
  846.3 47.1 %copy-start.89 = (f32[256]{0:T(256)S(1)}, f32[256]{0:T(256)}, u32[]{:S(2)}) copy-start(f32[256]{0:T(256)} %copy-done.88) | copy-start | bytes 3076
  849.5 94.0 %all-gather.29.cloned.1.call-start = ((), (), s32[]{:S(2)}) async-start(), calls=%async_computation.28 | async-start | bytes 2621440 | tf_op jit(solution)/shard_map/all_gather | solution.py:202
  898.1 105.9 %copy-start.22 = (f32[256,1024]{1,0:T(8,128)}, f32[256,1024]{1,0:T(8,128)S(1)}, u32[]{:S(2)}) copy-start(f32[256,1024]{1,0:T(8,128)S(1)} %get-tuple-element.1682) | copy-start | bytes 3145732
  898.1 101.5 %reduce-scatter.29.cloned.1.call-start = ((), (), s32[]{:S(2)}) async-start(), calls=%async_computation.29 | async-start | bytes 2621440 | tf_op jit(solution)/shard_map/reduce_scatter | solution.py:206
  953.1 46.6 %copy-start.4 = (bf16[256,1024]{1,0:T(8,128)(2,1)S(1)}, bf16[256,1024]{1,0:T(8,128)(2,1)}, u32[]{:S(2)}) copy-start(bf16[256,1024]{1,0:T(8,128)(2,1)} %param.26) | copy-start | bytes 1572868
  953.1 46.6 %copy-start.12 = (bf16[256,1024]{1,0:T(8,128)(2,1)S(1)}, bf16[256,1024]{1,0:T(8,128)(2,1)}, u32[]{:S(2)}) copy-start(bf16[256,1024]{1,0:T(8,128)(2,1)} %reduce-scatter.17.cloned.1.call-done) | copy-start | bytes 1572868
  953.1 46.6 %copy-start.59 = (f32[1,1,1024]{2,1,0:T(1,128)S(1)}, f32[1,1,1024]{2,1,0:T(1,128)}, u32[]{:S(2)}) copy-start(f32[1,1,1024]{2,1,0:T(1,128)} %copy-done.58) | copy-start | bytes 12292
  953.1 48.6 %copy-start.95 = (f32[256]{0:T(256)S(1)}, f32[256]{0:T(256)}, u32[]{:S(2)}) copy-start(f32[256]{0:T(256)} %copy-done.94) | copy-start | bytes 3076
  953.1 48.7 %copy-start.78 = (f32[256]{0:T(256)S(1)}, f32[256]{0:T(256)}, u32[]{:S(2)}) copy-start(f32[256]{0:T(256)} %copy-done.77) | copy-start | bytes 3076
  956.9 94.8 %all-gather.31.cloned.1.call-start = ((), (), s32[]{:S(2)}) async-start(), calls=%async_computation.30 | async-start | bytes 2621440 | tf_op jit(solution)/shard_map/all_gather | solution.py:202
  1006.3 210.2 %reduce-scatter.47.cloned.1.call-start = ((), (), s32[]{:S(2)}) async-start(), calls=%async_computation.39 | async-start | bytes 2359296 | tf_op jit(solution)/shard_map/reduce_scatter | solution.py:450
  1012.3 204.2 %reduce-scatter.45.cloned.1.call-start = ((), (), s32[]{:S(2)}) async-start(), calls=%async_computation.38 | async-start | bytes 2359296 | tf_op jit(solution)/shard_map/reduce_scatter | solution.py:438
  1018.7 201.5 %reduce-scatter.43.cloned.1.call-start = ((), (), s32[]{:S(2)}) async-start(), calls=%async_computation.37 | async-start | bytes 2359296 | tf_op jit(solution)/shard_map/reduce_scatter | solution.py:447
  1024.3 205.3 %reduce-scatter.41.cloned.1.call-start = ((), (), s32[]{:S(2)}) async-start(), calls=%async_computation.36 | async-start | bytes 2359296 | tf_op jit(solution)/shard_map/reduce_scatter | solution.py:435
  1030.5 241.7 %reduce-scatter.39.cloned.1.call-start = ((), (), s32[]{:S(2)}) async-start(), calls=%async_computation.35 | async-start | bytes 589824 | tf_op jit(solution)/shard_map/reduce_scatter | solution.py:444
  1032.2 272.1 %reduce-scatter.37.cloned.1.call-start = ((), (), s32[]{:S(2)}) async-start(), calls=%async_computation.34 | async-start | bytes 589824 | tf_op jit(solution)/shard_map/reduce_scatter | solution.py:432
  1054.9 291.5 %reduce-scatter.35.cloned.1.call-start = ((), (), s32[]{:S(2)}) async-start(), calls=%async_computation.33 | async-start | bytes 1769472 | tf_op jit(solution)/shard_map/reduce_scatter | solution.py:441
  1060.8 327.7 %reduce-scatter.33.cloned.1.call-start = ((), (), s32[]{:S(2)}) async-start(), calls=%async_computation.32 | async-start | bytes 1769472 | tf_op jit(solution)/shard_map/reduce_scatter | solution.py:429
  1209.7 224.9 %reduce-scatter.31.cloned.1.call-start = ((), (), s32[]{:S(2)}) async-start(), calls=%async_computation.31 | async-start | bytes 2621440 | tf_op jit(solution)/shard_map/reduce_scatter | solution.py:206
  1216.3 218.3 %copy-start.5 = (bf16[256,1024]{1,0:T(8,128)(2,1)S(1)}, bf16[256,1024]{1,0:T(8,128)(2,1)}, u32[]{:S(2)}) copy-start(bf16[256,1024]{1,0:T(8,128)(2,1)} %param.26) | copy-start | bytes 1572868
  1216.3 218.3 %copy-start.62 = (f32[1,1,1024]{2,1,0:T(1,128)S(1)}, f32[1,1,1024]{2,1,0:T(1,128)}, u32[]{:S(2)}) copy-start(f32[1,1,1024]{2,1,0:T(1,128)} %copy-done.61) | copy-start | bytes 12292
  1216.3 218.3 %copy-start.76 = (f32[256]{0:T(256)S(1)}, f32[256]{0:T(256)}, u32[]{:S(2)}) copy-start(f32[256]{0:T(256)} %copy-done.75) | copy-start | bytes 3076
  1216.3 219.7 %copy-start.93 = (f32[256]{0:T(256)S(1)}, f32[256]{0:T(256)}, u32[]{:S(2)}) copy-start(f32[256]{0:T(256)} %copy-done.92) | copy-start | bytes 3076
  1216.3 219.8 %copy-start.81 = (f32[1024]{0:T(1024)S(1)}, f32[1024]{0:T(1024)}, u32[]{:S(2)}) copy-start(f32[1024]{0:T(1024)} %get-tuple-element.1503) | copy-start | bytes 12292
  1216.3 219.8 %copy-start.83 = (f32[1024]{0:T(1024)S(1)}, f32[1024]{0:T(1024)}, u32[]{:S(2)}) copy-start(f32[1024]{0:T(1024)} %get-tuple-element.1501) | copy-start | bytes 12292
  1216.3 219.8 %copy-start.85 = (f32[1024]{0:T(1024)S(1)}, f32[1024]{0:T(1024)}, u32[]{:S(2)}) copy-start(f32[1024]{0:T(1024)} %get-tuple-element.1499) | copy-start | bytes 12292
  1216.4 219.8 %copy-start.91 = (f32[256]{0:T(256)S(1)}, f32[256]{0:T(256)}, u32[]{:S(2)}) copy-start(f32[256]{0:T(256)} %copy-done.90) | copy-start | bytes 3076
  1216.4 221.4 %copy-start.80 = (f32[1024]{0:T(1024)S(1)}, f32[1024]{0:T(1024)}, u32[]{:S(2)}) copy-start(f32[1024]{0:T(1024)} %get-tuple-element.1493) | copy-start | bytes 12292
  1216.4 221.4 %copy-start.82 = (f32[1024]{0:T(1024)S(1)}, f32[1024]{0:T(1024)}, u32[]{:S(2)}) copy-start(f32[1024]{0:T(1024)} %get-tuple-element.1491) | copy-start | bytes 12292
  1216.4 221.4 %copy-start.84 = (f32[1024]{0:T(1024)S(1)}, f32[1024]{0:T(1024)}, u32[]{:S(2)}) copy-start(f32[1024]{0:T(1024)} %get-tuple-element.1489) | copy-start | bytes 12292
  1216.4 262.9 %copy-start.13 = (bf16[256,1024]{1,0:T(8,128)(2,1)S(1)}, bf16[256,1024]{1,0:T(8,128)(2,1)}, u32[]{:S(2)}) copy-start(bf16[256,1024]{1,0:T(8,128)(2,1)} %reduce-scatter.17.cloned.1.call-done) | copy-start | bytes 1572868
  1216.4 262.9 %copy-start.23 = (f32[256,1024]{1,0:T(8,128)S(1)}, f32[256,1024]{1,0:T(8,128)}, u32[]{:S(2)}) copy-start(f32[256,1024]{1,0:T(8,128)} %copy-done.22) | copy-start | bytes 3145732
  1216.4 262.9 %copy-start.26 = (bf16[256,1024]{1,0:T(8,128)(2,1)S(1)}, bf16[256,1024]{1,0:T(8,128)(2,1)}, u32[]{:S(2)}) copy-start(bf16[256,1024]{1,0:T(8,128)(2,1)} %reduce-scatter.29.cloned.1.call-done) | copy-start | bytes 1572868
  1216.4 262.9 %copy-start.60 = (f32[1,1,1024]{2,1,0:T(1,128)S(1)}, f32[1,1,1024]{2,1,0:T(1,128)}, u32[]{:S(2)}) copy-start(f32[1,1,1024]{2,1,0:T(1,128)} %copy-done.58) | copy-start | bytes 12292
  1216.4 262.9 %copy-start.69 = (f32[256]{0:T(256)S(1)}, f32[256]{0:T(256)}, u32[]{:S(2)}) copy-start(f32[256]{0:T(256)} %copy-done.67) | copy-start | bytes 3076
  1216.5 262.9 %copy-start.79 = (f32[256]{0:T(256)S(1)}, f32[256]{0:T(256)}, u32[]{:S(2)}) copy-start(f32[256]{0:T(256)} %copy-done.77) | copy-start | bytes 3076
  1216.5 262.9 %copy-start.87 = (f32[256]{0:T(256)S(1)}, f32[256]{0:T(256)}, u32[]{:S(2)}) copy-start(f32[256]{0:T(256)} %copy-done.86) | copy-start | bytes 3076
  1216.5 262.9 %copy-start.99 = (f32[256]{0:T(256)S(1)}, f32[256]{0:T(256)}, u32[]{:S(2)}) copy-start(f32[256]{0:T(256)} %copy-done.98) | copy-start | bytes 3076
  (83 other events, 1031.1 us)
Sparse Core Ops, SparseCore 0:
  14.2 48.4 all-gather.16
  115.6 51.1 reduce-scatter.16
  171.7 45.2 all-gather.18
  237.1 42.5 reduce-scatter.18
  282.5 45.2 all-gather.20
  395.9 50.9 reduce-scatter.20
  449.6 45.2 all-gather.22
  496.5 44.5 all-gather.24
  554.5 42.6 reduce-scatter.24
  599.4 43.1 reduce-scatter.22
  647.1 45.2 all-gather.26
  849.6 41.7 reduce-scatter.26
  898.3 45.2 all-gather.28
  957.0 42.5 reduce-scatter.28
  1006.4 45.2 all-gather.30
  1055.2 40.7 reduce-scatter.46
  1099.1 41.1 reduce-scatter.44
  1143.8 41.2 reduce-scatter.42
  1188.3 41.2 reduce-scatter.40
  1232.8 34.1 reduce-scatter.38
  1270.1 34.1 reduce-scatter.36
  1307.9 38.4 reduce-scatter.34
  1350.0 38.4 reduce-scatter.32
  1390.8 43.8 reduce-scatter.30
where the time goes:
time: 1510 us; the launch traced here: 1490 us
  waiting for transfers between devices  769 us (51%)
  matrix products  213 us (14%)
  local copies, waits for them, and re-layouts  192 us (13%)
  blocking collectives  171 us (11%)
  other arithmetic  109 us (7%)
  between operations  21.1 us (1%)
    reduce_scatter x4, waiting for transfers between devices, sum_branch(): lax.psum_scatter(rows_times(left, weight).astype(jnp.bfloat16), 'feat', s...  188 us
    reduce_scatter x4, waiting for transfers between devices, sum_inputs(): lax.psum_scatter(rows_times(left, weight).astype(jnp.bfloat16), 'feat', s...  166 us
    all_gather x4, waiting for transfers between devices, gather_rows(): return lax.all_gather(normed, 'feat', axis=0, tiled=True)  155 us
    all_gather x4, waiting for transfers between devices, gather_grads(): return lax.all_gather(gradient, 'feat', axis=0, tiled=True)  134 us
    dynamic_update_slice x24, local copies, waits for them, and re-layouts, local(): lax.scan(block_forward, (state_in, total_in), pieces)  90.8 us
    reduce_scatter x1, waiting for transfers between devices, local(): lax.psum_scatter(first_layer[0].astype(jnp.bfloat16), 'rows', scatter_dim...  42.1 us
    reduce_scatter x1, waiting for transfers between devices, local(): lax.psum_scatter(second_layer[0].astype(jnp.bfloat16), 'rows', scatter_di...  40.6 us
    psum x1, blocking collectives, local(): lax.psum((jnp.stack(gain_parts), jnp.stack(bias_parts), log_total), ('row...  40.1 us
  transfers between devices with their start and end apart: 24, of which 20 were waited for; matrix products, arithmetic and copies ran while one was open for 14% of the time, Pallas kernels for 0%

commit v1 on v0

--- a/solution.py
+++ b/solution.py
@@ -1,9 +1,647 @@
-from functools import partial
+import functools
+import types
 
 import jax
 import jax.numpy as jnp
 from jax import lax
+from jax.experimental import pallas as pl
+from jax.experimental.pallas import tpu as pltpu
 from jax.sharding import PartitionSpec as P
+
+HD = 64
+EPS_NORM = 1e-05
+EPS_DEN = 1e-06
+MESH = pl.DeviceIdType.MESH
+BF = jnp.bfloat16
+F32 = jnp.float32
+LAG_FIRST, LAG_SECOND, LAG_CORE, LAG_READY = 2, 4, 6, 7
+RING = 4
+ROOT_HALF = 0.7071067811865476
+ROOT_TAU = 0.3989422804014327
+
+
+def sizes_of(mesh, tokens, weight_in, weight_up):
+    s = types.SimpleNamespace()
+    s.R, s.Z = mesh.shape["rows"], mesh.shape["feat"]
+    chips = s.R // 2
+    s.NX = 1
+    while s.NX * s.NX < chips:
+        s.NX *= 2
+    s.NY = chips // s.NX
+    s.T, s.D = tokens.shape
+    s.L = weight_in.shape[0]
+    s.PC = weight_in.shape[3]
+    s.PR = s.D // s.R
+    s.NJ = weight_up.shape[2] // s.PC
+    s.NU = 4 + 2 * s.NJ
+    s.U = s.L * s.NU
+    s.NP = s.PC // 128
+    s.MR = s.NP * HD + 16
+    s.NQ = s.NY * s.NX
+    return s
+
+
+def place(s):
+    r, z = lax.axis_index("rows"), lax.axis_index("feat")
+    return r, z, r // (2 * s.NX), (r // 2) % s.NX, r % 2
+
+
+def row_at(s, y, x, c):
+    return (y * s.NX + x) * 2 + c
+
+
+def greet(s, r, z):
+    barrier = pltpu.get_barrier_semaphore()
+    peers = [((r + d) % s.R, z) for d in range(1, s.R)] + [(r, (z + d) % s.Z) for d in range(1, s.Z)]
+    for peer in peers:
+        pl.semaphore_signal(barrier, inc=1, device_id=peer, device_id_type=MESH)
+    pl.semaphore_wait(barrier, len(peers))
+
+
+def remote(src, dst, send, recv, device):
+    return pltpu.make_async_remote_copy(
+        src_ref=src, dst_ref=dst, send_sem=send, recv_sem=recv, device_id=device, device_id_type=MESH
+    )
+
+
+def dot(a, b, dims=((1,), (0,))):
+    return lax.dot_general(a, b, (dims, ((), ())), preferred_element_type=F32)
+
+
+NT = ((1,), (1,))
+TN = ((0,), (0,))
+
+
+def norm_parts(v):
+    center = jnp.mean(v, axis=-1, keepdims=True)
+    shifted = v - center
+    spread = jnp.mean(shifted * shifted, axis=-1, keepdims=True)
+    inv = lax.rsqrt(spread + EPS_NORM)
+    return shifted * inv, inv
+
+
+def weight_gather(s, h, r, z, y, x, c):
+    half = s.PR // 2
+    F, piece = h["whole"], h["piece"]
+    rows = (pl.ds(0, half), pl.ds(half, half))
+
+    def z_copies(u):
+        return [
+            remote(
+                piece.at[u // s.NU, u % s.NU],
+                F.at[u, s.Z - d - 1, y, x, c],
+                h["z_send"].at[u % RING, d - 1],
+                h["z_recv"].at[u, s.Z - d - 1],
+                (r, (z + d) % s.Z),
+            )
+            for d in range(1, s.Z)
+        ]
+
+    def first(u):
+        out = []
+        for d in range(1, s.NX):
+            at = F.at[u, :, y, x, c, rows[0]]
+            out.append(remote(at, at, h["x_send"].at[u % RING, 0, d - 1], h["x_recv"].at[u, 0, s.NX - d - 1],
+                              (row_at(s, y, (x + d) % s.NX, c), z)))
+        for d in range(1, s.NY):
+            at = F.at[u, :, y, x, c, rows[1]]
+            out.append(remote(at, at, h["y_send"].at[u % RING, 0, d - 1], h["y_recv"].at[u, 0, s.NY - d - 1],
+                              (row_at(s, (y + d) % s.NY, x, c), z)))
+        return out
+
+    def first_landing(u):
+        out = []
+        for d in range(1, s.NX):
+            at = F.at[u, :, y, (x + d) % s.NX, c, rows[0]]
+            out.append(remote(at, at, h["x_send"].at[u % RING, 0, d - 1], h["x_recv"].at[u, 0, d - 1], (r, z)))
+        for d in range(1, s.NY):
+            at = F.at[u, :, (y + d) % s.NY, x, c, rows[1]]
+            out.append(remote(at, at, h["y_send"].at[u % RING, 0, d - 1], h["y_recv"].at[u, 0, d - 1], (r, z)))
+        return out
+
+    def second(u):
+        out = []
+        for d in range(1, s.NY):
+            at = F.at[u, :, y, :, c, rows[0]]
+            out.append(remote(at, at, h["y_send"].at[u % RING, 1, d - 1], h["y_recv"].at[u, 1, s.NY - d - 1],
+                              (row_at(s, (y + d) % s.NY, x, c), z)))
+        for d in range(1, s.NX):
+            at = F.at[u, :, :, x, c, rows[1]]
+            out.append(remote(at, at, h["x_send"].at[u % RING, 1, d - 1], h["x_recv"].at[u, 1, s.NX - d - 1],
+                              (row_at(s, y, (x + d) % s.NX, c), z)))
+        return out
+
+    def second_landing(u):
+        out = []
+        for d in range(1, s.NY):
+            at = F.at[u, :, (y + d) % s.NY, :, c, rows[0]]
+            out.append(remote(at, at, h["y_send"].at[u % RING, 1, d - 1], h["y_recv"].at[u, 1, d - 1], (r, z)))
+        for d in range(1, s.NX):
+            at = F.at[u, :, :, (x + d) % s.NX, c, rows[1]]
+            out.append(remote(at, at, h["x_send"].at[u % RING, 1, d - 1], h["x_recv"].at[u, 1, d - 1], (r, z)))
+        return out
+
+    def share(u):
+        at = F.at[u, :, :, :, c]
+        return remote(at, at, h["c_send"].at[u % RING], h["c_recv"].at[u], (row_at(s, y, x, 1 - c), z))
+
+    def share_landing(u):
+        at = F.at[u, :, :, :, 1 - c]
+        return remote(at, at, h["c_send"].at[u % RING], h["c_recv"].at[u], (r, z))
+
+    def z_landing(u):
+        return [
+            remote(piece.at[0, 0], F.at[u, k, y, x, c], h["z_send"].at[u % RING, 0], h["z_recv"].at[u, k], (r, z))
+            for k in range(s.Z - 1)
+        ]
+
+    def inside(u, what):
+        pl.when((u >= 0) & (u < s.U))(functools.partial(what, u))
+
+    def stage_z(u):
+        for cp in z_copies(u):
+            cp.start()
+
+    def stage_first(u):
+        for cp in z_landing(u):
+            cp.wait_recv()
+        for cp in first(u):
+            cp.start()
+
+    def stage_second(u):
+        for cp in first_landing(u):
+            cp.wait_recv()
+        for cp in second(u):
+            cp.start()
+
+    def stage_core(u):
+        for cp in second_landing(u):
+            cp.wait_recv()
+        share(u).start()
+
+    def stage_ready(u):
+        share_landing(u).wait_recv()
+
+    def tick(t):
+        inside(t - RING, lambda u: [cp.wait_send() for cp in z_copies(u)] and None)
+        inside(t, stage_z)
+        inside(t - LAG_FIRST - RING, lambda u: [cp.wait_send() for cp in first(u)] and None)
+        inside(t - LAG_FIRST, stage_first)
+        inside(t - LAG_SECOND - RING, lambda u: [cp.wait_send() for cp in second(u)] and None)
+        inside(t - LAG_SECOND, stage_second)
+        inside(t - LAG_CORE - RING, lambda u: share(u).wait_send())
+        inside(t - LAG_CORE, stage_core)
+        inside(t - LAG_READY, stage_ready)
+
+    def drain_all():
+        @pl.loop(s.U + LAG_READY, s.U + LAG_CORE + RING)
+        def _(t):
+            tick(t)
+
+    return tick, drain_all
+
+
+def head_masks(s):
+    lane = lax.broadcasted_iota(jnp.int32, (1, 128), 1)
+    first = lane < HD
+    return first, jnp.where(first, 1.0, 0.0), jnp.where(first, 0.0, 1.0)
+
+
+def pair_ones():
+    row = lax.broadcasted_iota(jnp.int32, (128, 128), 0) // HD
+    col = lax.broadcasted_iota(jnp.int32, (128, 128), 1) // HD
+    return jnp.where(row == col, 1.0, 0.0).astype(BF)
+
+
+def lanes(at, width):
+    return pl.ds(pl.multiple_of(at * width, width), width)
+
+
+def prefix_rounds(s, h, l, r, z):
+    msg, got, rows_got, back, out = h["msg"], h["r1"], h["r2"], h["pre"], h["r3"]
+
+    def one(k):
+        return remote(msg.at[k], got.at[s.Z - k], h["r1_send"].at[l, k], h["r1_recv"].at[l, s.Z - k], (r, (z + k) % s.Z))
+
+    def two(d):
+        return remote(rows_got.at[r], rows_got.at[r], h["r2_send"].at[l, d], h["r2_recv"].at[l, s.R - d],
+                      ((r + d) % s.R, z))
+
+    def two_landing(d):
+        at = rows_got.at[(r + d) % s.R]
+        return remote(at, at, h["r2_send"].at[l, d], h["r2_recv"].at[l, d], (r, z))
+
+    def three(k):
+        return remote(back.at[k], out.at[s.Z - k], h["r3_send"].at[l, k], h["r3_recv"].at[l, s.Z - k], (r, (z + k) % s.Z))
+
+    def round_one():
+        for k in range(1, s.Z):
+            one(k).start()
+
+    def round_two():
+        for k in range(1, s.Z):
+            remote(msg.at[k], got.at[k], h["r1_send"].at[l, k], h["r1_recv"].at[l, k], (r, z)).wait_recv()
+        total = h["coef_a"][0] * msg[0].astype(F32)
+        for k in range(1, s.Z):
+            total = total + h["coef_a"][k] * got[k].astype(F32)
+        rows_got[r] = total.astype(BF)
+        for d in range(1, s.R):
+            two(d).start()
+
+    def round_three():
+        for d in range(1, s.R):
+            two_landing(d).wait_recv()
+        for k in range(s.Z):
+            total = h["coef_b"][k * s.Z] * msg[0].astype(F32)
+            for j in range(1, s.Z):
+                total = total + h["coef_b"][k * s.Z + j] * got[j].astype(F32)
+            for q in range(s.R):
+                total = total + h["coef_c"][k * s.R + q] * rows_got[q].astype(F32)
+            if k == 0:
+                out[0] = total.astype(BF)
+            else:
+                back[k] = total.astype(BF)
+                three(k).start()
+
+    def arrive():
+        for k in range(1, s.Z):
+            remote(back.at[k], out.at[k], h["r3_send"].at[l, k], h["r3_recv"].at[l, k], (r, z)).wait_recv()
+
+    def settle():
+        for k in range(1, s.Z):
+            one(k).wait_send()
+            three(k).wait_send()
+        for d in range(1, s.R):
+            two(d).wait_send()
+
+    return round_one, round_two, round_three, arrive, settle
+
+
+def pack_state(full, first):
+    return jnp.where(first, full[:HD], full[HD:])
+
+
+def unpack_state(packed, first):
+    zero = jnp.zeros_like(packed)
+    return jnp.concatenate([jnp.where(first, packed, zero), jnp.where(first, zero, packed)], axis=0)
+
+
+def spread_rows(s, rows_list):
+    at = lax.broadcasted_iota(jnp.int32, (16, 128), 0)
+    block = jnp.zeros((16, 128), F32)
+    for i, row in enumerate(rows_list):
+        block = block + jnp.where(at == i, row, 0.0)
+    return block
+
+
+def pick_row(block, i):
+    at = lax.broadcasted_iota(jnp.int32, (16, 128), 0)
+    return jnp.sum(jnp.where(at == i, block.astype(F32), 0.0), axis=0, keepdims=True)
+
+
+FWD_IN = ("tokens", "gain", "bias", "coef_a", "coef_b", "coef_c", "w_in", "w_mix", "w_up", "w_down")
+FWD_OUT = ("output", "logs", "whole", "k_stream", "k_middle", "k_qkv", "k_mixed", "k_den", "k_state", "k_act", "k_slope",
+           "k_normt", "s_mixed", "s_act")
+
+
+def fwd_scratch(s):
+    dma = pltpu.SemaphoreType.DMA
+    return {
+        "piece": pltpu.VMEM((s.L, s.NU, s.PR, s.PC), BF),
+        "w": pltpu.VMEM((s.Z, s.NY, s.NX, 2, s.PR, s.PC), BF),
+        "stream": pltpu.VMEM((s.T, s.D), F32),
+        "acc": pltpu.VMEM((s.T, s.D), F32),
+        "middle": pltpu.VMEM((s.T, s.D), F32),
+        "den": pltpu.VMEM((s.T, s.D), F32),
+        "nrm": pltpu.VMEM((s.T, s.D), BF),
+        "nrmt": pltpu.VMEM((2, s.NY, s.NX, 2, s.PR, s.T), BF),
+        "qkv": pltpu.VMEM((3, s.T, s.D), BF),
+        "mixed": pltpu.VMEM((s.T, s.D), BF),
+        "act": pltpu.VMEM((s.NJ, s.T, s.D), BF),
+        "slope": pltpu.VMEM((s.NJ, s.T, s.D), BF),
+        "msg": pltpu.VMEM((s.Z, s.MR, 128), BF),
+        "r1": pltpu.VMEM((s.Z, s.MR, 128), BF),
+        "r2": pltpu.VMEM((s.R, s.MR, 128), BF),
+        "pre": pltpu.VMEM((s.Z, s.MR, 128), BF),
+        "r3": pltpu.VMEM((s.Z, s.MR, 128), BF),
+        "piece_sem": dma((2 + 2 * s.NJ,)),
+        "w_sem": dma((s.Z,)),
+        "z_send": dma((RING, s.Z - 1)),
+        "z_recv": dma((s.U, s.Z - 1)),
+        "x_send": dma((RING, 2, s.NX - 1)),
+        "x_recv": dma((s.U, 2, s.NX - 1)),
+        "y_send": dma((RING, 2, s.NY - 1)),
+        "y_recv": dma((s.U, 2, s.NY - 1)),
+        "c_send": dma((RING,)),
+        "c_recv": dma((s.U,)),
+        "r1_send": dma((s.L, s.Z)),
+        "r1_recv": dma((s.L, s.Z)),
+        "r2_send": dma((s.L, s.R)),
+        "r2_recv": dma((s.L, s.R)),
+        "r3_send": dma((s.L, s.Z)),
+        "r3_recv": dma((s.L, s.Z)),
+        "keep": dma((8,)),
+        "keep_j": dma((2, s.NJ)),
+        "sib_send": dma((3 + s.NJ,)),
+        "sib_recv": dma((s.L, 3 + s.NJ)),
+    }
+
+
+def fwd_kernel(s, *refs):
+    names = FWD_IN + FWD_OUT + tuple(fwd_scratch(s))
+    h = dict(zip(names, refs, strict=True))
+    r, z, y, x, c = place(s)
+    sibling = (row_at(s, y, x, 1 - c), z)
+    greet(s, r, z)
+    tick, drain_all = weight_gather(s, h, r, z, y, x, c)
+    first, _, _ = head_masks(s)
+
+    pieces = [
+        pltpu.make_async_copy(h["w_in"].at[:, :, y, x, c], h["piece"].at[:, 0:3], h["piece_sem"].at[0]),
+        pltpu.make_async_copy(h["w_mix"].at[:, y, x, c], h["piece"].at[:, 3], h["piece_sem"].at[1]),
+    ]
+    for j in range(s.NJ):
+        cols = pl.ds(j * s.PC, s.PC)
+        pieces.append(pltpu.make_async_copy(h["w_up"].at[:, y, x, c, :, cols], h["piece"].at[:, 4 + j], h["piece_sem"].at[2 + j]))
+        pieces.append(pltpu.make_async_copy(h["w_down"].at[:, y, x, c, :, cols], h["piece"].at[:, 4 + s.NJ + j],
+                                            h["piece_sem"].at[2 + s.NJ + j]))
+    for cp in pieces:
+        cp.start()
+    for cp in pieces:
+        cp.wait()
+
+    def own(kind, l, j):
+        if kind == "in":
+            src = h["w_in"].at[l, j]
+        elif kind == "mix":
+            src = h["w_mix"].at[l]
+        else:
+            src = h["w_" + kind].at[l, :, :, :, :, lanes(j, s.PC)]
+        return pltpu.make_async_copy(src, h["w"].at[0], h["w_sem"].at[0])
+
+    def load(u, k):
+        return pltpu.make_async_copy(h["whole"].at[u, k - 1], h["w"].at[k], h["w_sem"].at[k])
+
+    def with_unit(kind, l, j, u, advance, body):
+        own(kind, l, j).start()
+        advance()
+        for k in range(1, s.Z):
+            load(u, k).start()
+        own(kind, l, j).wait()
+        body(0, h["w"][0].reshape(s.D, s.PC))
+
+        @pl.loop(1, s.Z)
+        def _(k):
+            load(u, k).wait()
+            body(k, h["w"][k].reshape(s.D, s.PC))
+
+    def normalize(l, n, source):
+        xhat, _ = norm_parts(source)
+        v = xhat * h["gain"][pl.ds(l * 2 + n, 1), :] + h["bias"][pl.ds(l * 2 + n, 1), :]
+        h["nrm"][...] = v.astype(BF)
+        h["nrmt"][n] = v.T.astype(BF).reshape(s.NY, s.NX, 2, s.PR, s.T)
+        keep_norm(l, n).start()
+        send_norm(l, n).start()
+
+    def keep_norm(l, n):
+        return pltpu.make_async_copy(h["nrmt"].at[n, :, :, c], h["k_normt"].at[l, n, 0], h["keep"].at[n])
+
+    def send_norm(l, n):
+        return remote(h["nrmt"].at[n, :, :, 1 - c], h["k_normt"].at[l, n, 1], h["sib_send"].at[n], h["sib_recv"].at[l, n],
+                      sibling)
+
+    def keep_one(l, name, index):
+        return pltpu.make_async_copy(h[name], h["k_" + name].at[l], h["keep"].at[index])
+
+    def send_mixed(l):
+        return remote(h["mixed"], h["s_mixed"].at[l], h["sib_send"].at[2], h["sib_recv"].at[l, 2], sibling)
+
+    def keep_act(l, j):
+        return pltpu.make_async_copy(h["act"].at[j], h["k_act"].at[l, j], h["keep_j"].at[0, j])
+
+    def keep_slope(l, j):
+        return pltpu.make_async_copy(h["slope"].at[j], h["k_slope"].at[l, j], h["keep_j"].at[1, j])
+
+    def send_act(l, j):
+        return remote(h["act"].at[j], h["s_act"].at[l, j], h["sib_send"].at[3 + j], h["sib_recv"].at[l, 3 + j], sibling)
+
+    h["stream"][...] = h["tokens"][...].astype(F32)
+    h["logs"][...] = jnp.where(lax.broadcasted_iota(jnp.int32, (8, 128), 0) == 1, -jnp.inf, 0.0)
+    ones = pair_ones()
+    tall = jnp.ones((s.T, 128), BF)
+
+    @pl.loop(0, LAG_READY)
+    def _(t):
+        tick(t)
+
+    def one_layer(l, carry):
+        base = l * s.NU
+        keep_one(l, "stream", 2).start()
+        normalize(l, 0, h["stream"][...])
+
+        def project(kind, carry):
+            u = base + kind
+
+            def body(k, weight):
+                v = dot(h["nrm"][...], weight)
+                phi = jnp.where(v > 0, v + 1.0, jnp.exp(jnp.minimum(v, 0.0)))
+                h["qkv"][kind, :, lanes(k, s.PC)] = jnp.where(kind < 2, phi, v).astype(BF)
+
+            with_unit("in", l, kind, u, lambda: tick(u + LAG_READY), body)
+            return carry
+
+        lax.fori_loop(0, 3, project, 0)
+        keep_one(l, "qkv", 3).start()
+        round_one, round_two, round_three, arrive, settle = prefix_rounds(s, h, l, r, z)
+
+        def local_state(k, carry):
+            totals = []
+            for i in range(s.NP):
+                at = lanes(k * s.NP + i, 128)
+                keys, vals = h["qkv"][1, :, at], h["qkv"][2, :, at]
+                h["msg"][k, i * HD:(i + 1) * HD] = pack_state(dot(keys, vals, TN), first).astype(BF)
+                totals.append(jnp.sum(keys.astype(F32), axis=0, keepdims=True))
+            h["msg"][k, s.NP * HD:] = spread_rows(s, totals).astype(BF)
+            return carry
+
+        lax.fori_loop(0, s.Z, local_state, 0)
+        round_one()
+        tick(base + 3 + LAG_READY)
+        round_two()
+        tick(base + 4 + LAG_READY)
+        round_three()
+        tick(base + 5 + LAG_READY)
+        arrive()
+        keep_one(l, "r3", 7) if False else pltpu.make_async_copy(h["r3"], h["k_state"].at[l], h["keep"].at[7]).start()
+        causal = (lax.broadcasted_iota(jnp.int32, (s.T, s.T), 1) <= lax.broadcasted_iota(jnp.int32, (s.T, s.T), 0))
+
+        def attend(p, carry):
+            k, i = p // s.NP, p % s.NP
+            at = lanes(p, 128)
+            query, key, value = h["qkv"][0, :, at], h["qkv"][1, :, at], h["qkv"][2, :, at]
+            wide = query.astype(F32)
+            value_ones = jnp.concatenate([value, tall], axis=1)
+            zero = jnp.zeros_like(query)
+            results = []
+            for head in range(2):
+                mine = first if head == 0 else jnp.logical_not(first)
+                scores = dot(jnp.where(mine, query, zero), key, NT)
+                weights = jnp.where(causal, scores, 0.0).astype(BF)
+                results.append(dot(weights, value_ones))
+            state = unpack_state(h["r3"][k, pl.ds(pl.multiple_of(i * HD, HD), HD), :], first)
+            total = pick_row(h["r3"][k, s.NP * HD:, :], i)
+            square = jnp.zeros((128, 128), BF)
+            right = jnp.concatenate(
+                [jnp.concatenate([state, square], axis=1), jnp.concatenate([square, ones], axis=1)], axis=0)
+            left = jnp.concatenate([query, (wide * total).astype(BF)], axis=1)
+            earlier = dot(left, right)
+            num = jnp.where(first, results[0][:, :128], results[1][:, :128]) + earlier[:, :128]
+            den = jnp.where(first, results[0][:, 128:], results[1][:, 128:]) + earlier[:, 128:] + EPS_DEN
+            h["mixed"][:, at] = (num / den).astype(BF)
+            h["den"][:, at] = den
+            logs = jnp.log(den)
+            h["logs"][0:1] += jnp.sum(logs, axis=0, keepdims=True)
+            h["logs"][1:2] = jnp.maximum(h["logs"][1:2], jnp.max(logs, axis=0, keepdims=True))
+            return carry
+
+        half = s.Z * s.NP // 2
+        lax.fori_loop(0, half, attend, 0)
+        tick(base + 6 + LAG_READY)
+        lax.fori_loop(half, s.Z * s.NP, attend, 0)
+        settle()
+        keep_one(l, "mixed", 4).start()
+        send_mixed(l).start()
+        keep_one(l, "den", 5).start()
+
+        h["acc"][...] = jnp.zeros_like(h["acc"])
+
+        def mix(k, weight):
+            h["acc"][...] += dot(h["mixed"][:, lanes(k, s.PC)], weight, NT)
+
+        with_unit("mix", l, 0, base + 3, lambda: None, mix)
+        h["middle"][...] = h["stream"][...] + h["acc"][...]
+        keep_one(l, "middle", 6).start()
+        normalize(l, 1, h["middle"][...])
+
+        def up(j, carry):
+            u = base + 4 + j
+
+            def body(k, weight):
+                v = dot(h["nrm"][...], weight)
+                cdf = 0.5 * (1.0 + lax.erf(v * ROOT_HALF))
+                h["act"][j, :, lanes(k, s.PC)] = (v * cdf).astype(BF)
+                h["slope"][j, :, lanes(k, s.PC)] = (cdf + v * (ROOT_TAU * jnp.exp(-0.5 * v * v))).astype(BF)
+
+            with_unit("up", l, j, u, lambda: pl.when(j >= 3)(lambda: tick(u + LAG_READY)), body)
+            keep_act(l, j).start()
+            keep_slope(l, j).start()
+            send_act(l, j).start()
+            return carry
+
+        lax.fori_loop(0, s.NJ, up, 0)
+        h["acc"][...] = jnp.zeros_like(h["acc"])
+
+        def down(j, carry):
+            u = base + 4 + s.NJ + j
+
+            def body(k, weight):
+                h["acc"][...] += dot(h["act"][j, :, lanes(k, s.PC)], weight, NT)
+
+            with_unit("down", l, j, u, lambda: tick(u + LAG_READY), body)
+            return carry
+
+        lax.fori_loop(0, s.NJ, down, 0)
+        keep_one(l, "stream", 2).wait()
+        h["stream"][...] = h["middle"][...] + h["acc"][...]
+        for n in range(2):
+            keep_norm(l, n).wait()
+            send_norm(l, n).wait_send()
+            send_norm(l, n).wait_recv()
+        for name, index in (("qkv", 3), ("mixed", 4), ("den", 5), ("middle", 6)):
+            keep_one(l, name, index).wait()
+        pltpu.make_async_copy(h["r3"], h["k_state"].at[l], h["keep"].at[7]).wait()
+        send_mixed(l).wait()
+
+        def finish(j, carry):
+            keep_act(l, j).wait()
+            keep_slope(l, j).wait()
+            send_act(l, j).wait()
+            return carry
+
+        lax.fori_loop(0, s.NJ, finish, 0)
+        return carry
+
+    lax.fori_loop(0, s.L, one_layer, 0)
+    h["output"][...] = h["stream"][...].astype(BF)
+    drain_all()
+
+
+def split_rows(s, weight_in, *rest):
+    cut = (s.NY, s.NX, 2, s.PR)
+    turned = jnp.transpose(weight_in, (0, 2, 1, 3)).reshape((s.L, 3) + cut + (s.PC,))
+    return (turned,) + tuple(w.reshape((s.L,) + cut + w.shape[2:]) for w in rest)
+
+
+def forward_call(s, tokens, gain, bias, coefs, weights):
+    vmem = pl.BlockSpec(memory_space=pltpu.VMEM)
+    smem = pl.BlockSpec(memory_space=pltpu.SMEM)
+    hbm = pl.BlockSpec(memory_space=pl.ANY)
+    shape = jax.ShapeDtypeStruct
+    outs = {
+        "output": shape((s.T, s.D), BF),
+        "logs": shape((8, 128), F32),
+        "whole": shape((s.U, s.Z - 1, s.NY, s.NX, 2, s.PR, s.PC), BF),
+        "k_stream": shape((s.L, s.T, s.D), F32),
+        "k_middle": shape((s.L, s.T, s.D), F32),
+        "k_qkv": shape((s.L, 3, s.T, s.D), BF),
+        "k_mixed": shape((s.L, s.T, s.D), BF),
+        "k_den": shape((s.L, s.T, s.D), F32),
+        "k_state": shape((s.L, s.Z, s.MR, 128), BF),
+        "k_act": shape((s.L, s.NJ, s.T, s.D), BF),
+        "k_slope": shape((s.L, s.NJ, s.T, s.D), BF),
+        "k_normt": shape((s.L, 2, 2, s.NY, s.NX, s.PR, s.T), BF),
+        "s_mixed": shape((s.L, s.T, s.D), BF),
+        "s_act": shape((s.L, s.NJ, s.T, s.D), BF),
+    }
+    out = pl.pallas_call(
+        functools.partial(fwd_kernel, s),
+        out_shape=[outs[name] for name in FWD_OUT],
+        in_specs=[vmem] * 3 + [smem] * 3 + [hbm] * 4,
+        out_specs=[vmem] * 2 + [hbm] * (len(FWD_OUT) - 2),
+        scratch_shapes=list(fwd_scratch(s).values()),
+        compiler_params=pltpu.CompilerParams(
+            collective_id=0, has_side_effects=True, vmem_limit_bytes=56 * 1024 * 1024),
+        name="forward",
+    )(tokens, gain, bias, *coefs, *weights)
+    return dict(zip(FWD_OUT, out, strict=True))
+
+
+def segments_of_units(s, image_length, image_start):
+    first = jnp.arange(s.R * s.Z, dtype=jnp.int32) * s.T
+    live = (image_length > 0)[None, :]
+    return (jnp.sum(((image_start[None, :] <= first[:, None]) & live).astype(jnp.int32), axis=1) - 1).reshape(s.R, s.Z)
+
+
+def coefficients(s, image_length, image_start):
+    seg = segments_of_units(s, image_length, image_start)
+    r, z = lax.axis_index("rows"), lax.axis_index("feat")
+    turn = (z + jnp.arange(s.Z)) % s.Z
+    row = seg[r][turn]
+    order = jnp.arange(s.R)
+    f = lambda v: v.astype(F32).reshape(-1)
+    same = row[:, None] == row[None, :]
+    forward = (
+        f(row == seg[r, s.Z - 1]),
+        f(same & (turn[None, :] < turn[:, None])),
+        f((seg[None, :, s.Z - 1] == row[:, None]) & (order[None, :] < r)),
+    )
+    backward = (
+        f(row == seg[r, 0]),
+        f(same & (turn[None, :] > turn[:, None])),
+        f((seg[None, :, 0] == row[:, None]) & (order[None, :] > r)),
+    )
+    return forward, backward
+
 
 HEADS = 16
 HD = 64
@@ -249,6 +887,7 @@
 
 
 def local(
+    mesh,
     tokens,
     cotangent,
     image_length,
@@ -260,6 +899,10 @@
     weight_up,
     weight_down,
 ):
+    s = sizes_of(mesh, tokens, weight_in, weight_up)
+    fw, bw = coefficients(s, image_length, image_start)
+    got = forward_call(s, tokens, norm_gain.reshape(-1, s.D), norm_bias.reshape(-1, s.D), fw,
+                       split_rows(s, weight_in, weight_mix, weight_up, weight_down))
     local_rows = tokens.shape[0]
     shard_rows = local_rows * lax.axis_size("feat")
     all_rows = shard_rows * lax.axis_size("rows")
@@ -365,7 +1008,7 @@
         down_grad = gather_grads(gradient.astype(jnp.bfloat16))
         grad_down = jnp.einsum("td,tf->df", down_grad, active, preferred_element_type=jnp.float32)
         active_grad = jnp.dot(down_grad, weight_down[level], preferred_element_type=jnp.float32)
-        _, gelu_back = jax.vjp(partial(jax.nn.gelu, approximate=False), upward)
+        _, gelu_back = jax.vjp(functools.partial(jax.nn.gelu, approximate=False), upward)
         upward_grad = gelu_back(active_grad)[0].astype(jnp.bfloat16)
         grad_up = jnp.einsum(
             "td,tf->df", normed_mid, upward_grad, preferred_element_type=jnp.float32
@@ -457,8 +1100,11 @@
     )
     log_max = lax.pmax(log_top, ("rows", "feat"))
     log_mean = log_sum / (all_rows * HEADS * LAYERS)
+    log_sum = lax.psum(jnp.sum(got["logs"][0]) / HD, ("rows", "feat"))
+    log_mean = log_sum / (all_rows * HEADS * LAYERS)
+    log_max = lax.pmax(jnp.max(got["logs"][1]), ("rows", "feat"))
     return (
-        output,
+        got["output"],
         gradient,
         gain_sum,
         bias_sum,
@@ -486,7 +1132,7 @@
         P(None, None, "feat"),
     )
     return jax.shard_map(
-        local,
+        functools.partial(local, mesh),
         mesh=mesh,
         in_specs=placed,
         out_specs=(

time: 1510 us -> 1550 us (1.026)
  Pallas kernels: 0 us -> 219 us
  waiting for transfers between devices: 769 us -> 567 us
  matrix products: 213 us -> 233 us
    pallas_call x0 -> x1, Pallas kernels: none -> 219 us  [forward_call(): pl.pallas_call(functools.partial(fwd_kernel, s), out_shape=[outs[name] fo...]
    reduce_scatter x1, waiting for transfers between devices: 42.1 us -> 0.01 us  [local(): lax.psum_scatter(first_layer[0].astype(jnp.bfloat16), 'rows', scatter_dim...]
    reduce_scatter x1, waiting for transfers between devices: 40.6 us -> 0.01 us  [local(): lax.psum_scatter(second_layer[0].astype(jnp.bfloat16), 'rows', scatter_di...]
    reduce_scatter x4, waiting for transfers between devices: 166 us -> 127 us  [sum_inputs(): lax.psum_scatter(rows_times(left, weight).astype(jnp.bfloat16), 'feat', s...]
    reduce_scatter x4 -> x3, waiting for transfers between devices: 188 us -> 151 us  [sum_branch(): lax.psum_scatter(rows_times(left, weight).astype(jnp.bfloat16), 'feat', s...]
    reduce_scatter x1, waiting for transfers between devices: 32.1 us -> 0.01 us  [local(): lax.psum_scatter(first_layer[1].astype(jnp.bfloat16), 'rows', scatter_dim...]
  transfers between devices with their start and end apart: 24 -> 23, of which waited for: 20 -> 14; matrix products, arithmetic and copies ran while one was open for 14% -> 14% of each run, Pallas kernels for 0% -> 14%
where the time goes in v1:
time: 1550 us; the launch traced here: 1530 us
  waiting for transfers between devices  567 us (37%)
  matrix products  233 us (15%)
  Pallas kernels  219 us (14%)
  local copies, waits for them, and re-layouts  197 us (13%)
  blocking collectives  173 us (11%)
  other arithmetic  106 us (7%)
  between operations  19 us (1%)
    pallas_call x1, Pallas kernels, forward_call(): pl.pallas_call(functools.partial(fwd_kernel, s), out_shape=[outs[name] fo...  219 us
    all_gather x4, waiting for transfers between devices, gather_rows(): return lax.all_gather(normed, 'feat', axis=0, tiled=True)  156 us
    reduce_scatter x3, waiting for transfers between devices, sum_branch(): lax.psum_scatter(rows_times(left, weight).astype(jnp.bfloat16), 'feat', s...  151 us
    all_gather x4, waiting for transfers between devices, gather_grads(): return lax.all_gather(gradient, 'feat', axis=0, tiled=True)  132 us
    reduce_scatter x4, waiting for transfers between devices, sum_inputs(): lax.psum_scatter(rows_times(left, weight).astype(jnp.bfloat16), 'feat', s...  127 us
    dynamic_update_slice x24, local copies, waits for them, and re-layouts, local(): lax.scan(block_forward, (state_in, total_in), pieces)  90.9 us
    psum x1, blocking collectives, local(): lax.psum((jnp.stack(gain_parts), jnp.stack(bias_parts), log_total), ('row...  40.2 us
    pmax x1, blocking collectives, local(): log_max = lax.pmax(jnp.max(got['logs'][1]), ('rows', 'feat'))  39.2 us
  transfers between devices with their start and end apart: 23, of which 14 were waited for; matrix products, arithmetic and copies ran while one was open for 14% of the time, Pallas kernels for 14%

profile of v1, /device:TPU:0, one launch (start us, length us, event | category | flops | bytes accessed | tf_op | source)
XLA Modules:
  0.0 1529.9 jit_solution(13376639828908387371)
XLA Ops:
  24.7 16.5 %all-reduce.3 = (bf16[8]{0:T(256)(128)(2,1)S(1)}, bf16[8]{0:T(256)(128)(2,1)}) all-reduce(bf16[8]{0:T(256)(128)(2,1)S(1)} %dynamic-update-slice, bf16[8]{0:T(256)(128)(2,1)S(1)} %dynamic-update-slice.1), channel_id=1, replica_groups=mesh['rows'=8,'feat'=4] {'rows'}, use_global_device_ids=true, to_apply=%add | all-reduce | flops 16 | bytes 64
  41.2 21.7 %all-gather.17.cloned.1.call-done = bf16[1024,1024]{1,0:T(8,128)(2,1)} async-done(((bf16[256,1024]{1,0:T(8,128)(2,1)}), bf16[1024,1024]{1,0:T(8,128)(2,1)}) %all-gather.17.cloned.1.call-update) | async-done | bytes 2097168 | tf_op jit(solution)/shard_map/all_gather | solution.py:830
  62.9 3.9 fusion.237
  74.6 10.0 all-gather
  84.6 8.8 all_gather.89
  98.2 27.0 %while.149 = (s32[]{:T(128)}, f32[4,64,64]{2,1,0:T(8,128)S(1)}, f32[4,64]{1,0:T(4,128)S(1)}, f32[2,512,4,64]{1,3,2,0:T(8,128)S(1)}, f32[2,512,4]{1,2,0:T(4,128)S...) while((s32[]{:T(128)}, f32[4,64,64]{2,1,0:T(8,128)S(1)}, ...), condition=%wide.region_11.12_spmd, body=%wide.region_8.11_spmd.sunk | while | flops 393655552 | bytes 15769328 | solution.py:950
  130.7 51.0 %reduce-scatter.16.cloned.1.call-done = bf16[256,1024]{1,0:T(8,128)(2,1)} async-done(((bf16[1024,1024]{1,0:T(8,128)(2,1)}), bf16[256,1024]{1,0:T(8,128)(2,1)}) %reduce-scatter.16.cloned.1.call-update) | async-done | bytes 524304 | tf_op jit(solution)/shard_map/reduce_scatter | solution.py:834
  186.8 45.2 %all-gather.19.cloned.1.call-done = bf16[1024,1024]{1,0:T(8,128)(2,1)} async-done(((bf16[256,1024]{1,0:T(8,128)(2,1)}), bf16[1024,1024]{1,0:T(8,128)(2,1)}) %all-gather.19.cloned.1.call-update) | async-done | bytes 2097168 | tf_op jit(solution)/shard_map/all_gather | solution.py:830
  231.9 14.9 multiply_convert_fusion.29
  248.3 3.7 fusion.244
  252.1 42.7 %reduce-scatter.18.cloned.1.call-done = bf16[256,1024]{1,0:T(8,128)(2,1)} async-done(((bf16[1024,1024]{1,0:T(8,128)(2,1)}), bf16[256,1024]{1,0:T(8,128)(2,1)}) %reduce-scatter.18.cloned.1.call-update) | async-done | bytes 524304 | tf_op jit(solution)/shard_map/reduce_scatter | solution.py:834
  297.9 44.9 %all-gather.21.cloned.1.call-done = bf16[1024,1024]{1,0:T(8,128)(2,1)} async-done(((bf16[256,1024]{1,0:T(8,128)(2,1)}), bf16[1024,1024]{1,0:T(8,128)(2,1)}) %all-gather.21.cloned.1.call-update) | async-done | bytes 2097168 | tf_op jit(solution)/shard_map/all_gather | solution.py:830
  342.9 3.9 fusion.223
  354.2 10.8 all-gather.1
  365.2 8.8 all_gather.95
  379.6 28.1 %while.151 = (s32[]{:T(128)}, f32[4,64,64]{2,1,0:T(8,128)S(1)}, f32[4,64]{1,0:T(4,128)S(1)}, f32[2,512,4,64]{1,3,2,0:T(8,128)S(1)}, f32[2,512,4]{1,2,0:T(4,128)S...) while((s32[]{:T(128)}, f32[4,64,64]{2,1,0:T(8,128)S(1)}, ...), condition=%wide.region_24.25_spmd, body=%wide.region_21.24_spmd.sunk | while | flops 393655552 | bytes 15769328 | solution.py:950
  408.5 3.3 convolution_convert_fusion.3
  411.9 56.9 %reduce-scatter.20.cloned.1.call-done = bf16[256,1024]{1,0:T(8,128)(2,1)} async-done(((bf16[1024,1024]{1,0:T(8,128)(2,1)}), bf16[256,1024]{1,0:T(8,128)(2,1)}) %reduce-scatter.20.cloned.1.call-update) | async-done | bytes 524304 | tf_op jit(solution)/shard_map/reduce_scatter | solution.py:834
  472.4 44.5 %all-gather.23.cloned.1.call-done = bf16[1024,1024]{1,0:T(8,128)(2,1)} async-done(((bf16[256,1024]{1,0:T(8,128)(2,1)}), bf16[1024,1024]{1,0:T(8,128)(2,1)}) %all-gather.23.cloned.1.call-update) | async-done | bytes 2097168 | tf_op jit(solution)/shard_map/all_gather | solution.py:830
  516.9 14.4 fusion.201
  531.2 32.0 %all-gather.25.cloned.1.call-done = bf16[1024,1024]{1,0:T(8,128)(2,1)} async-done(((bf16[256,1024]{1,0:T(8,128)(2,1)}), bf16[1024,1024]{1,0:T(8,128)(2,1)}) %all-gather.25.cloned.1.call-update) | async-done | bytes 2097168 | tf_op jit(solution)/shard_map/all_gather | solution.py:840
  563.2 8.1 add_convert_fusion.1
  572.7 3.7 fusion.247
  576.4 42.7 %reduce-scatter.22.cloned.1.call-done = bf16[256,1024]{1,0:T(8,128)(2,1)} async-done(((bf16[1024,1024]{1,0:T(8,128)(2,1)}), bf16[256,1024]{1,0:T(8,128)(2,1)}) %reduce-scatter.22.cloned.1.call-update) | async-done | bytes 524304 | tf_op jit(solution)/shard_map/reduce_scatter | solution.py:844
  634.0 37.4 %all-gather.27.cloned.1.call-done = bf16[1024,1024]{1,0:T(8,128)(2,1)} async-done(((bf16[256,1024]{1,0:T(8,128)(2,1)}), bf16[1024,1024]{1,0:T(8,128)(2,1)}) %all-gather.27.cloned.1.call-update) | async-done | bytes 2097168 | tf_op jit(solution)/shard_map/all_gather | solution.py:840
  671.4 3.9 multiply_reduce_fusion.3
  679.8 9.8 all-gather.2
  690.5 8.8 all-gather.6
  699.3 10.8 while.154
  714.2 93.1 %while.152 = (s32[]{:T(128)}, f32[4,64,64]{2,1,0:T(8,128)S(1)}, f32[4,64]{1,0:T(4,128)S(1)}, f32[2,512,4,64]{1,0,3,2:T(2,128)}, f32[2,512,4,64]{1,0,3,2:T(2,128)...) while((s32[]{:T(128)}, f32[4,64,64]{2,1,0:T(8,128)S(1)}, ...), condition=%wide.region_35.36_spmd, body=%wide.region_34.35_spmd.sunk | while | flops 1083085824 | bytes 22254372 | solution.py:1047
  734.5 10.4 dynamic_update_slice.115
  747.1 10.4 dynamic_update_slice.116
  757.5 3.1 fusion.581
  780.9 10.4 dynamic_update_slice.115
  793.4 10.4 dynamic_update_slice.116
  810.1 3.2 stack_reshape.12
  824.5 3.2 convolution_convert_fusion.6
  827.8 41.8 %reduce-scatter.24.cloned.1.call-done = bf16[256,1024]{1,0:T(8,128)(2,1)} async-done(((bf16[1024,1024]{1,0:T(8,128)(2,1)}), bf16[256,1024]{1,0:T(8,128)(2,1)}) %reduce-scatter.24.cloned.1.call-update) | async-done | bytes 524304 | tf_op jit(solution)/shard_map/reduce_scatter | solution.py:844
  876.5 45.2 %all-gather.29.cloned.1.call-done = bf16[1024,1024]{1,0:T(8,128)(2,1)} async-done(((bf16[256,1024]{1,0:T(8,128)(2,1)}), bf16[1024,1024]{1,0:T(8,128)(2,1)}) %all-gather.29.cloned.1.call-update) | async-done | bytes 2097168 | tf_op jit(solution)/shard_map/all_gather | solution.py:840
  921.7 8.1 add_convert_fusion
  931.3 3.7 fusion.241
  935.1 42.7 %reduce-scatter.26.cloned.1.call-done = bf16[256,1024]{1,0:T(8,128)(2,1)} async-done(((bf16[1024,1024]{1,0:T(8,128)(2,1)}), bf16[256,1024]{1,0:T(8,128)(2,1)}) %reduce-scatter.26.cloned.1.call-update) | async-done | bytes 524304 | tf_op jit(solution)/shard_map/reduce_scatter | solution.py:844
  984.5 6.1 convolution_convert_fusion.1
  990.7 5.4 convolution_convert_fusion.2
  996.6 7.8 convert_bitcast_fusion
  1004.5 6.1 convolution_convert_fusion
  1012.3 17.5 %all-gather.31.cloned.1.call-done = bf16[1024,1024]{1,0:T(8,128)(2,1)} async-done(((bf16[256,1024]{1,0:T(8,128)(2,1)}), bf16[1024,1024]{1,0:T(8,128)(2,1)}) %all-gather.31.cloned.1.call-update) | async-done | bytes 2097168 | tf_op jit(solution)/shard_map/all_gather | solution.py:840
  1029.8 3.1 convolution_convert_fusion.8
  1033.2 4.8 fusion.259
  1038.0 4.1 multiply_reduce_fusion.2
  1046.8 11.3 all-gather.4
  1058.9 9.0 all-gather.7
  1067.9 10.8 while.155
  1082.8 92.9 %while.153 = (s32[]{:T(128)}, f32[4,64,64]{2,1,0:T(8,128)S(1)}, f32[4,64]{1,0:T(4,128)S(1)}, f32[2,512,4,64]{1,0,3,2:T(2,128)}, f32[2,512,4,64]{1,0,3,2:T(2,128)...) while((s32[]{:T(128)}, f32[4,64,64]{2,1,0:T(8,128)S(1)}, ...), condition=%wide.region_46.47_spmd, body=%wide.region_45.46_spmd.sunk | while | flops 1083085824 | bytes 22254372 | solution.py:1047
  1103.2 10.4 dynamic_update_slice.118
  1115.8 10.4 dynamic_update_slice.119
  1149.6 10.4 dynamic_update_slice.118
  1162.2 10.4 dynamic_update_slice.119
  1172.6 3.2 fusion.611
  1178.5 3.3 stack_reshape.14
  1194.7 4.7 convolution_convert_fusion.5
  1204.9 219.3 %forward.1 = (bf16[256,1024]{1,0:T(8,128)(2,1)}, f32[8,128]{1,0:T(8,128)}, bf16[24,3,2,2,2,128,256]{6,5,4,3,2,1,0:T(8,128)(2,1)}, f32[2,256,1024]{2,1,0:T(8,128)...) custom-call(bf16[256,1024]{1,0:T(8,128)(2,1)} %refs_0_.1, ...), custom_call_target="tpu_custom_call" | custom-call | tf_op jit(solution)/shard_map/forward/pallas_call | solution.py:606
  1425.9 39.2 %pmax.7 = f32[]{:T(128)} all-reduce(f32[]{:T(128)} %get-tuple-element.1509), channel_id=1, replica_groups=mesh['rows'=8,'feat'=4] {'rows','feat'}, use_global_device_ids=true, to_apply=%region_69.70 | all-reduce | flops 1 | bytes 8 | tf_op jit(solution)/shard_map/pmax | solution.py:1105
  1476.9 40.2 %all-reduce.2 = (f32[2,2,1024]{2,1,0:T(2,128)}, f32[2,2,1024]{2,1,0:T(2,128)S(1)}, f32[]{:T(128)}) all-reduce(f32[2,2,1024]{2,1,0:T(2,128)S(1)} %pad_maximum_fusion.2, f32[2,2,1024]{2,1,0:T(2,128)S(1)} %pad_maximum_fusion.3, f32[]{:T(128)S(6)} %div.178), channel_id=1, replica_groups=mesh['rows'=8,'feat'=4] {'rows','feat'}, use_global_device_ids=true, to_apply=%region_54.55 | all-reduce | flops 8193 | bytes 65544 | tf_op jit(solution)/shard_map/psum | solution.py:1098
  (654 shorter events, 327.2 us)
Async XLA Ops:
  7.2 55.7 %all-gather.17.cloned.1.call-start = ((), (), s32[]{:S(2)}) async-start(), calls=%async_computation.15 | async-start | bytes 2621440 | tf_op jit(solution)/shard_map/all_gather | solution.py:830
  9.4 175.0 %copy-start.54 = (f32[1,1,1024]{2,1,0:T(1,128)}, f32[1,1,1024]{2,1,0:T(1,128)S(1)}, u32[]{:S(2)}) copy-start(f32[1,1,1024]{2,1,0:T(1,128)S(1)} %get-tuple-element.1730) | copy-start | bytes 12292
  12.0 54.9 %copy-start.91 = (f32[256]{0:T(256)}, f32[256]{0:T(256)S(1)}, u32[]{:S(2)}) copy-start(f32[256]{0:T(256)S(1)} %fusion.283) | copy-start | bytes 3076
  14.1 167.6 %reduce-scatter.16.cloned.1.call-start = ((), (), s32[]{:S(2)}) async-start(), calls=%async_computation.16 | async-start | bytes 2621440 | tf_op jit(solution)/shard_map/reduce_scatter | solution.py:834
  14.9 52.0 %copy-start.102 = (pred[32]{0:T(512)(128)(4,1)}, pred[32]{0:T(512)(128)(4,1)S(1)}, u32[]{:S(2)}) copy-start(pred[32]{0:T(512)(128)(4,1)S(1)} %broadcast_compare_fusion) | copy-start | bytes 100
  19.5 47.4 %copy-start.67 = (f32[1024]{0:T(1024)}, f32[1024]{0:T(1024)S(1)}, u32[]{:S(2)}) copy-start(f32[1024]{0:T(1024)S(1)} %get-tuple-element.1737) | copy-start | bytes 12292
  127.0 54.7 %copy-start = (bf16[256,1024]{1,0:T(8,128)(2,1)S(1)}, bf16[256,1024]{1,0:T(8,128)(2,1)}, u32[]{:S(2)}) copy-start(bf16[256,1024]{1,0:T(8,128)(2,1)} %refs_0_.1) | copy-start | bytes 1572868
  130.7 101.3 %all-gather.19.cloned.1.call-start = ((), (), s32[]{:S(2)}) async-start(), calls=%async_computation.17 | async-start | bytes 2621440 | tf_op jit(solution)/shard_map/all_gather | solution.py:830
  183.0 63.9 %copy-start.64 = (f32[256]{0:T(256)}, f32[256]{0:T(256)S(1)}, u32[]{:S(2)}) copy-start(f32[256]{0:T(256)S(1)} %broadcast_multiply_fusion.2) | copy-start | bytes 3076
  184.3 62.5 %copy-start.93 = (f32[256]{0:T(256)}, f32[256]{0:T(256)S(1)}, u32[]{:S(2)}) copy-start(f32[256]{0:T(256)S(1)} %multiply_reduce_fusion.6) | copy-start | bytes 3076
  184.4 62.5 %copy-start.75 = (f32[256]{0:T(256)}, f32[256]{0:T(256)S(1)}, u32[]{:S(2)}) copy-start(f32[256]{0:T(256)S(1)} %fusion.361) | copy-start | bytes 3076
  186.5 108.2 %reduce-scatter.18.cloned.1.call-start = ((), (), s32[]{:S(2)}) async-start(), calls=%async_computation.18 | async-start | bytes 2621440 | tf_op jit(solution)/shard_map/reduce_scatter | solution.py:834
  252.0 90.8 %all-gather.21.cloned.1.call-start = ((), (), s32[]{:S(2)}) async-start(), calls=%async_computation.19 | async-start | bytes 2621440 | tf_op jit(solution)/shard_map/all_gather | solution.py:830
  296.1 172.8 %copy-start.3 = (f32[256,1024]{1,0:T(8,128)}, f32[256,1024]{1,0:T(8,128)S(1)}, u32[]{:S(2)}) copy-start(f32[256,1024]{1,0:T(8,128)S(1)} %get-tuple-element.1690) | copy-start | bytes 3145732
  296.1 50.7 %copy-start.71 = (f32[256]{0:T(256)}, f32[256]{0:T(256)S(1)}, u32[]{:S(2)}) copy-start(f32[256]{0:T(256)S(1)} %broadcast_multiply_fusion.1) | copy-start | bytes 3076
  296.3 50.4 %copy-start.95 = (f32[256]{0:T(256)}, f32[256]{0:T(256)S(1)}, u32[]{:S(2)}) copy-start(f32[256]{0:T(256)S(1)} %multiply_reduce_fusion.5) | copy-start | bytes 3076
  296.4 50.4 %copy-start.87 = (f32[256]{0:T(256)}, f32[256]{0:T(256)S(1)}, u32[]{:S(2)}) copy-start(f32[256]{0:T(256)S(1)} %fusion.362) | copy-start | bytes 3076
  297.5 171.4 %reduce-scatter.20.cloned.1.call-start = ((), (), s32[]{:S(2)}) async-start(), calls=%async_computation.20 | async-start | bytes 2621440 | tf_op jit(solution)/shard_map/reduce_scatter | solution.py:834
  408.5 61.9 %copy-start.42 = (bf16[32,8,2,512]{3,1,2,0:T(8,128)(2,1)}, bf16[32,8,2,512]{3,1,2,0:T(8,128)(2,1)S(1)}, u32[]{:S(2)}) copy-start(bf16[32,8,2,512]{3,1,2,0:T(8,128)(2,1)S(1)} %copy.246) | copy-start | bytes 1572868
  408.5 61.9 %copy-start.81 = (f32[1,1,1024]{2,1,0:T(1,128)S(1)}, f32[1,1,1024]{2,1,0:T(1,128)}, u32[]{:S(2)}) copy-start(f32[1,1,1024]{2,1,0:T(1,128)} %get-tuple-element.1733) | copy-start | bytes 12292
  411.8 105.0 %all-gather.23.cloned.1.call-start = ((), (), s32[]{:S(2)}) async-start(), calls=%async_computation.21 | async-start | bytes 2621440 | tf_op jit(solution)/shard_map/all_gather | solution.py:830
  471.4 91.8 %all-gather.25.cloned.1.call-start = ((), (), s32[]{:S(2)}) async-start(), calls=%async_computation.22 | async-start | bytes 2621440 | tf_op jit(solution)/shard_map/all_gather | solution.py:840
  472.2 146.9 %reduce-scatter.22.cloned.1.call-start = ((), (), s32[]{:S(2)}) async-start(), calls=%async_computation.23 | async-start | bytes 2621440 | tf_op jit(solution)/shard_map/reduce_scatter | solution.py:844
  576.4 95.0 %all-gather.27.cloned.1.call-start = ((), (), s32[]{:S(2)}) async-start(), calls=%async_computation.24 | async-start | bytes 2621440 | tf_op jit(solution)/shard_map/all_gather | solution.py:840
  626.0 243.6 %reduce-scatter.24.cloned.1.call-start = ((), (), s32[]{:S(2)}) async-start(), calls=%async_computation.25 | async-start | bytes 2621440 | tf_op jit(solution)/shard_map/reduce_scatter | solution.py:844
  824.5 47.1 %copy-start.96 = (f32[256]{0:T(256)S(1)}, f32[256]{0:T(256)}, u32[]{:S(2)}) copy-start(f32[256]{0:T(256)} %copy-done.95) | copy-start | bytes 3076
  824.5 47.1 %copy-start.88 = (f32[256]{0:T(256)S(1)}, f32[256]{0:T(256)}, u32[]{:S(2)}) copy-start(f32[256]{0:T(256)} %copy-done.87) | copy-start | bytes 3076
  827.7 94.0 %all-gather.29.cloned.1.call-start = ((), (), s32[]{:S(2)}) async-start(), calls=%async_computation.26 | async-start | bytes 2621440 | tf_op jit(solution)/shard_map/all_gather | solution.py:840
  876.3 105.9 %copy-start.16 = (f32[256,1024]{1,0:T(8,128)}, f32[256,1024]{1,0:T(8,128)S(1)}, u32[]{:S(2)}) copy-start(f32[256,1024]{1,0:T(8,128)S(1)} %get-tuple-element.1684) | copy-start | bytes 3145732
  876.3 101.4 %reduce-scatter.26.cloned.1.call-start = ((), (), s32[]{:S(2)}) async-start(), calls=%async_computation.27 | async-start | bytes 2621440 | tf_op jit(solution)/shard_map/reduce_scatter | solution.py:844
  931.2 46.5 %copy-start.1 = (bf16[256,1024]{1,0:T(8,128)(2,1)S(1)}, bf16[256,1024]{1,0:T(8,128)(2,1)}, u32[]{:S(2)}) copy-start(bf16[256,1024]{1,0:T(8,128)(2,1)} %refs_0_.1) | copy-start | bytes 1572868
  931.2 46.5 %copy-start.6 = (bf16[256,1024]{1,0:T(8,128)(2,1)S(1)}, bf16[256,1024]{1,0:T(8,128)(2,1)}, u32[]{:S(2)}) copy-start(bf16[256,1024]{1,0:T(8,128)(2,1)} %reduce-scatter.16.cloned.1.call-done) | copy-start | bytes 1572868
  931.2 46.5 %copy-start.55 = (f32[1,1,1024]{2,1,0:T(1,128)S(1)}, f32[1,1,1024]{2,1,0:T(1,128)}, u32[]{:S(2)}) copy-start(f32[1,1,1024]{2,1,0:T(1,128)} %copy-done.54) | copy-start | bytes 12292
  931.2 48.6 %copy-start.94 = (f32[256]{0:T(256)S(1)}, f32[256]{0:T(256)}, u32[]{:S(2)}) copy-start(f32[256]{0:T(256)} %copy-done.93) | copy-start | bytes 3076
  931.2 48.6 %copy-start.76 = (f32[256]{0:T(256)S(1)}, f32[256]{0:T(256)}, u32[]{:S(2)}) copy-start(f32[256]{0:T(256)} %copy-done.75) | copy-start | bytes 3076
  935.0 94.8 %all-gather.31.cloned.1.call-start = ((), (), s32[]{:S(2)}) async-start(), calls=%async_computation.28 | async-start | bytes 2621440 | tf_op jit(solution)/shard_map/all_gather | solution.py:840
  984.5 481.3 %reduce-scatter.40.cloned.1.call-start = ((), (), s32[]{:S(2)}) async-start(), calls=%async_computation.35 | async-start | bytes 2359296 | tf_op jit(solution)/shard_map/reduce_scatter | solution.py:1090
  990.6 475.2 %reduce-scatter.38.cloned.1.call-start = ((), (), s32[]{:S(2)}) async-start(), calls=%async_computation.34 | async-start | bytes 2359296 | tf_op jit(solution)/shard_map/reduce_scatter | solution.py:1078
  996.1 471.8 %reduce-scatter.44.cloned.1.call-start = ((), (), s32[]{:S(2)}) async-start(), calls=%async_computation.37 | async-start | bytes 2359296 | tf_op jit(solution)/shard_map/reduce_scatter | solution.py:1093
  1004.4 463.5 %reduce-scatter.42.cloned.1.call-start = ((), (), s32[]{:S(2)}) async-start(), calls=%async_computation.36 | async-start | bytes 2359296 | tf_op jit(solution)/shard_map/reduce_scatter | solution.py:1081
  1010.6 459.4 %reduce-scatter.36.cloned.1.call-start = ((), (), s32[]{:S(2)}) async-start(), calls=%async_computation.33 | async-start | bytes 589824 | tf_op jit(solution)/shard_map/reduce_scatter | solution.py:1087
  1012.3 457.7 %reduce-scatter.34.cloned.1.call-start = ((), (), s32[]{:S(2)}) async-start(), calls=%async_computation.32 | async-start | bytes 589824 | tf_op jit(solution)/shard_map/reduce_scatter | solution.py:1075
  1033.0 438.7 %reduce-scatter.32.cloned.1.call-start = ((), (), s32[]{:S(2)}) async-start(), calls=%async_computation.31 | async-start | bytes 1769472 | tf_op jit(solution)/shard_map/reduce_scatter | solution.py:1084
  1038.0 433.7 %reduce-scatter.30.cloned.1.call-start = ((), (), s32[]{:S(2)}) async-start(), calls=%async_computation.30 | async-start | bytes 1769472 | tf_op jit(solution)/shard_map/reduce_scatter | solution.py:1072
  1192.5 281.1 %reduce-scatter.28.cloned.1.call-start = ((), (), s32[]{:S(2)}) async-start(), calls=%async_computation.29 | async-start | bytes 2621440 | tf_op jit(solution)/shard_map/reduce_scatter | solution.py:844
  1424.3 49.4 %copy-start.2 = (bf16[256,1024]{1,0:T(8,128)(2,1)S(1)}, bf16[256,1024]{1,0:T(8,128)(2,1)}, u32[]{:S(2)}) copy-start(bf16[256,1024]{1,0:T(8,128)(2,1)} %refs_0_.1) | copy-start | bytes 1572868
  1424.3 49.3 %copy-start.57 = (f32[1,1,1024]{2,1,0:T(1,128)S(1)}, f32[1,1,1024]{2,1,0:T(1,128)}, u32[]{:S(2)}) copy-start(f32[1,1,1024]{2,1,0:T(1,128)} %copy-done.56) | copy-start | bytes 12292
  1424.3 49.3 %copy-start.74 = (f32[256]{0:T(256)S(1)}, f32[256]{0:T(256)}, u32[]{:S(2)}) copy-start(f32[256]{0:T(256)} %copy-done.73) | copy-start | bytes 3076
  1424.3 50.8 %copy-start.92 = (f32[256]{0:T(256)S(1)}, f32[256]{0:T(256)}, u32[]{:S(2)}) copy-start(f32[256]{0:T(256)} %copy-done.91) | copy-start | bytes 3076
  1424.3 50.8 %copy-start.90 = (f32[256]{0:T(256)S(1)}, f32[256]{0:T(256)}, u32[]{:S(2)}) copy-start(f32[256]{0:T(256)} %copy-done.89) | copy-start | bytes 3076
  1424.3 52.4 %copy-start.79 = (f32[1024]{0:T(1024)S(1)}, f32[1024]{0:T(1024)}, u32[]{:S(2)}) copy-start(f32[1024]{0:T(1024)} %get-tuple-element.1497) | copy-start | bytes 12292
  1424.3 52.4 %copy-start.82 = (f32[1024]{0:T(1024)S(1)}, f32[1024]{0:T(1024)}, u32[]{:S(2)}) copy-start(f32[1024]{0:T(1024)} %get-tuple-element.1495) | copy-start | bytes 12292
  1424.3 52.4 %copy-start.84 = (f32[1024]{0:T(1024)S(1)}, f32[1024]{0:T(1024)}, u32[]{:S(2)}) copy-start(f32[1024]{0:T(1024)} %get-tuple-element.1493) | copy-start | bytes 12292
  1424.3 52.5 %copy-start.78 = (f32[1024]{0:T(1024)S(1)}, f32[1024]{0:T(1024)}, u32[]{:S(2)}) copy-start(f32[1024]{0:T(1024)} %get-tuple-element.1507) | copy-start | bytes 12292
  1424.3 52.5 %copy-start.80 = (f32[1024]{0:T(1024)S(1)}, f32[1024]{0:T(1024)}, u32[]{:S(2)}) copy-start(f32[1024]{0:T(1024)} %get-tuple-element.1505) | copy-start | bytes 12292
  1424.4 52.5 %copy-start.83 = (f32[1024]{0:T(1024)S(1)}, f32[1024]{0:T(1024)}, u32[]{:S(2)}) copy-start(f32[1024]{0:T(1024)} %get-tuple-element.1503) | copy-start | bytes 12292
  1424.4 94.0 %copy-start.7 = (bf16[256,1024]{1,0:T(8,128)(2,1)S(1)}, bf16[256,1024]{1,0:T(8,128)(2,1)}, u32[]{:S(2)}) copy-start(bf16[256,1024]{1,0:T(8,128)(2,1)} %reduce-scatter.16.cloned.1.call-done) | copy-start | bytes 1572868
  1424.4 94.0 %copy-start.17 = (f32[256,1024]{1,0:T(8,128)S(1)}, f32[256,1024]{1,0:T(8,128)}, u32[]{:S(2)}) copy-start(f32[256,1024]{1,0:T(8,128)} %copy-done.16) | copy-start | bytes 3145732
  1424.4 94.0 %copy-start.23 = (bf16[256,1024]{1,0:T(8,128)(2,1)S(1)}, bf16[256,1024]{1,0:T(8,128)(2,1)}, u32[]{:S(2)}) copy-start(bf16[256,1024]{1,0:T(8,128)(2,1)} %reduce-scatter.26.cloned.1.call-done) | copy-start | bytes 1572868
  1424.4 94.0 %copy-start.66 = (f32[256]{0:T(256)S(1)}, f32[256]{0:T(256)}, u32[]{:S(2)}) copy-start(f32[256]{0:T(256)} %copy-done.64) | copy-start | bytes 3076
  1424.4 94.0 %copy-start.77 = (f32[256]{0:T(256)S(1)}, f32[256]{0:T(256)}, u32[]{:S(2)}) copy-start(f32[256]{0:T(256)} %copy-done.75) | copy-start | bytes 3076
  1424.4 94.0 %copy-start.86 = (f32[256]{0:T(256)S(1)}, f32[256]{0:T(256)}, u32[]{:S(2)}) copy-start(f32[256]{0:T(256)} %copy-done.85) | copy-start | bytes 3076
  1424.4 94.0 %copy-start.98 = (f32[256]{0:T(256)S(1)}, f32[256]{0:T(256)}, u32[]{:S(2)}) copy-start(f32[256]{0:T(256)} %copy-done.97) | copy-start | bytes 3076
  1470.0 51.2 %copy-start.48 = (bf16[256,1024]{1,0:T(8,128)(2,1)S(1)}, bf16[256,1024]{1,0:T(8,128)(2,1)}, u32[]{:S(2)}) copy-start(bf16[256,1024]{1,0:T(8,128)(2,1)} %get-tuple-element.2643) | copy-start | bytes 1572868
  (72 other events, 928.7 us)
Sparse Core Ops, SparseCore 0:
  14.2 48.6 all-gather.16
  130.8 50.8 reduce-scatter.15
  186.6 45.2 all-gather.18
  252.1 42.5 reduce-scatter.17
  297.6 45.2 all-gather.20
  411.9 56.8 reduce-scatter.19
  471.5 45.2 all-gather.22
  518.5 44.6 all-gather.24
  576.5 42.5 reduce-scatter.21
  626.1 45.2 all-gather.26
  827.8 41.6 reduce-scatter.23
  876.4 45.2 all-gather.28
  935.1 42.5 reduce-scatter.25
  984.6 45.2 all-gather.30
  1032.9 39.9 reduce-scatter.39
  1076.4 41.2 reduce-scatter.37
  1120.8 41.1 reduce-scatter.43
  1165.6 41.2 reduce-scatter.41
  1209.9 34.9 reduce-scatter.35
  1248.1 37.8 reduce-scatter.33
  1289.3 45.9 reduce-scatter.31
  1338.6 46.2 reduce-scatter.29
  1387.2 44.9 reduce-scatter.27

commit v2 on v1

v2 whole, which is shorter than its diff:
```python
import functools
import types
import typing

import jax
import jax.numpy as jnp
from jax import lax
from jax.experimental import pallas as pl
from jax.experimental.pallas import tpu as pltpu
from jax.sharding import PartitionSpec as P

HD = 64
EPS_NORM = 1e-05
EPS_DEN = 1e-06
MESH = pl.DeviceIdType.MESH
BF = jnp.bfloat16
F32 = jnp.float32
LAG_FIRST, LAG_SECOND, LAG_CORE, LAG_READY = 2, 4, 6, 7
RING = 4
ROOT_HALF = 0.7071067811865476
ROOT_TAU = 0.3989422804014327


def sizes_of(mesh, tokens, weight_in, weight_up):
    s = types.SimpleNamespace()
    s.R, s.Z = mesh.shape["rows"], mesh.shape["feat"]
    chips = s.R // 2
    s.NX = 1
    while s.NX * s.NX < chips:
        s.NX *= 2
    s.NY = chips // s.NX
    s.T, s.D = tokens.shape
    s.L = weight_in.shape[0]
    s.PC = weight_in.shape[3]
    s.PR = s.D // s.R
    s.NJ = weight_up.shape[2] // s.PC
    s.NU = 4 + 2 * s.NJ
    s.U = s.L * s.NU
    s.NP = s.PC // 128
    s.MR = s.NP * HD + 16
    s.NQ = s.NY * s.NX
    return s


def place(s):
    r, z = lax.axis_index("rows"), lax.axis_index("feat")
    return r, z, r // (2 * s.NX), (r // 2) % s.NX, r % 2


def row_at(s, y, x, c):
    return (y * s.NX + x) * 2 + c


def greet(s, r, z):
    barrier = pltpu.get_barrier_semaphore()
    peers = [((r + d) % s.R, z) for d in range(1, s.R)] + [(r, (z + d) % s.Z) for d in range(1, s.Z)]
    for peer in peers:
        pl.semaphore_signal(barrier, inc=1, device_id=peer, device_id_type=MESH)
    pl.semaphore_wait(barrier, len(peers))


def remote(src, dst, send, recv, device):
    return pltpu.make_async_remote_copy(
        src_ref=src, dst_ref=dst, send_sem=send, recv_sem=recv, device_id=device, device_id_type=MESH
    )


def dot(a, b, dims=((1,), (0,))):
    return lax.dot_general(a, b, (dims, ((), ())), preferred_element_type=F32)


NT = ((1,), (1,))
TN = ((0,), (0,))


def norm_parts(v):
    center = jnp.mean(v, axis=-1, keepdims=True)
    shifted = v - center
    spread = jnp.mean(shifted * shifted, axis=-1, keepdims=True)
    inv = lax.rsqrt(spread + EPS_NORM)
    return shifted * inv, inv


def weight_gather(s, h, r, z, y, x, c):
    half = s.PR // 2
    F, piece = h.whole, h.piece
    rows = (pl.ds(0, half), pl.ds(half, half))

    def z_copies(u):
        return [
            remote(
                piece.at[u // s.NU, u % s.NU],
                F.at[u, s.Z - d - 1, y, x, c],
                h.z_send.at[u % RING, d - 1],
                h.z_recv.at[u, s.Z - d - 1],
                (r, (z + d) % s.Z),
            )
            for d in range(1, s.Z)
        ]

    def first(u):
        out = []
        for d in range(1, s.NX):
            at = F.at[u, :, y, x, c, rows[0]]
            out.append(remote(at, at, h.x_send.at[u % RING, 0, d - 1], h.x_recv.at[u, 0, s.NX - d - 1],
                              (row_at(s, y, (x + d) % s.NX, c), z)))
        for d in range(1, s.NY):
            at = F.at[u, :, y, x, c, rows[1]]
            out.append(remote(at, at, h.y_send.at[u % RING, 0, d - 1], h.y_recv.at[u, 0, s.NY - d - 1],
                              (row_at(s, (y + d) % s.NY, x, c), z)))
        return out

    def first_landing(u):
        out = []
        for d in range(1, s.NX):
            at = F.at[u, :, y, (x + d) % s.NX, c, rows[0]]
            out.append(remote(at, at, h.x_send.at[u % RING, 0, d - 1], h.x_recv.at[u, 0, d - 1], (r, z)))
        for d in range(1, s.NY):
            at = F.at[u, :, (y + d) % s.NY, x, c, rows[1]]
            out.append(remote(at, at, h.y_send.at[u % RING, 0, d - 1], h.y_recv.at[u, 0, d - 1], (r, z)))
        return out

    def second(u):
        out = []
        for d in range(1, s.NY):
            at = F.at[u, :, y, :, c, rows[0]]
            out.append(remote(at, at, h.y_send.at[u % RING, 1, d - 1], h.y_recv.at[u, 1, s.NY - d - 1],
                              (row_at(s, (y + d) % s.NY, x, c), z)))
        for d in range(1, s.NX):
            at = F.at[u, :, :, x, c, rows[1]]
            out.append(remote(at, at, h.x_send.at[u % RING, 1, d - 1], h.x_recv.at[u, 1, s.NX - d - 1],
                              (row_at(s, y, (x + d) % s.NX, c), z)))
        return out

    def second_landing(u):
        out = []
        for d in range(1, s.NY):
            at = F.at[u, :, (y + d) % s.NY, :, c, rows[0]]
            out.append(remote(at, at, h.y_send.at[u % RING, 1, d - 1], h.y_recv.at[u, 1, d - 1], (r, z)))
        for d in range(1, s.NX):
            at = F.at[u, :, :, (x + d) % s.NX, c, rows[1]]
            out.append(remote(at, at, h.x_send.at[u % RING, 1, d - 1], h.x_recv.at[u, 1, d - 1], (r, z)))
        return out

    def share(u):
        at = F.at[u, :, :, :, c]
        return remote(at, at, h.c_send.at[u % RING], h.c_recv.at[u], (row_at(s, y, x, 1 - c), z))

    def share_landing(u):
        at = F.at[u, :, :, :, 1 - c]
        return remote(at, at, h.c_send.at[u % RING], h.c_recv.at[u], (r, z))

    def z_landing(u):
        return [
            remote(piece.at[0, 0], F.at[u, k, y, x, c], h.z_send.at[u % RING, 0], h.z_recv.at[u, k], (r, z))
            for k in range(s.Z - 1)
        ]

    def inside(u, what):
        pl.when((u >= 0) & (u < s.U))(functools.partial(what, u))

    def stage_z(u):
        for cp in z_copies(u):
            cp.start()

    def stage_first(u):
        for cp in z_landing(u):
            cp.wait_recv()
        for cp in first(u):
            cp.start()

    def stage_second(u):
        for cp in first_landing(u):
            cp.wait_recv()
        for cp in second(u):
            cp.start()

    def stage_core(u):
        for cp in second_landing(u):
            cp.wait_recv()
        share(u).start()

    def stage_ready(u):
        share_landing(u).wait_recv()

    def tick(t):
        inside(t - RING, lambda u: [cp.wait_send() for cp in z_copies(u)] and None)
        inside(t, stage_z)
        inside(t - LAG_FIRST - RING, lambda u: [cp.wait_send() for cp in first(u)] and None)
        inside(t - LAG_FIRST, stage_first)
        inside(t - LAG_SECOND - RING, lambda u: [cp.wait_send() for cp in second(u)] and None)
        inside(t - LAG_SECOND, stage_second)
        inside(t - LAG_CORE - RING, lambda u: share(u).wait_send())
        inside(t - LAG_CORE, stage_core)
        inside(t - LAG_READY, stage_ready)

    def drain_all():
        @pl.loop(s.U + LAG_READY, s.U + LAG_CORE + RING)
        def _(t):
            tick(t)

    return tick, drain_all


def head_masks(s):
    lane = lax.broadcasted_iota(jnp.int32, (1, 128), 1)
    first = lane < HD
    return first, jnp.where(first, 1.0, 0.0), jnp.where(first, 0.0, 1.0)


def pair_ones():
    row = lax.broadcasted_iota(jnp.int32, (128, 128), 0) // HD
    col = lax.broadcasted_iota(jnp.int32, (128, 128), 1) // HD
    return jnp.where(row == col, 1.0, 0.0).astype(BF)


def lanes(at, width):
    return pl.ds(pl.multiple_of(at * width, width), width)


def prefix_rounds(s, h, l, r, z):
    msg, got, rows_got, back, out = h.msg, h.r1, h.r2, h.pre, h.r3

    def one(k):
        return remote(msg.at[k], got.at[s.Z - k], h.r1_send.at[l, k], h.r1_recv.at[l, s.Z - k], (r, (z + k) % s.Z))

    def two(d):
        return remote(rows_got.at[r], rows_got.at[r], h.r2_send.at[l, d], h.r2_recv.at[l, s.R - d],
                      ((r + d) % s.R, z))

    def two_landing(d):
        at = rows_got.at[(r + d) % s.R]
        return remote(at, at, h.r2_send.at[l, d], h.r2_recv.at[l, d], (r, z))

    def three(k):
        return remote(back.at[k], out.at[s.Z - k], h.r3_send.at[l, k], h.r3_recv.at[l, s.Z - k], (r, (z + k) % s.Z))

    def round_one():
        for k in range(1, s.Z):
            one(k).start()

    def round_two():
        for k in range(1, s.Z):
            remote(msg.at[k], got.at[k], h.r1_send.at[l, k], h.r1_recv.at[l, k], (r, z)).wait_recv()
        total = h.coef_a[0] * msg[0].astype(F32)
        for k in range(1, s.Z):
            total = total + h.coef_a[k] * got[k].astype(F32)
        rows_got[r] = total.astype(BF)
        for d in range(1, s.R):
            two(d).start()

    def round_three():
        for d in range(1, s.R):
            two_landing(d).wait_recv()
        for k in range(s.Z):
            total = h.coef_b[k * s.Z] * msg[0].astype(F32)
            for j in range(1, s.Z):
                total = total + h.coef_b[k * s.Z + j] * got[j].astype(F32)
            for q in range(s.R):
                total = total + h.coef_c[k * s.R + q] * rows_got[q].astype(F32)
            if k == 0:
                out[0] = total.astype(BF)
            else:
                back[k] = total.astype(BF)
                three(k).start()

    def arrive():
        for k in range(1, s.Z):
            remote(back.at[k], out.at[k], h.r3_send.at[l, k], h.r3_recv.at[l, k], (r, z)).wait_recv()

    def settle():
        for k in range(1, s.Z):
            one(k).wait_send()
            three(k).wait_send()
        for d in range(1, s.R):
            two(d).wait_send()

    return round_one, round_two, round_three, arrive, settle


def pack_state(full, first):
    return jnp.where(first, full[:HD], full[HD:])


def unpack_state(packed, first):
    zero = jnp.zeros_like(packed)
    return jnp.concatenate([jnp.where(first, packed, zero), jnp.where(first, zero, packed)], axis=0)


def spread_rows(s, rows_list):
    at = lax.broadcasted_iota(jnp.int32, (16, 128), 0)
    block = jnp.zeros((16, 128), F32)
    for i, row in enumerate(rows_list):
        block = block + jnp.where(at == i, row, 0.0)
    return block


def pick_row(block, i):
    at = lax.broadcasted_iota(jnp.int32, (16, 128), 0)
    return jnp.sum(jnp.where(at == i, block.astype(F32), 0.0), axis=0, keepdims=True)


class FwdIn(typing.NamedTuple):
    tokens: object
    gain: object
    bias: object
    coef_a: object
    coef_b: object
    coef_c: object
    w_in: object
    w_mix: object
    w_up: object
    w_down: object
class FwdOut(typing.NamedTuple):
    output: object
    logs: object
    whole: object
    k_stream: object
    k_middle: object
    k_qkv: object
    k_mixed: object
    k_den: object
    k_state: object
    k_act: object
    k_slope: object
    k_normt: object
    s_mixed: object
    s_act: object


def fwd_scratch(s):
    dma = pltpu.SemaphoreType.DMA
    return dict(
        piece=pltpu.VMEM((s.L, s.NU, s.PR, s.PC), BF),
        w=pltpu.VMEM((s.Z, s.NY, s.NX, 2, s.PR, s.PC), BF),
        stream=pltpu.VMEM((s.T, s.D), F32),
        acc=pltpu.VMEM((s.T, s.D), F32),
        middle=pltpu.VMEM((s.T, s.D), F32),
        den=pltpu.VMEM((s.T, s.D), F32),
        nrm=pltpu.VMEM((s.T, s.D), BF),
        nrmt=pltpu.VMEM((2, s.NY, s.NX, 2, s.PR, s.T), BF),
        qkv=pltpu.VMEM((3, s.T, s.D), BF),
        mixed=pltpu.VMEM((s.T, s.D), BF),
        act=pltpu.VMEM((s.NJ, s.T, s.D), BF),
        slope=pltpu.VMEM((s.NJ, s.T, s.D), BF),
        msg=pltpu.VMEM((s.Z, s.MR, 128), BF),
        r1=pltpu.VMEM((s.Z, s.MR, 128), BF),
        r2=pltpu.VMEM((s.R, s.MR, 128), BF),
        pre=pltpu.VMEM((s.Z, s.MR, 128), BF),
        r3=pltpu.VMEM((s.Z, s.MR, 128), BF),
        piece_sem=dma((2 + 2 * s.NJ,)),
        w_sem=dma((s.Z,)),
        z_send=dma((RING, s.Z - 1)),
        z_recv=dma((s.U, s.Z - 1)),
        x_send=dma((RING, 2, s.NX - 1)),
        x_recv=dma((s.U, 2, s.NX - 1)),
        y_send=dma((RING, 2, s.NY - 1)),
        y_recv=dma((s.U, 2, s.NY - 1)),
        c_send=dma((RING,)),
        c_recv=dma((s.U,)),
        r1_send=dma((s.L, s.Z)),
        r1_recv=dma((s.L, s.Z)),
        r2_send=dma((s.L, s.R)),
        r2_recv=dma((s.L, s.R)),
        r3_send=dma((s.L, s.Z)),
        r3_recv=dma((s.L, s.Z)),
        keep=dma((8,)),
        keep_j=dma((2, s.NJ)),
        sib_send=dma((3 + s.NJ,)),
        sib_recv=dma((s.L, 3 + s.NJ)),
    )


def fwd_kernel(s, *refs):
    names = FwdIn._fields + FwdOut._fields + tuple(fwd_scratch(s))
    h = types.SimpleNamespace(**dict(zip(names, refs, strict=True)))
    r, z, y, x, c = place(s)
    sibling = (row_at(s, y, x, 1 - c), z)
    greet(s, r, z)
    tick, drain_all = weight_gather(s, h, r, z, y, x, c)
    first, _, _ = head_masks(s)

    pieces = [
        pltpu.make_async_copy(h.w_in.at[:, :, y, x, c], h.piece.at[:, 0:3], h.piece_sem.at[0]),
        pltpu.make_async_copy(h.w_mix.at[:, y, x, c], h.piece.at[:, 3], h.piece_sem.at[1]),
    ]
    for j in range(s.NJ):
        cols = pl.ds(j * s.PC, s.PC)
        pieces.append(pltpu.make_async_copy(h.w_up.at[:, y, x, c, :, cols], h.piece.at[:, 4 + j], h.piece_sem.at[2 + j]))
        pieces.append(pltpu.make_async_copy(h.w_down.at[:, y, x, c, :, cols], h.piece.at[:, 4 + s.NJ + j],
                                            h.piece_sem.at[2 + s.NJ + j]))
    for cp in pieces:
        cp.start()
    for cp in pieces:
        cp.wait()

    with_unit = unit_reader(s, h)

    def normalize(l, n, source):
        xhat, _ = norm_parts(source)
        v = xhat * h.gain[pl.ds(l * 2 + n, 1), :] + h.bias[pl.ds(l * 2 + n, 1), :]
        h.nrm[...] = v.astype(BF)
        h.nrmt[n] = v.T.astype(BF).reshape(s.NY, s.NX, 2, s.PR, s.T)
        keep_norm(l, n).start()
        send_norm(l, n).start()

    def keep_norm(l, n):
        return pltpu.make_async_copy(h.nrmt.at[n, :, :, c], h.k_normt.at[l, n, 0], h.keep.at[n])

    def send_norm(l, n):
        return remote(h.nrmt.at[n, :, :, 1 - c], h.k_normt.at[l, n, 1], h.sib_send.at[n], h.sib_recv.at[l, n],
                      sibling)

    def keep_one(l, index):
        src, dst = ((h.stream, h.k_stream), (h.qkv, h.k_qkv), (h.mixed, h.k_mixed), (h.den, h.k_den),
                    (h.middle, h.k_middle), (h.r3, h.k_state))[index - 2]
        return pltpu.make_async_copy(src, dst.at[l], h.keep.at[index])

    def send_mixed(l):
        return remote(h.mixed, h.s_mixed.at[l], h.sib_send.at[2], h.sib_recv.at[l, 2], sibling)

    def keep_act(l, j):
        return pltpu.make_async_copy(h.act.at[j], h.k_act.at[l, j], h.keep_j.at[0, j])

    def keep_slope(l, j):
        return pltpu.make_async_copy(h.slope.at[j], h.k_slope.at[l, j], h.keep_j.at[1, j])

    def send_act(l, j):
        return remote(h.act.at[j], h.s_act.at[l, j], h.sib_send.at[3 + j], h.sib_recv.at[l, 3 + j], sibling)

    h.stream[...] = h.tokens[...].astype(F32)
    h.logs[...] = jnp.where(lax.broadcasted_iota(jnp.int32, (8, 128), 0) == 1, -jnp.inf, 0.0)
    ones = pair_ones()
    tall = jnp.ones((s.T, 128), BF)

    @pl.loop(0, LAG_READY)
    def _(t):
        tick(t)

    def one_layer(l, carry):
        base = l * s.NU
        keep_one(l, 2).start()
        normalize(l, 0, h.stream[...])

        def project(kind, carry):
            u = base + kind

            def body(k, weight):
                v = dot(h.nrm[...], weight)
                phi = jnp.where(v > 0, v + 1.0, jnp.exp(jnp.minimum(v, 0.0)))
                h.qkv[kind, :, lanes(k, s.PC)] = jnp.where(kind < 2, phi, v).astype(BF)

            with_unit(h.w_in, l, kind, u, body, lambda: tick(u + LAG_READY))
            return carry

        lax.fori_loop(0, 3, project, 0)
        keep_one(l, 3).start()
        round_one, round_two, round_three, arrive, settle = prefix_rounds(s, h, l, r, z)

        def local_state(k, carry):
            totals = []
            for i in range(s.NP):
                at = lanes(k * s.NP + i, 128)
                keys, vals = h.qkv[1, :, at], h.qkv[2, :, at]
                h.msg[k, i * HD:(i + 1) * HD] = pack_state(dot(keys, vals, TN), first).astype(BF)
                totals.append(jnp.sum(keys.astype(F32), axis=0, keepdims=True))
            h.msg[k, s.NP * HD:] = spread_rows(s, totals).astype(BF)
            return carry

        lax.fori_loop(0, s.Z, local_state, 0)
        round_one()
        tick(base + 3 + LAG_READY)
        round_two()
        tick(base + 4 + LAG_READY)
        round_three()
        tick(base + 5 + LAG_READY)
        arrive()
        keep_one(l, 7).start()
        causal = (lax.broadcasted_iota(jnp.int32, (s.T, s.T), 1) <= lax.broadcasted_iota(jnp.int32, (s.T, s.T), 0))

        def attend(p, carry):
            k, i = p // s.NP, p % s.NP
            at = lanes(p, 128)
            query, key, value = h.qkv[0, :, at], h.qkv[1, :, at], h.qkv[2, :, at]
            wide = query.astype(F32)
            value_ones = jnp.concatenate([value, tall], axis=1)
            zero = jnp.zeros_like(query)
            results = []
            for head in range(2):
                mine = first if head == 0 else jnp.logical_not(first)
                scores = dot(jnp.where(mine, query, zero), key, NT)
                weights = jnp.where(causal, scores, 0.0).astype(BF)
                results.append(dot(weights, value_ones))
            state = unpack_state(h.r3[k, pl.ds(pl.multiple_of(i * HD, HD), HD), :], first)
            total = pick_row(h.r3[k, s.NP * HD:, :], i)
            square = jnp.zeros((128, 128), BF)
            right = jnp.concatenate(
                [jnp.concatenate([state, square], axis=1), jnp.concatenate([square, ones], axis=1)], axis=0)
            left = jnp.concatenate([query, (wide * total).astype(BF)], axis=1)
            earlier = dot(left, right)
            num = jnp.where(first, results[0][:, :128], results[1][:, :128]) + earlier[:, :128]
            den = jnp.where(first, results[0][:, 128:], results[1][:, 128:]) + earlier[:, 128:] + EPS_DEN
            h.mixed[:, at] = (num / den).astype(BF)
            h.den[:, at] = den
            logs = jnp.log(den)
            h.logs[0:1] += jnp.sum(logs, axis=0, keepdims=True)
            h.logs[1:2] = jnp.maximum(h.logs[1:2], jnp.max(logs, axis=0, keepdims=True))
            return carry

        half = s.Z * s.NP // 2
        lax.fori_loop(0, half, attend, 0)
        tick(base + 6 + LAG_READY)
        lax.fori_loop(half, s.Z * s.NP, attend, 0)
        settle()
        keep_one(l, 4).start()
        send_mixed(l).start()
        keep_one(l, 5).start()

        h.acc[...] = jnp.zeros_like(h.acc)

        def mix(k, weight):
            h.acc[...] += dot(h.mixed[:, lanes(k, s.PC)], weight, NT)

        with_unit(h.w_mix, l, 0, base + 3, mix)
        h.middle[...] = h.stream[...] + h.acc[...]
        keep_one(l, 6).start()
        normalize(l, 1, h.middle[...])

        def up(j, carry):
            u = base + 4 + j

            def body(k, weight):
                v = dot(h.nrm[...], weight)
                cdf = 0.5 * (1.0 + lax.erf(v * ROOT_HALF))
                h.act[j, :, lanes(k, s.PC)] = (v * cdf).astype(BF)
                h.slope[j, :, lanes(k, s.PC)] = (cdf + v * (ROOT_TAU * jnp.exp(-0.5 * v * v))).astype(BF)

            with_unit(h.w_up, l, j, u, body, lambda: pl.when(j >= 3)(lambda: tick(u + LAG_READY)))
            keep_act(l, j).start()
            keep_slope(l, j).start()
            send_act(l, j).start()
            return carry

        lax.fori_loop(0, s.NJ, up, 0)
        h.acc[...] = jnp.zeros_like(h.acc)

        def down(j, carry):
            u = base + 4 + s.NJ + j

            def body(k, weight):
                h.acc[...] += dot(h.act[j, :, lanes(k, s.PC)], weight, NT)

            with_unit(h.w_down, l, j, u, body, lambda: tick(u + LAG_READY))
            return carry

        lax.fori_loop(0, s.NJ, down, 0)
        keep_one(l, 2).wait()
        h.stream[...] = h.middle[...] + h.acc[...]
        for n in range(2):
            keep_norm(l, n).wait()
            send_norm(l, n).wait_send()
            send_norm(l, n).wait_recv()
        for index in range(3, 8):
            keep_one(l, index).wait()
        send_mixed(l).wait()

        def finish(j, carry):
            keep_act(l, j).wait()
            keep_slope(l, j).wait()
            send_act(l, j).wait()
            return carry

        lax.fori_loop(0, s.NJ, finish, 0)
        return carry

    lax.fori_loop(0, s.L, one_layer, 0)
    h.output[...] = h.stream[...].astype(BF)
    drain_all()


def split_rows(s, weight_in, *rest):
    cut = (s.NY, s.NX, 2, s.PR)
    turned = jnp.transpose(weight_in, (0, 2, 1, 3)).reshape((s.L, 3) + cut + (s.PC,))
    return (turned,) + tuple(w.reshape((s.L,) + cut + w.shape[2:]) for w in rest)


def forward_call(s, tokens, gain, bias, coefs, weights):
    vmem = pl.BlockSpec(memory_space=pltpu.VMEM)
    smem = pl.BlockSpec(memory_space=pltpu.SMEM)
    hbm = pl.BlockSpec(memory_space=pl.ANY)
    shape = jax.ShapeDtypeStruct
    outs = FwdOut(
        output=shape((s.T, s.D), BF),
        logs=shape((8, 128), F32),
        whole=shape((s.U, s.Z - 1, s.NY, s.NX, 2, s.PR, s.PC), BF),
        k_stream=shape((s.L, s.T, s.D), F32),
        k_middle=shape((s.L, s.T, s.D), F32),
        k_qkv=shape((s.L, 3, s.T, s.D), BF),
        k_mixed=shape((s.L, s.T, s.D), BF),
        k_den=shape((s.L, s.T, s.D), F32),
        k_state=shape((s.L, s.Z, s.MR, 128), BF),
        k_act=shape((s.L, s.NJ, s.T, s.D), BF),
        k_slope=shape((s.L, s.NJ, s.T, s.D), BF),
        k_normt=shape((s.L, 2, 2, s.NY, s.NX, s.PR, s.T), BF),
        s_mixed=shape((s.L, s.T, s.D), BF),
        s_act=shape((s.L, s.NJ, s.T, s.D), BF),
    )
    out = pl.pallas_call(
        functools.partial(fwd_kernel, s),
        out_shape=list(outs),
        in_specs=[vmem] * 3 + [smem] * 3 + [hbm] * 4,
        out_specs=[vmem] * 2 + [hbm] * (len(outs) - 2),
        scratch_shapes=list(fwd_scratch(s).values()),
        compiler_params=pltpu.CompilerParams(
            collective_id=0, has_side_effects=True, vmem_limit_bytes=56 * 1024 * 1024),
    )(tokens, gain, bias, *coefs, *weights)
    return FwdOut(*out)


def segments_of_units(s, image_length, image_start):
    first = jnp.arange(s.R * s.Z, dtype=jnp.int32) * s.T
    live = (image_length > 0)[None, :]
    return (jnp.sum(((image_start[None, :] <= first[:, None]) & live).astype(jnp.int32), axis=1) - 1).reshape(s.R, s.Z)


def coefficients(s, image_length, image_start):
    seg = segments_of_units(s, image_length, image_start)
    r, z = lax.axis_index("rows"), lax.axis_index("feat")
    turn = (z + jnp.arange(s.Z)) % s.Z
    row = seg[r][turn]
    order = jnp.arange(s.R)
    f = lambda v: v.astype(F32).reshape(-1)
    same = row[:, None] == row[None, :]
    forward = (
        f(row == seg[r, s.Z - 1]),
        f(same & (turn[None, :] < turn[:, None])),
        f((seg[None, :, s.Z - 1] == row[:, None]) & (order[None, :] < r)),
    )
    backward = (
        f(row == seg[r, 0]),
        f(same & (turn[None, :] > turn[:, None])),
        f((seg[None, :, 0] == row[:, None]) & (order[None, :] > r)),
    )
    return forward, backward


BACK_FIRST, BACK_SECOND, BACK_LAST = 2, 4, 6
SLOTS = 8
OUT_RING = 4
X_EARLY, X_LATE, X_DOWN, X_MIX = 0, 1, 2, 3

class BwdIn(typing.NamedTuple):
    cotangent: object
    logs: object
    gain: object
    coef_a: object
    coef_b: object
    coef_c: object
    w_in: object
    w_mix: object
    w_up: object
    w_down: object
    whole: object
    k_stream: object
    k_middle: object
    k_qkv: object
    k_mixed: object
    k_den: object
    k_state: object
    k_act: object
    k_slope: object
    k_normt: object
    s_mixed: object
    s_act: object
class BwdOut(typing.NamedTuple):
    grad: object
    vector: object
    g_in: object
    g_mix: object
    g_up: object
    g_down: object


def bwd_scratch(s):
    dma = pltpu.SemaphoreType.DMA
    half = s.PR // 2
    return dict(
        w=pltpu.VMEM((s.Z, s.NY, s.NX, 2, s.PR, s.PC), BF),
        part=pltpu.VMEM((SLOTS, s.NY, s.NX, s.Z, s.PR, s.PC), BF),
        land_x1=pltpu.VMEM((SLOTS, s.NX - 1, s.NY, s.Z, half, s.PC), BF),
        land_y1=pltpu.VMEM((SLOTS, s.NY - 1, s.NX, s.Z, half, s.PC), BF),
        land_x2=pltpu.VMEM((SLOTS, s.NX - 1, s.Z, half, s.PC), BF),
        land_y2=pltpu.VMEM((SLOTS, s.NY - 1, s.Z, half, s.PC), BF),
        land_z=pltpu.VMEM((SLOTS, s.Z - 1, s.PR, s.PC), BF),
        final=pltpu.VMEM((OUT_RING, s.PR, s.PC), F32),
        acc=pltpu.VMEM((s.T, s.D), F32),
        resid=pltpu.VMEM((s.T, s.D), F32),
        gb=pltpu.VMEM((s.T, s.D), BF),
        turned=pltpu.VMEM((s.NY, s.NX, 2, s.PR, s.T), BF),
        xt=pltpu.VMEM((4, 2, s.NY, s.NX, s.PR, s.T), BF),
        act=pltpu.VMEM((2, s.T, s.D), BF),
        slope=pltpu.VMEM((s.T, s.D), BF),
        ug=pltpu.VMEM((s.NJ, s.T, s.D), BF),
        ug_sib=pltpu.VMEM((s.NJ, s.T, s.D), BF),
        pg=pltpu.VMEM((3, s.T, s.D), BF),
        pg_sib=pltpu.VMEM((3, s.T, s.D), BF),
        qkv=pltpu.VMEM((3, s.T, s.D), BF),
        mixed=pltpu.VMEM((2, s.T, s.D), BF),
        den=pltpu.VMEM((s.T, s.D), F32),
        rg=pltpu.VMEM((s.T, s.D), BF),
        ng=pltpu.VMEM((s.T, s.D), BF),
        dg=pltpu.VMEM((s.T, s.D), F32),
        state=pltpu.VMEM((s.Z, s.MR, 128), BF),
        msg=pltpu.VMEM((s.Z, s.MR, 128), BF),
        r1=pltpu.VMEM((s.Z, s.MR, 128), BF),
        r2=pltpu.VMEM((s.R, s.MR, 128), BF),
        pre=pltpu.VMEM((s.Z, s.MR, 128), BF),
        r3=pltpu.VMEM((s.Z, s.MR, 128), BF),
        vec=pltpu.VMEM((16, s.D), F32),
        v_z=pltpu.VMEM((s.Z, 16, s.D), F32),
        v_c=pltpu.VMEM((2, 16, s.D), F32),
        v_x=pltpu.VMEM((s.NX, 16, s.D), F32),
        v_y=pltpu.VMEM((s.NY, 16, s.D), F32),
        w_sem=dma((s.Z,)),
        x1_send=dma((SLOTS, s.NX - 1)),
        x1_recv=dma((SLOTS, s.NX - 1)),
        y1_send=dma((SLOTS, s.NY - 1)),
        y1_recv=dma((SLOTS, s.NY - 1)),
        x2_send=dma((SLOTS, s.NX - 1)),
        x2_recv=dma((SLOTS, s.NX - 1)),
        y2_send=dma((SLOTS, s.NY - 1)),
        y2_recv=dma((SLOTS, s.NY - 1)),
        z_send=dma((SLOTS, s.Z - 1)),
        z_recv=dma((SLOTS, s.Z - 1)),
        out_sem=dma((OUT_RING,)),
        xt_sem=dma((2, 2, s.NQ)),
        xt_send=dma((2, s.NQ)),
        xt_recv=dma((s.L, 2, s.NQ)),
        g_send=dma((s.NJ + 3,)),
        g_recv=dma((s.L, s.NJ + 3)),
        get=dma((8,)),
        r1_send=dma((s.L, s.Z)),
        r1_recv=dma((s.L, s.Z)),
        r2_send=dma((s.L, s.R)),
        r2_recv=dma((s.L, s.R)),
        r3_send=dma((s.L, s.Z)),
        r3_recv=dma((s.L, s.Z)),
        v_send=dma((4, max(s.Z, s.NX, s.NY))),
        v_recv=dma((4, max(s.Z, s.NX, s.NY))),
    )


def gradient_sums(s, h, r, z, y, x, c):
    half = s.PR // 2
    rows = (pl.ds(0, half), pl.ds(half, half))
    part = h.part

    def to_x(d):
        return (row_at(s, y, (x + d) % s.NX, c), z)

    def to_y(d):
        return (row_at(s, (y + d) % s.NY, x, c), z)

    def first(v):
        b = v % SLOTS
        return [
            remote(part.at[b, :, d, :, rows[0]], h.land_x1.at[b, s.NX - d - 1], h.x1_send.at[b, d - 1],
                   h.x1_recv.at[b, s.NX - d - 1], to_x(d)) for d in range(1, s.NX)
        ] + [
            remote(part.at[b, d, :, :, rows[1]], h.land_y1.at[b, s.NY - d - 1], h.y1_send.at[b, d - 1],
                   h.y1_recv.at[b, s.NY - d - 1], to_y(d)) for d in range(1, s.NY)
        ]

    def second(v):
        b = v % SLOTS
        return [
            remote(part.at[b, d, 0, :, rows[0]], h.land_y2.at[b, s.NY - d - 1], h.y2_send.at[b, d - 1],
                   h.y2_recv.at[b, s.NY - d - 1], to_y(d)) for d in range(1, s.NY)
        ] + [
            remote(part.at[b, 0, d, :, rows[1]], h.land_x2.at[b, s.NX - d - 1], h.x2_send.at[b, d - 1],
                   h.x2_recv.at[b, s.NX - d - 1], to_x(d)) for d in range(1, s.NX)
        ]

    def last(v):
        b = v % SLOTS
        return [
            remote(part.at[b, 0, 0, d], h.land_z.at[b, s.Z - d - 1], h.z_send.at[b, d - 1],
                   h.z_recv.at[b, s.Z - d - 1], (r, (z + d) % s.Z)) for d in range(1, s.Z)
        ]

    def stage_second(v):
        b = v % SLOTS
        for cp in first(v):
            cp.wait_recv()

        def add(k, carry):
            for dy in range(s.NY):
                total = part[b, dy, 0, k, :half].astype(F32)
                for i in range(s.NX - 1):
                    total = total + h.land_x1[b, i, dy, k].astype(F32)
                part[b, dy, 0, k, :half] = total.astype(BF)
            for dx in range(s.NX):
                total = part[b, 0, dx, k, half:].astype(F32)
                for i in range(s.NY - 1):
                    total = total + h.land_y1[b, i, dx, k].astype(F32)
                part[b, 0, dx, k, half:] = total.astype(BF)
            return carry

        lax.fori_loop(0, s.Z, add, 0)
        for cp in second(v):
            cp.start()

    def stage_last(v):
        b = v % SLOTS
        for cp in second(v):
            cp.wait_recv()

        def add(k, carry):
            total = part[b, 0, 0, k, :half].astype(F32)
            for i in range(s.NY - 1):
                total = total + h.land_y2[b, i, k].astype(F32)
            part[b, 0, 0, k, :half] = total.astype(BF)
            total = part[b, 0, 0, k, half:].astype(F32)
            for i in range(s.NX - 1):
                total = total + h.land_x2[b, i, k].astype(F32)
            part[b, 0, 0, k, half:] = total.astype(BF)
            return carry

        lax.fori_loop(0, s.Z, add, 0)
        for cp in last(v):
            cp.start()

    def out_copy(at, o):
        return pltpu.make_async_copy(h.final.at[o], at, h.out_sem.at[o])

    def stage_out(v):
        b, o = v % SLOTS, v % OUT_RING
        for cp in last(v):
            cp.wait_recv()

        @pl.when(v >= OUT_RING)
        def _():
            out_copy(h.g_mix.at[0], o).wait()

        total = part[b, 0, 0, 0].astype(F32)
        for i in range(s.Z - 1):
            total = total + h.land_z[b, i].astype(F32)
        h.final[o] = total
        l, q = s.L - 1 - v // s.NU, v % s.NU
        wide = 2 * s.NJ
        pl.when((q < wide) & (q % 2 == 0))(lambda: out_copy(h.g_down.at[l, :, lanes(q // 2, s.PC)], o).start())
        pl.when((q < wide) & (q % 2 == 1))(lambda: out_copy(h.g_up.at[l, :, lanes(q // 2, s.PC)], o).start())
        pl.when(q == wide)(lambda: out_copy(h.g_mix.at[l], o).start())
        pl.when(q > wide)(lambda: out_copy(h.g_in.at[l, q - wide - 1], o).start())

    def inside(v, what):
        pl.when((v >= 0) & (v < s.U))(functools.partial(what, v))

    def wait_sends(v):
        for cp in first(v) + second(v) + last(v):
            cp.wait_send()

    def tick(t):
        def start(v):
            for cp in first(v):
                cp.start()

        inside(t, start)
        inside(t - BACK_FIRST, stage_second)
        inside(t - BACK_SECOND, stage_last)
        inside(t - BACK_LAST, stage_out)

    def produce(v, which, own, sibling):
        b = v % SLOTS
        inside(v - SLOTS, wait_sends)
        left = [h.xt[which, i].reshape(s.NQ * s.PR, s.T) for i in range(2)]

        def block(k, carry):
            at = lanes(k, s.PC)
            total = dot(left[0], own[:, at]) + dot(left[1], sibling[:, at])
            part[b, :, :, k] = total.astype(BF).reshape(s.NY, s.NX, s.PR, s.PC)
            return carry

        lax.fori_loop(0, s.Z, block, 0)
        tick(v)

    def drain():
        @pl.loop(s.U, s.U + BACK_LAST)
        def _(t):
            tick(t)

    def settle():
        @pl.loop(s.U - SLOTS, s.U)
        def _(v):
            wait_sends(v)

        for o in range(OUT_RING):
            out_copy(h.g_mix.at[0], o).wait()

    return produce, drain, settle


def bwd_kernel(s, *refs):
    names = BwdIn._fields + BwdOut._fields + tuple(bwd_scratch(s))
    h = types.SimpleNamespace(**dict(zip(names, refs, strict=True)))
    r, z, y, x, c = place(s)
    sibling = (row_at(s, y, x, 1 - c), z)
    greet(s, r, z)
    produce, drain, settle_sums = gradient_sums(s, h, r, z, y, x, c)
    first, _, _ = head_masks(s)
    ones = pair_ones()
    tall = jnp.ones((s.T, 128), BF)
    with_unit = unit_reader(s, h)
    squares = [(dy, dx) for dy in range(s.NY) for dx in range(s.NX)]

    def get(src, dst, index):
        return pltpu.make_async_copy(src, dst, h.get.at[index])

    def xt_loads(l):
        return [
            pltpu.make_async_copy(h.k_normt.at[l, n, i, (y + dy) % s.NY, (x + dx) % s.NX], h.xt.at[n, i, dy, dx],
                                  h.xt_sem.at[n, i, q])
            for n in range(2) for i in range(2) for q, (dy, dx) in enumerate(squares)
        ]

    def xt_sends(l, which):
        return [
            remote(h.turned.at[(y + dy) % s.NY, (x + dx) % s.NX, 1 - c], h.xt.at[which, 1, dy, dx],
                   h.xt_send.at[which - 2, q], h.xt_recv.at[l, which - 2, q], sibling)
            for q, (dy, dx) in enumerate(squares)
        ]

    def turn(l, which):
        wide = h.grad[...]
        h.gb[...] = wide.astype(BF)
        h.turned[...] = wide.T.astype(BF).reshape(s.NY, s.NX, 2, s.PR, s.T)
        for cp in xt_sends(l, which):
            cp.start()
        for dy, dx in squares:
            h.xt[which, 0, dy, dx] = h.turned[(y + dy) % s.NY, (x + dx) % s.NX, c]
        for cp in xt_sends(l, which):
            cp.wait_recv()

    def g_send(l, src, dst, j, index):
        return remote(src.at[j], dst.at[j], h.g_send.at[index], h.g_recv.at[l, index], sibling)

    def norm_back(l, n):
        back = h.acc[...]
        xhat, inv = norm_parts(h.resid[...])
        at = l * 2 + n
        h.vec[pl.ds(at, 1)] = jnp.sum(back * xhat, axis=0, keepdims=True)
        h.vec[pl.ds(2 * s.L + at, 1)] = jnp.sum(back, axis=0, keepdims=True)
        scaled = back * h.gain[pl.ds(at, 1), :]
        mean = jnp.mean(scaled, axis=-1, keepdims=True)
        along = jnp.mean(scaled * xhat, axis=-1, keepdims=True)
        h.grad[...] += inv * (scaled - mean - xhat * along)

    h.grad[...] = h.cotangent[...].astype(F32)
    h.vec[...] = jnp.zeros_like(h.vec)
    h.vec[4 * s.L:4 * s.L + 2, :128] = h.logs[0:2]

    def one_layer(li, carry):
        l = s.L - 1 - li
        base = li * s.NU
        unit = l * s.NU
        loads = [
            get(h.k_qkv.at[l], h.qkv, 0),
            get(h.k_mixed.at[l], h.mixed.at[0], 1),
            get(h.s_mixed.at[l], h.mixed.at[1], 2),
            get(h.k_den.at[l], h.den, 3),
            get(h.k_state.at[l], h.state, 4),
        ]
        act_loads = lambda j: [get(h.k_act.at[l, j], h.act.at[0], 5), get(h.s_act.at[l, j], h.act.at[1], 6)]
        slope_load = lambda j: get(h.k_slope.at[l, j], h.slope, 7)
        for cp in act_loads(0) + [slope_load(0)] + loads + xt_loads(l):
            cp.start()
        turn(l, X_DOWN)
        h.acc[...] = jnp.zeros_like(h.acc)
        for cp in xt_loads(l):
            cp.wait()

        def feed_back(j, carry):
            for cp in act_loads(j):
                cp.wait()
            produce(base + 2 * j, X_DOWN, h.act.at[0], h.act.at[1])

            @pl.when(j + 1 < s.NJ)
            def _():
                for cp in act_loads(j + 1):
                    cp.start()

            slope_load(j).wait()

            def body(k, weight):
                at = lanes(k, s.PC)
                h.ug[j, :, at] = (dot(h.gb[...], weight) * h.slope[:, at].astype(F32)).astype(BF)

            with_unit(h.w_down, l, j, unit + 4 + s.NJ + j, body)

            @pl.when(j + 1 < s.NJ)
            def _():
                slope_load(j + 1).start()

            g_send(l, h.ug, h.ug_sib, j, j).start()

            def body_up(k, weight):
                h.acc[...] += dot(h.ug[j, :, lanes(k, s.PC)], weight, NT)

            with_unit(h.w_up, l, j, unit + 4 + j, body_up)
            g_send(l, h.ug, h.ug_sib, j, j).wait_recv()
            produce(base + 2 * j + 1, X_LATE, h.ug.at[j], h.ug_sib.at[j])
            return carry

        lax.fori_loop(0, s.NJ, feed_back, 0)
        middle = get(h.k_middle.at[l], h.resid, 5)
        middle.start()
        for cp in xt_sends(l, X_DOWN):
            cp.wait_send()
        middle.wait()
        norm_back(l, 1)
        turn(l, X_MIX)
        stream = get(h.k_stream.at[l], h.resid, 5)
        stream.start()

        def body_mix(k, weight):
            h.rg[:, lanes(k, s.PC)] = dot(h.gb[...], weight).astype(BF)

        with_unit(h.w_mix, l, 0, unit + 3, body_mix)
        for cp in loads:
            cp.wait()
        round_one, round_two, round_three, arrive, settle = prefix_rounds(s, h, l, r, z)

        def local_state(k, carry):
            totals = []
            for i in range(s.NP):
                at = lanes(k * s.NP + i, 128)
                query, wide = h.qkv[0, :, at], h.rg[:, at].astype(F32)
                den = h.den[:, at]
                num = (wide / den).astype(BF)
                product = wide * h.mixed[0, :, at].astype(F32)
                high = product.astype(BF)
                low = (product - high.astype(F32)).astype(BF)
                slope = -(dot(high, ones) + dot(low, ones)) / den
                h.ng[:, at] = num
                h.dg[:, at] = slope
                h.msg[k, i * HD:(i + 1) * HD] = pack_state(dot(query, num, TN), first).astype(BF)
                totals.append(jnp.sum(query.astype(F32) * slope, axis=0, keepdims=True))
            h.msg[k, s.NP * HD:] = spread_rows(s, totals).astype(BF)
            return carry

        lax.fori_loop(0, s.Z, local_state, 0)
        round_one()
        produce(base + 2 * s.NJ, X_MIX, h.mixed.at[0], h.mixed.at[1])
        round_two()
        round_three()
        arrive()
        causal = (lax.broadcasted_iota(jnp.int32, (s.T, s.T), 1) <= lax.broadcasted_iota(jnp.int32, (s.T, s.T), 0))
        lane = lax.broadcasted_iota(jnp.int32, (1, 128), 1)

        def attend_back(p, carry):
            k, i = p // s.NP, p % s.NP
            at = lanes(p, 128)
            query, key, value, num = h.qkv[0, :, at], h.qkv[1, :, at], h.qkv[2, :, at], h.ng[:, at]
            slope = h.dg[:, at]
            high = slope.astype(BF)
            low = (slope - high.astype(F32)).astype(BF)
            zero = jnp.zeros_like(query)
            value_ones = jnp.concatenate([value, tall], axis=1)
            rows = pl.ds(pl.multiple_of(i * HD, HD), HD)
            state = unpack_state(h.state[k, rows, :], first)
            after = unpack_state(h.r3[k, rows, :], first)
            total = pick_row(h.state[k, s.NP * HD:, :], i)
            total_after = pick_row(h.r3[k, s.NP * HD:, :], i)
            value_grad = dot(key, after)
            query_grad = dot(num, state, NT) + slope * total
            key_grad = dot(value, after, NT) + total_after
            for head in range(2):
                mine = first if head == 0 else jnp.logical_not(first)
                query_mine = jnp.where(mine, query, zero)
                num_mine = jnp.where(mine, num, zero)
                key_mine = jnp.where(mine, key, zero)
                weights = jnp.where(causal, dot(query_mine, key, NT), 0.0).astype(BF)
                extra = jnp.where(lane == head * HD, high, jnp.where(lane == head * HD + 1, low, zero))
                score = dot(jnp.concatenate([num_mine, extra], axis=1), value_ones, NT)
                score = jnp.where(causal, score, 0.0).astype(BF)
                value_grad = value_grad + dot(weights, num_mine, TN)
                query_grad = query_grad + dot(score, key_mine)
                key_grad = key_grad + dot(score, query_mine, TN)
            h.pg[0, :, at] = (query_grad * jnp.minimum(query.astype(F32), 1.0)).astype(BF)
            h.pg[1, :, at] = (key_grad * jnp.minimum(key.astype(F32), 1.0)).astype(BF)
            h.pg[2, :, at] = value_grad.astype(BF)
            return carry

        lax.fori_loop(0, s.Z * s.NP, attend_back, 0)
        settle()
        for kind in range(3):
            g_send(l, h.pg, h.pg_sib, kind, s.NJ + kind).start()
        h.acc[...] = jnp.zeros_like(h.acc)

        def project_back(kind, carry):
            def body(k, weight):
                h.acc[...] += dot(h.pg[kind, :, lanes(k, s.PC)], weight, NT)

            with_unit(h.w_in, l, kind, unit + kind, body)
            g_send(l, h.pg, h.pg_sib, kind, s.NJ + kind).wait_recv()
            produce(base + 2 * s.NJ + 1 + kind, X_EARLY, h.pg.at[kind], h.pg_sib.at[kind])
            return carry

        lax.fori_loop(0, 3, project_back, 0)
        stream.wait()
        norm_back(l, 0)
        for cp in xt_sends(l, X_MIX):
            cp.wait_send()
        for j in range(s.NJ):
            g_send(l, h.ug, h.ug_sib, j, j).wait_send()
        for kind in range(3):
            g_send(l, h.pg, h.pg_sib, kind, s.NJ + kind).wait_send()
        return carry

    lax.fori_loop(0, s.L, one_layer, 0)

    source = h.vec[...]
    top = lax.broadcasted_iota(jnp.int32, (16, s.D), 0) == 4 * s.L + 1
    stages = (
        (h.v_z, s.Z, z, lambda d: (r, (z + d) % s.Z)),
        (h.v_c, 2, c, lambda d: sibling),
        (h.v_x, s.NX, x, lambda d: (row_at(s, y, (x + d) % s.NX, c), z)),
        (h.v_y, s.NY, y, lambda d: (row_at(s, (y + d) % s.NY, x, c), z)),
    )
    pending = []
    for i, (slots, count, me, peer) in enumerate(stages):
        slots[me] = source
        for d in range(1, count):
            at = slots.at[me]
            cp = remote(at, at, h.v_send.at[i, d], h.v_recv.at[i, count - d], peer(d))
            cp.start()
            pending.append(cp)
        for d in range(1, count):
            at = slots.at[(me + d) % count]
            remote(at, at, h.v_send.at[i, d], h.v_recv.at[i, d], (r, z)).wait_recv()
        total, largest = slots[0], slots[0]
        for k in range(1, count):
            total = total + slots[k]
            largest = jnp.maximum(largest, slots[k])
        source = jnp.where(top, largest, total)
    h.vector[...] = source
    for cp in pending:
        cp.wait_send()
    drain()
    settle_sums()


def unit_reader(s, h):
    def own(kind, l, j):
        if kind is h.w_in:
            src = h.w_in.at[l, j]
        elif kind is h.w_mix:
            src = h.w_mix.at[l]
        else:
            src = kind.at[l, :, :, :, :, lanes(j, s.PC)]
        return pltpu.make_async_copy(src, h.w.at[0], h.w_sem.at[0])

    def load(u, k):
        return pltpu.make_async_copy(h.whole.at[u, k - 1], h.w.at[k], h.w_sem.at[k])

    def with_unit(kind, l, j, u, body, advance=lambda: None):
        own(kind, l, j).start()
        advance()
        for k in range(1, s.Z):
            load(u, k).start()
        own(kind, l, j).wait()
        body(0, h.w[0].reshape(s.D, s.PC))

        @pl.loop(1, s.Z)
        def _(k):
            load(u, k).wait()
            body(k, h.w[k].reshape(s.D, s.PC))

    return with_unit


def backward_call(s, cotangent, kept, gain, coefs, weights):
    vmem = pl.BlockSpec(memory_space=pltpu.VMEM)
    smem = pl.BlockSpec(memory_space=pltpu.SMEM)
    hbm = pl.BlockSpec(memory_space=pl.ANY)
    shape = jax.ShapeDtypeStruct
    outs = [
        shape((s.T, s.D), F32),
        shape((16, s.D), F32),
        shape((s.L, 3, s.PR, s.PC), F32),
        shape((s.L, s.PR, s.PC), F32),
        shape((s.L, s.PR, s.NJ * s.PC), F32),
        shape((s.L, s.PR, s.NJ * s.PC), F32),
    ]
    saved = list(kept[2:])
    out = pl.pallas_call(
        functools.partial(bwd_kernel, s),
        out_shape=outs,
        in_specs=[vmem] * 3 + [smem] * 3 + [hbm] * (4 + len(saved)),
        out_specs=[vmem] * 2 + [hbm] * 4,
        scratch_shapes=list(bwd_scratch(s).values()),
        compiler_params=pltpu.CompilerParams(
            collective_id=1, has_side_effects=True, vmem_limit_bytes=60 * 1024 * 1024),
    )(cotangent, kept.logs, gain, *coefs, *weights, *saved)
    return BwdOut(*out)


def local(mesh, tokens, cotangent, image_length, image_start, norm_gain, norm_bias, weight_in, weight_mix, weight_up,
          weight_down):
    s = sizes_of(mesh, tokens, weight_in, weight_up)
    ahead, behind = coefficients(s, image_length, image_start)
    gain, bias = norm_gain.reshape(-1, s.D), norm_bias.reshape(-1, s.D)
    weights = split_rows(s, weight_in, weight_mix, weight_up, weight_down)
    kept = forward_call(s, tokens, gain, bias, ahead, weights)
    got = backward_call(s, cotangent, kept, gain, behind, weights)
    vector = got.vector
    grad_gain = vector[:2 * s.L].reshape(norm_gain.shape)
    grad_bias = vector[2 * s.L:4 * s.L].reshape(norm_bias.shape)
    heads = s.D // HD
    log_mean = jnp.sum(vector[4 * s.L, :128]) / (HD * s.R * s.Z * s.T * heads * s.L)
    log_max = jnp.max(vector[4 * s.L + 1, :128])
    return (
        kept.output,
        got.grad,
        grad_gain,
        grad_bias,
        grad_bias[s.L - 1, 1],
        jnp.transpose(got.g_in, (0, 2, 1, 3)),
        got.g_mix,
        got.g_up,
        got.g_down,
        log_max,
        log_mean,
    )


def solution(mesh):
    pixels = P(("rows", "feat"), None)
    placed = (pixels, pixels, P(), P(), P(), P(), P(None, None, None, "feat"), P(None, None, "feat"), P(None, None, "feat"),
              P(None, None, "feat"))
    return jax.shard_map(
        functools.partial(local, mesh),
        mesh=mesh,
        in_specs=placed,
        out_specs=(pixels, pixels, P(), P(), P(), P(None, "rows", None, "feat"), P(None, "rows", "feat"),
                   P(None, "rows", "feat"), P(None, "rows", "feat"), P(), P()),
        check_vma=False,
    )
```

time: 1550 us -> 516 us (0.33); the launches traced: 1530 us -> 514 us
  waiting for transfers between devices: 567 us -> 0 us
  Pallas kernels: 219 us -> 490 us
  matrix products: 233 us -> 0 us
  local copies, waits for them, and re-layouts: 197 us -> 16.5 us
  blocking collectives: 173 us -> 0 us
  other arithmetic: 106 us -> 4.94 us
  between operations: 19 us -> 2.53 us
    all_gather x8 -> x0, waiting for transfers between devices: 288 us -> none  [the longest x4 156 us: gather_rows(): return lax.all_gather(normed, 'feat', axis=0, tiled=True)]
    reduce_scatter x15 -> x0, waiting for transfers between devices: 278 us -> none  [the longest x3 151 us: sum_branch(): lax.psum_scatter(rows_times(left, weight).astype(jnp.bfloat16), 'feat', s...]
    pallas_call x1 -> x2, Pallas kernels: 219 us -> 490 us  [the longest x1 281 us: backward_call(): pl.pallas_call(functools.partial(bwd_kernel, s), out_shape=outs, in_specs...]
    dot_general x85 -> x0, matrix products: 233 us -> none  [the longest x2 29.3 us: local(): jnp.dot(normed_mid, weight_up[level], preferred_element_type=jnp.float32)]
    dynamic_update_slice x24 -> x0, local copies, waits for them, and re-layouts: 90.9 us -> none  [local(): lax.scan(block_forward, (state_in, total_in), pieces)]
    all_gather x8 -> x0, blocking collectives: 77.3 us -> none  [the longest x4 39 us: entering(): lax.all_gather(part.astype(kind), axis)]
    convert_element_type x35 -> x0, other arithmetic: 41.8 us -> none  [the longest x4 7.62 us: block_masks(): ((segment == segment[0]) & jnp.logical_not(opening[0])).astype(jnp.float32)]
    psum x1 -> x0, blocking collectives: 40.2 us -> none  [local(): lax.psum((jnp.stack(gain_parts), jnp.stack(bias_parts), log_total), ('row...]
  transfers between devices with their start and end apart: 23 -> 0, of which waited for: 14 -> 0; matrix products, arithmetic and copies ran while one was open for 14% -> 0% of each run, Pallas kernels for 14% -> 0%
where the time goes in v2:
time: 516 us; the launch traced here: 514 us
  Pallas kernels  490 us (95%)
  local copies, waits for them, and re-layouts  16.5 us (3%)
    pallas_call x1, Pallas kernels, backward_call(): pl.pallas_call(functools.partial(bwd_kernel, s), out_shape=outs, in_specs...  281 us
    pallas_call x1, Pallas kernels, forward_call(): pl.pallas_call(functools.partial(fwd_kernel, s), out_shape=list(outs), in...  209 us

profile of v2, /device:TPU:0, one launch (start us, length us, event | category | flops | bytes accessed | tf_op | source)
XLA Modules:
  0.0 514.3 jit_solution(9806110005977422338)
XLA Ops:
  0.6 0.7 broadcast_compare_fusion
  1.3 0.8 convert_reduce_fusion
  2.2 0.1 sub.7
  2.3 0.6 constant_dynamic-slice_fusion
  2.9 0.2 slice_reduce_fusion
  3.1 0.6 gather_fusion
  3.7 1.8 compare_convert_fusion
  5.5 0.1 and_convert_fusion
  5.6 0.6 reshape.182.refs_5_
  6.2 0.6 reshape.180.refs_5_
  6.8 0.1 fusion.1
  6.9 0.6 reshape.181.refs_4_
  7.5 0.6 reshape.179.refs_4_
  8.0 1.3 reshape.171.refs_1_.refs_2_
  9.4 1.3 reshape.172.refs_2_
  10.7 209.1 %shard_map.185 = (bf16[256,1024]{1,0:T(8,128)(2,1)}, f32[8,128]{1,0:T(8,128)}, bf16[24,3,2,2,2,128,256]{6,5,4,3,2,1,0:T(8,128)(2,1)}, f32[2,256,1024]{2,1,0:T(8,...) custom-call(bf16[256,1024]{1,0:T(8,128)(2,1)} %refs_0_.2, ...), custom_call_target="tpu_custom_call" | custom-call | tf_op jit(solution)/shard_map/pallas_call | solution.py:608
  219.8 0.0 copy-start.2
  219.8 281.3 %shard_map.186 = (f32[256,1024]{1,0:T(8,128)}, f32[16,1024]{1,0:T(8,128)}, f32[2,3,128,256]{3,2,1,0:T(8,128)}, f32[2,128,256]{2,1,0:T(8,128)}, f32[2,128,1024]{2,1,0:T(8,128)}, /*index=5*/f32[2,128,1024]{2,1,0:T(8,128)}) custom-call(bf16[256,1024]{1,0:T(8,128)(2,1)} %refs_0_.3, f32[8,128]{1,0:T(8,128)} %get-tuple-element.32.refs_1_, ...), custom_call_target="tpu_custom_call" | custom-call | tf_op jit(solution)/shard_map/pallas_call | solution.py:1196
  501.1 0.0 copy-start.3
  501.1 0.0 copy-start.1
  501.1 0.0 copy-start
  501.1 1.4 slice_reduce_fusion.2
  503.2 0.8 fusion.5
  504.1 0.0 copy-start.4
  504.1 0.6 slice.30
  504.7 0.6 reshape.177
  505.3 0.0 copy-done.2
  505.3 0.8 copy.27
  506.1 2.3 copy.28
  508.4 2.1 copy.29
  510.5 0.0 copy-done.3
  510.5 0.7 copy.30
  511.2 0.0 copy-done.1
  511.2 1.0 copy.31
  512.2 0.0 copy-done
  512.2 1.0 copy.32
  513.1 0.0 copy-done.4
  (8 shorter events, 0.1 us)
Async XLA Ops:
  219.8 285.5 %copy-start.2 = (bf16[256,1024]{1,0:T(8,128)(2,1)S(1)}, bf16[256,1024]{1,0:T(8,128)(2,1)}, u32[]{:S(2)}) copy-start(bf16[256,1024]{1,0:T(8,128)(2,1)} %get-tuple-element.78) | copy-start | bytes 1572868
  501.1 9.4 %copy-start.3 = (f32[2,128,256]{2,1,0:T(8,128)S(1)}, f32[2,128,256]{2,1,0:T(8,128)}, u32[]{:S(2)}) copy-start(f32[2,128,256]{2,1,0:T(8,128)} %get-tuple-element.84) | copy-start | bytes 786436
  501.1 10.1 %copy-start.1 = (f32[2,128,1024]{2,1,0:T(8,128)S(1)}, f32[2,128,1024]{2,1,0:T(8,128)}, u32[]{:S(2)}) copy-start(f32[2,128,1024]{2,1,0:T(8,128)} %get-tuple-element.85) | copy-start | bytes 3145732
  501.1 11.1 %copy-start = (f32[2,128,1024]{2,1,0:T(8,128)S(1)}, f32[2,128,1024]{2,1,0:T(8,128)}, u32[]{:S(2)}) copy-start(f32[2,128,1024]{2,1,0:T(8,128)} %get-tuple-element.86) | copy-start | bytes 3145732
  504.1 9.1 %copy-start.4 = (f32[2,2,1024]{2,1,0:T(2,128)}, f32[2,2,1024]{2,1,0:T(2,128)S(1)}, u32[]{:S(2)}) copy-start(f32[2,2,1024]{2,1,0:T(2,128)S(1)} %reshape.178) | copy-start | bytes 49156

commit v3 on v2

--- a/solution.py
+++ b/solution.py
@@ -15,7 +15,7 @@
 MESH = pl.DeviceIdType.MESH
 BF = jnp.bfloat16
 F32 = jnp.float32
-LAG_FIRST, LAG_SECOND, LAG_CORE, LAG_READY = 2, 4, 6, 7
+LAG_FIRST, LAG_SECOND, LAG_CORE, LAG_READY = 2, 3, 4, 5
 RING = 4
 ROOT_HALF = 0.7071067811865476
 ROOT_TAU = 0.3989422804014327
@@ -218,22 +218,23 @@
     return pl.ds(pl.multiple_of(at * width, width), width)
 
 
-def prefix_rounds(s, h, l, r, z):
+def prefix_rounds(s, h, l, r, z, way):
+    at = way * s.L + l
     msg, got, rows_got, back, out = h.msg, h.r1, h.r2, h.pre, h.r3
 
     def one(k):
-        return remote(msg.at[k], got.at[s.Z - k], h.r1_send.at[l, k], h.r1_recv.at[l, s.Z - k], (r, (z + k) % s.Z))
+        return remote(msg.at[k], got.at[s.Z - k], h.r1_send.at[at, k], h.r1_recv.at[at, s.Z - k], (r, (z + k) % s.Z))
 
     def two(d):
-        return remote(rows_got.at[r], rows_got.at[r], h.r2_send.at[l, d], h.r2_recv.at[l, s.R - d],
+        return remote(rows_got.at[r], rows_got.at[r], h.r2_send.at[at, d], h.r2_recv.at[at, s.R - d],
                       ((r + d) % s.R, z))
 
     def two_landing(d):
-        at = rows_got.at[(r + d) % s.R]
-        return remote(at, at, h.r2_send.at[l, d], h.r2_recv.at[l, d], (r, z))
+        spot = rows_got.at[(r + d) % s.R]
+        return remote(spot, spot, h.r2_send.at[at, d], h.r2_recv.at[at, d], (r, z))
 
     def three(k):
-        return remote(back.at[k], out.at[s.Z - k], h.r3_send.at[l, k], h.r3_recv.at[l, s.Z - k], (r, (z + k) % s.Z))
+        return remote(back.at[k], out.at[s.Z - k], h.r3_send.at[at, k], h.r3_recv.at[at, s.Z - k], (r, (z + k) % s.Z))
 
     def round_one():
         for k in range(1, s.Z):
@@ -241,10 +242,10 @@
 
     def round_two():
         for k in range(1, s.Z):
-            remote(msg.at[k], got.at[k], h.r1_send.at[l, k], h.r1_recv.at[l, k], (r, z)).wait_recv()
-        total = h.coef_a[0] * msg[0].astype(F32)
+            remote(msg.at[k], got.at[k], h.r1_send.at[at, k], h.r1_recv.at[at, k], (r, z)).wait_recv()
+        total = h.coef_a[way * s.Z] * msg[0].astype(F32)
         for k in range(1, s.Z):
-            total = total + h.coef_a[k] * got[k].astype(F32)
+            total = total + h.coef_a[way * s.Z + k] * got[k].astype(F32)
         rows_got[r] = total.astype(BF)
         for d in range(1, s.R):
             two(d).start()
@@ -253,11 +254,11 @@
         for d in range(1, s.R):
             two_landing(d).wait_recv()
         for k in range(s.Z):
-            total = h.coef_b[k * s.Z] * msg[0].astype(F32)
+            total = h.coef_b[(way * s.Z + k) * s.Z] * msg[0].astype(F32)
             for j in range(1, s.Z):
-                total = total + h.coef_b[k * s.Z + j] * got[j].astype(F32)
+                total = total + h.coef_b[(way * s.Z + k) * s.Z + j] * got[j].astype(F32)
             for q in range(s.R):
-                total = total + h.coef_c[k * s.R + q] * rows_got[q].astype(F32)
+                total = total + h.coef_c[(way * s.Z + k) * s.R + q] * rows_got[q].astype(F32)
             if k == 0:
                 out[0] = total.astype(BF)
             else:
@@ -266,7 +267,7 @@
 
     def arrive():
         for k in range(1, s.Z):
-            remote(back.at[k], out.at[k], h.r3_send.at[l, k], h.r3_recv.at[l, k], (r, z)).wait_recv()
+            remote(back.at[k], out.at[k], h.r3_send.at[at, k], h.r3_recv.at[at, k], (r, z)).wait_recv()
 
     def settle():
         for k in range(1, s.Z):
@@ -278,6 +279,46 @@
     return round_one, round_two, round_three, arrive, settle
 
 
+def weigh_kernel(s, length, begin, gain, bias, coef_a, coef_b, coef_c, gain_out, bias_out):
+    r, z = lax.axis_index("rows"), lax.axis_index("feat")
+    for l in range(s.L):
+        gain_out[2 * l:2 * l + 2] = gain[l]
+        bias_out[2 * l:2 * l + 2] = bias[l]
+    rows = range(s.R)
+    turn = [(z + k) % s.Z for k in range(s.Z)]
+    spots = [(r * s.Z + k) * s.T for k in turn] + [(r * s.Z + s.Z - 1) * s.T, r * s.Z * s.T]
+    spots += [(q * s.Z + s.Z - 1) * s.T for q in rows] + [q * s.Z * s.T for q in rows]
+
+    def count(n, begun):
+        start, live = begin[n], jnp.where(length[n] > 0, 1, 0)
+        return tuple(v + jnp.where(start <= at, live, 0) for v, at in zip(begun, spots))
+
+    found = lax.fori_loop(0, begin.shape[0], count, tuple(jnp.int32(0) for _ in spots))
+    mine, ends, row_ends = found[:s.Z], found[s.Z:s.Z + 2], (found[s.Z + 2:s.Z + 2 + s.R], found[s.Z + 2 + s.R:])
+    for way in range(2):
+        for k in range(s.Z):
+            coef_a[way * s.Z + k] = jnp.where(mine[k] == ends[way], 1.0, 0.0)
+            for j in range(s.Z):
+                order = turn[j] < turn[k] if way == 0 else turn[j] > turn[k]
+                coef_b[(way * s.Z + k) * s.Z + j] = jnp.where((mine[k] == mine[j]) & order, 1.0, 0.0)
+            for q in rows:
+                order = q < r if way == 0 else q > r
+                coef_c[(way * s.Z + k) * s.R + q] = jnp.where((mine[k] == row_ends[way][q]) & order, 1.0, 0.0)
+
+
+def weigh_units(s, image_length, image_start, gain, bias):
+    vmem = pl.BlockSpec(memory_space=pltpu.VMEM)
+    smem = pl.BlockSpec(memory_space=pltpu.SMEM)
+    shape = jax.ShapeDtypeStruct
+    return pl.pallas_call(
+        functools.partial(weigh_kernel, s),
+        out_shape=[shape((2 * s.Z,), F32), shape((2 * s.Z * s.Z,), F32), shape((2 * s.Z * s.R,), F32),
+                   shape((2 * s.L, s.D), F32), shape((2 * s.L, s.D), F32)],
+        in_specs=[smem] * 2 + [vmem] * 2,
+        out_specs=[smem] * 3 + [vmem] * 2,
+    )(image_length, image_start, gain, bias)
+
+
 def pack_state(full, first):
     return jnp.where(first, full[:HD], full[HD:])
 
@@ -300,8 +341,9 @@
     return jnp.sum(jnp.where(at == i, block.astype(F32), 0.0), axis=0, keepdims=True)
 
 
-class FwdIn(typing.NamedTuple):
+class Inputs(typing.NamedTuple):
     tokens: object
+    cotangent: object
     gain: object
     bias: object
     coef_a: object
@@ -311,9 +353,16 @@
     w_mix: object
     w_up: object
     w_down: object
-class FwdOut(typing.NamedTuple):
+
+
+class Outputs(typing.NamedTuple):
     output: object
-    logs: object
+    grad: object
+    vector: object
+    g_in: object
+    g_mix: object
+    g_up: object
+    g_down: object
     whole: object
     k_stream: object
     k_middle: object
@@ -328,9 +377,10 @@
     s_act: object
 
 
-def fwd_scratch(s):
+def forward_scratch(s):
     dma = pltpu.SemaphoreType.DMA
     return dict(
+        logs=pltpu.VMEM((8, 128), F32),
         piece=pltpu.VMEM((s.L, s.NU, s.PR, s.PC), BF),
         w=pltpu.VMEM((s.Z, s.NY, s.NX, 2, s.PR, s.PC), BF),
         stream=pltpu.VMEM((s.T, s.D), F32),
@@ -358,12 +408,12 @@
         y_recv=dma((s.U, 2, s.NY - 1)),
         c_send=dma((RING,)),
         c_recv=dma((s.U,)),
-        r1_send=dma((s.L, s.Z)),
-        r1_recv=dma((s.L, s.Z)),
-        r2_send=dma((s.L, s.R)),
-        r2_recv=dma((s.L, s.R)),
-        r3_send=dma((s.L, s.Z)),
-        r3_recv=dma((s.L, s.Z)),
+        r1_send=dma((2 * s.L, s.Z)),
+        r1_recv=dma((2 * s.L, s.Z)),
+        r2_send=dma((2 * s.L, s.R)),
+        r2_recv=dma((2 * s.L, s.R)),
+        r3_send=dma((2 * s.L, s.Z)),
+        r3_recv=dma((2 * s.L, s.Z)),
         keep=dma((8,)),
         keep_j=dma((2, s.NJ)),
         sib_send=dma((3 + s.NJ,)),
@@ -371,30 +421,10 @@
     )
 
 
-def fwd_kernel(s, *refs):
-    names = FwdIn._fields + FwdOut._fields + tuple(fwd_scratch(s))
-    h = types.SimpleNamespace(**dict(zip(names, refs, strict=True)))
-    r, z, y, x, c = place(s)
+def forward_part(s, h, spots, tick, with_unit, early):
+    r, z, y, x, c = spots
     sibling = (row_at(s, y, x, 1 - c), z)
-    greet(s, r, z)
-    tick, drain_all = weight_gather(s, h, r, z, y, x, c)
     first, _, _ = head_masks(s)
-
-    pieces = [
-        pltpu.make_async_copy(h.w_in.at[:, :, y, x, c], h.piece.at[:, 0:3], h.piece_sem.at[0]),
-        pltpu.make_async_copy(h.w_mix.at[:, y, x, c], h.piece.at[:, 3], h.piece_sem.at[1]),
-    ]
-    for j in range(s.NJ):
-        cols = pl.ds(j * s.PC, s.PC)
-        pieces.append(pltpu.make_async_copy(h.w_up.at[:, y, x, c, :, cols], h.piece.at[:, 4 + j], h.piece_sem.at[2 + j]))
-        pieces.append(pltpu.make_async_copy(h.w_down.at[:, y, x, c, :, cols], h.piece.at[:, 4 + s.NJ + j],
-                                            h.piece_sem.at[2 + s.NJ + j]))
-    for cp in pieces:
-        cp.start()
-    for cp in pieces:
-        cp.wait()
-
-    with_unit = unit_reader(s, h)
 
     def normalize(l, n, source):
         xhat, _ = norm_parts(source)
@@ -428,12 +458,16 @@
     def send_act(l, j):
         return remote(h.act.at[j], h.s_act.at[l, j], h.sib_send.at[3 + j], h.sib_recv.at[l, 3 + j], sibling)
 
-    h.stream[...] = h.tokens[...].astype(F32)
-    h.logs[...] = jnp.where(lax.broadcasted_iota(jnp.int32, (8, 128), 0) == 1, -jnp.inf, 0.0)
     ones = pair_ones()
     tall = jnp.ones((s.T, 128), BF)
-
-    @pl.loop(0, LAG_READY)
+    h.logs[...] = jnp.where(lax.broadcasted_iota(jnp.int32, (8, 128), 0) == 1, -jnp.inf, 0.0)
+    tick(0)
+    tick(1)
+    early()
+    tick(2)
+    h.stream[...] = h.tokens[...].astype(F32)
+
+    @pl.loop(3, LAG_READY)
     def _(t):
         tick(t)
 
@@ -455,7 +489,7 @@
 
         lax.fori_loop(0, 3, project, 0)
         keep_one(l, 3).start()
-        round_one, round_two, round_three, arrive, settle = prefix_rounds(s, h, l, r, z)
+        round_one, round_two, round_three, arrive, settle = prefix_rounds(s, h, l, r, z, 0)
 
         def local_state(k, carry):
             totals = []
@@ -542,20 +576,22 @@
             return carry
 
         lax.fori_loop(0, s.NJ, up, 0)
-        h.acc[...] = jnp.zeros_like(h.acc)
+        keep_one(l, 2).wait()
+        h.stream[...] = h.middle[...]
 
         def down(j, carry):
             u = base + 4 + s.NJ + j
 
             def body(k, weight):
-                h.acc[...] += dot(h.act[j, :, lanes(k, s.PC)], weight, NT)
+                h.stream[...] += dot(h.act[j, :, lanes(k, s.PC)], weight, NT)
 
             with_unit(h.w_down, l, j, u, body, lambda: tick(u + LAG_READY))
             return carry
 
-        lax.fori_loop(0, s.NJ, down, 0)
-        keep_one(l, 2).wait()
-        h.stream[...] = h.middle[...] + h.acc[...]
+        @pl.when(l + 1 < s.L)
+        def _():
+            lax.fori_loop(0, s.NJ, down, 0)
+
         for n in range(2):
             keep_norm(l, n).wait()
             send_norm(l, n).wait_send()
@@ -574,8 +610,6 @@
         return carry
 
     lax.fori_loop(0, s.L, one_layer, 0)
-    h.output[...] = h.stream[...].astype(BF)
-    drain_all()
 
 
 def split_rows(s, weight_in, *rest):
@@ -584,108 +618,15 @@
     return (turned,) + tuple(w.reshape((s.L,) + cut + w.shape[2:]) for w in rest)
 
 
-def forward_call(s, tokens, gain, bias, coefs, weights):
-    vmem = pl.BlockSpec(memory_space=pltpu.VMEM)
-    smem = pl.BlockSpec(memory_space=pltpu.SMEM)
-    hbm = pl.BlockSpec(memory_space=pl.ANY)
-    shape = jax.ShapeDtypeStruct
-    outs = FwdOut(
-        output=shape((s.T, s.D), BF),
-        logs=shape((8, 128), F32),
-        whole=shape((s.U, s.Z - 1, s.NY, s.NX, 2, s.PR, s.PC), BF),
-        k_stream=shape((s.L, s.T, s.D), F32),
-        k_middle=shape((s.L, s.T, s.D), F32),
-        k_qkv=shape((s.L, 3, s.T, s.D), BF),
-        k_mixed=shape((s.L, s.T, s.D), BF),
-        k_den=shape((s.L, s.T, s.D), F32),
-        k_state=shape((s.L, s.Z, s.MR, 128), BF),
-        k_act=shape((s.L, s.NJ, s.T, s.D), BF),
-        k_slope=shape((s.L, s.NJ, s.T, s.D), BF),
-        k_normt=shape((s.L, 2, 2, s.NY, s.NX, s.PR, s.T), BF),
-        s_mixed=shape((s.L, s.T, s.D), BF),
-        s_act=shape((s.L, s.NJ, s.T, s.D), BF),
-    )
-    out = pl.pallas_call(
-        functools.partial(fwd_kernel, s),
-        out_shape=list(outs),
-        in_specs=[vmem] * 3 + [smem] * 3 + [hbm] * 4,
-        out_specs=[vmem] * 2 + [hbm] * (len(outs) - 2),
-        scratch_shapes=list(fwd_scratch(s).values()),
-        compiler_params=pltpu.CompilerParams(
-            collective_id=0, has_side_effects=True, vmem_limit_bytes=56 * 1024 * 1024),
-    )(tokens, gain, bias, *coefs, *weights)
-    return FwdOut(*out)
-
-
-def segments_of_units(s, image_length, image_start):
-    first = jnp.arange(s.R * s.Z, dtype=jnp.int32) * s.T
-    live = (image_length > 0)[None, :]
-    return (jnp.sum(((image_start[None, :] <= first[:, None]) & live).astype(jnp.int32), axis=1) - 1).reshape(s.R, s.Z)
-
-
-def coefficients(s, image_length, image_start):
-    seg = segments_of_units(s, image_length, image_start)
-    r, z = lax.axis_index("rows"), lax.axis_index("feat")
-    turn = (z + jnp.arange(s.Z)) % s.Z
-    row = seg[r][turn]
-    order = jnp.arange(s.R)
-    f = lambda v: v.astype(F32).reshape(-1)
-    same = row[:, None] == row[None, :]
-    forward = (
-        f(row == seg[r, s.Z - 1]),
-        f(same & (turn[None, :] < turn[:, None])),
-        f((seg[None, :, s.Z - 1] == row[:, None]) & (order[None, :] < r)),
-    )
-    backward = (
-        f(row == seg[r, 0]),
-        f(same & (turn[None, :] > turn[:, None])),
-        f((seg[None, :, 0] == row[:, None]) & (order[None, :] > r)),
-    )
-    return forward, backward
-
-
-BACK_FIRST, BACK_SECOND, BACK_LAST = 2, 4, 6
+BACK_FIRST, BACK_SECOND, BACK_LAST = 1, 2, 4
 SLOTS = 8
 OUT_RING = 4
 X_EARLY, X_LATE, X_DOWN, X_MIX = 0, 1, 2, 3
 
-class BwdIn(typing.NamedTuple):
-    cotangent: object
-    logs: object
-    gain: object
-    coef_a: object
-    coef_b: object
-    coef_c: object
-    w_in: object
-    w_mix: object
-    w_up: object
-    w_down: object
-    whole: object
-    k_stream: object
-    k_middle: object
-    k_qkv: object
-    k_mixed: object
-    k_den: object
-    k_state: object
-    k_act: object
-    k_slope: object
-    k_normt: object
-    s_mixed: object
-    s_act: object
-class BwdOut(typing.NamedTuple):
-    grad: object
-    vector: object
-    g_in: object
-    g_mix: object
-    g_up: object
-    g_down: object
-
-
-def bwd_scratch(s):
+def backward_scratch(s):
     dma = pltpu.SemaphoreType.DMA
     half = s.PR // 2
     return dict(
-        w=pltpu.VMEM((s.Z, s.NY, s.NX, 2, s.PR, s.PC), BF),
         part=pltpu.VMEM((SLOTS, s.NY, s.NX, s.Z, s.PR, s.PC), BF),
         land_x1=pltpu.VMEM((SLOTS, s.NX - 1, s.NY, s.Z, half, s.PC), BF),
         land_y1=pltpu.VMEM((SLOTS, s.NY - 1, s.NX, s.Z, half, s.PC), BF),
@@ -693,35 +634,26 @@
         land_y2=pltpu.VMEM((SLOTS, s.NY - 1, s.Z, half, s.PC), BF),
         land_z=pltpu.VMEM((SLOTS, s.Z - 1, s.PR, s.PC), BF),
         final=pltpu.VMEM((OUT_RING, s.PR, s.PC), F32),
-        acc=pltpu.VMEM((s.T, s.D), F32),
         resid=pltpu.VMEM((s.T, s.D), F32),
         gb=pltpu.VMEM((s.T, s.D), BF),
         turned=pltpu.VMEM((s.NY, s.NX, 2, s.PR, s.T), BF),
         xt=pltpu.VMEM((4, 2, s.NY, s.NX, s.PR, s.T), BF),
-        act=pltpu.VMEM((2, s.T, s.D), BF),
-        slope=pltpu.VMEM((s.T, s.D), BF),
+        b_act=pltpu.VMEM((2, s.T, s.D), BF),
+        b_slope=pltpu.VMEM((s.T, s.D), BF),
         ug=pltpu.VMEM((s.NJ, s.T, s.D), BF),
         ug_sib=pltpu.VMEM((s.NJ, s.T, s.D), BF),
         pg=pltpu.VMEM((3, s.T, s.D), BF),
         pg_sib=pltpu.VMEM((3, s.T, s.D), BF),
-        qkv=pltpu.VMEM((3, s.T, s.D), BF),
-        mixed=pltpu.VMEM((2, s.T, s.D), BF),
-        den=pltpu.VMEM((s.T, s.D), F32),
+        b_mixed=pltpu.VMEM((2, s.T, s.D), BF),
         rg=pltpu.VMEM((s.T, s.D), BF),
         ng=pltpu.VMEM((s.T, s.D), BF),
         dg=pltpu.VMEM((s.T, s.D), F32),
         state=pltpu.VMEM((s.Z, s.MR, 128), BF),
-        msg=pltpu.VMEM((s.Z, s.MR, 128), BF),
-        r1=pltpu.VMEM((s.Z, s.MR, 128), BF),
-        r2=pltpu.VMEM((s.R, s.MR, 128), BF),
-        pre=pltpu.VMEM((s.Z, s.MR, 128), BF),
-        r3=pltpu.VMEM((s.Z, s.MR, 128), BF),
         vec=pltpu.VMEM((16, s.D), F32),
         v_z=pltpu.VMEM((s.Z, 16, s.D), F32),
         v_c=pltpu.VMEM((2, 16, s.D), F32),
         v_x=pltpu.VMEM((s.NX, 16, s.D), F32),
         v_y=pltpu.VMEM((s.NY, 16, s.D), F32),
-        w_sem=dma((s.Z,)),
         x1_send=dma((SLOTS, s.NX - 1)),
         x1_recv=dma((SLOTS, s.NX - 1)),
         y1_send=dma((SLOTS, s.NY - 1)),
@@ -730,8 +662,8 @@
         x2_recv=dma((SLOTS, s.NX - 1)),
         y2_send=dma((SLOTS, s.NY - 1)),
         y2_recv=dma((SLOTS, s.NY - 1)),
-        z_send=dma((SLOTS, s.Z - 1)),
-        z_recv=dma((SLOTS, s.Z - 1)),
+        bz_send=dma((SLOTS, s.Z - 1)),
+        bz_recv=dma((SLOTS, s.Z - 1)),
         out_sem=dma((OUT_RING,)),
         xt_sem=dma((2, 2, s.NQ)),
         xt_send=dma((2, s.NQ)),
@@ -739,12 +671,6 @@
         g_send=dma((s.NJ + 3,)),
         g_recv=dma((s.L, s.NJ + 3)),
         get=dma((8,)),
-        r1_send=dma((s.L, s.Z)),
-        r1_recv=dma((s.L, s.Z)),
-        r2_send=dma((s.L, s.R)),
-        r2_recv=dma((s.L, s.R)),
-        r3_send=dma((s.L, s.Z)),
-        r3_recv=dma((s.L, s.Z)),
         v_send=dma((4, max(s.Z, s.NX, s.NY))),
         v_recv=dma((4, max(s.Z, s.NX, s.NY))),
     )
@@ -784,8 +710,8 @@
     def last(v):
         b = v % SLOTS
         return [
-            remote(part.at[b, 0, 0, d], h.land_z.at[b, s.Z - d - 1], h.z_send.at[b, d - 1],
-                   h.z_recv.at[b, s.Z - d - 1], (r, (z + d) % s.Z)) for d in range(1, s.Z)
+            remote(part.at[b, 0, 0, d], h.land_z.at[b, s.Z - d - 1], h.bz_send.at[b, d - 1],
+                   h.bz_recv.at[b, s.Z - d - 1], (r, (z + d) % s.Z)) for d in range(1, s.Z)
         ]
 
     def stage_second(v):
@@ -848,8 +774,8 @@
         h.final[o] = total
         l, q = s.L - 1 - v // s.NU, v % s.NU
         wide = 2 * s.NJ
-        pl.when((q < wide) & (q % 2 == 0))(lambda: out_copy(h.g_down.at[l, :, lanes(q // 2, s.PC)], o).start())
-        pl.when((q < wide) & (q % 2 == 1))(lambda: out_copy(h.g_up.at[l, :, lanes(q // 2, s.PC)], o).start())
+        pl.when(q < s.NJ)(lambda: out_copy(h.g_down.at[l, :, lanes(q, s.PC)], o).start())
+        pl.when((q >= s.NJ) & (q < wide))(lambda: out_copy(h.g_up.at[l, :, lanes(q - s.NJ, s.PC)], o).start())
         pl.when(q == wide)(lambda: out_copy(h.g_mix.at[l], o).start())
         pl.when(q > wide)(lambda: out_copy(h.g_in.at[l, q - wide - 1], o).start())
 
@@ -885,7 +811,7 @@
         tick(v)
 
     def drain():
-        @pl.loop(s.U, s.U + BACK_LAST)
+        @pl.loop(s.U + 4, s.U + max(BACK_LAST + 1, 4))
         def _(t):
             tick(t)
 
@@ -897,20 +823,16 @@
         for o in range(OUT_RING):
             out_copy(h.g_mix.at[0], o).wait()
 
-    return produce, drain, settle
-
-
-def bwd_kernel(s, *refs):
-    names = BwdIn._fields + BwdOut._fields + tuple(bwd_scratch(s))
-    h = types.SimpleNamespace(**dict(zip(names, refs, strict=True)))
-    r, z, y, x, c = place(s)
+    return produce, tick, drain, settle
+
+
+def backward_part(s, h, spots, tick_weights, with_unit, sums):
+    r, z, y, x, c = spots
+    produce, tick, drain, settle_sums = sums
     sibling = (row_at(s, y, x, 1 - c), z)
-    greet(s, r, z)
-    produce, drain, settle_sums = gradient_sums(s, h, r, z, y, x, c)
     first, _, _ = head_masks(s)
     ones = pair_ones()
     tall = jnp.ones((s.T, 128), BF)
-    with_unit = unit_reader(s, h)
     squares = [(dy, dx) for dy in range(s.NY) for dx in range(s.NX)]
 
     def get(src, dst, index):
@@ -938,9 +860,6 @@
             cp.start()
         for dy, dx in squares:
             h.xt[which, 0, dy, dx] = h.turned[(y + dy) % s.NY, (x + dx) % s.NX, c]
-        for cp in xt_sends(l, which):
-            cp.wait_recv()
-
     def g_send(l, src, dst, j, index):
         return remote(src.at[j], dst.at[j], h.g_send.at[index], h.g_recv.at[l, index], sibling)
 
@@ -950,14 +869,14 @@
         at = l * 2 + n
         h.vec[pl.ds(at, 1)] = jnp.sum(back * xhat, axis=0, keepdims=True)
         h.vec[pl.ds(2 * s.L + at, 1)] = jnp.sum(back, axis=0, keepdims=True)
-        scaled = back * h.gain[pl.ds(at, 1), :]
+        scaled = back * h.gain[pl.ds(l * 2 + n, 1), :]
         mean = jnp.mean(scaled, axis=-1, keepdims=True)
         along = jnp.mean(scaled * xhat, axis=-1, keepdims=True)
         h.grad[...] += inv * (scaled - mean - xhat * along)
 
-    h.grad[...] = h.cotangent[...].astype(F32)
-    h.vec[...] = jnp.zeros_like(h.vec)
-    h.vec[4 * s.L:4 * s.L + 2, :128] = h.logs[0:2]
+    def early():
+        h.grad[...] = h.cotangent[...].astype(F32)
+        turn(s.L - 1, X_DOWN)
 
     def one_layer(li, carry):
         l = s.L - 1 - li
@@ -965,37 +884,43 @@
         unit = l * s.NU
         loads = [
             get(h.k_qkv.at[l], h.qkv, 0),
-            get(h.k_mixed.at[l], h.mixed.at[0], 1),
-            get(h.s_mixed.at[l], h.mixed.at[1], 2),
+            get(h.k_mixed.at[l], h.b_mixed.at[0], 1),
+            get(h.s_mixed.at[l], h.b_mixed.at[1], 2),
             get(h.k_den.at[l], h.den, 3),
             get(h.k_state.at[l], h.state, 4),
         ]
-        act_loads = lambda j: [get(h.k_act.at[l, j], h.act.at[0], 5), get(h.s_act.at[l, j], h.act.at[1], 6)]
-        slope_load = lambda j: get(h.k_slope.at[l, j], h.slope, 7)
+        act_loads = lambda j: [get(h.k_act.at[l, j], h.b_act.at[0], 5), get(h.s_act.at[l, j], h.b_act.at[1], 6)]
+        slope_load = lambda j: get(h.k_slope.at[l, j], h.b_slope, 7)
         for cp in act_loads(0) + [slope_load(0)] + loads + xt_loads(l):
             cp.start()
-        turn(l, X_DOWN)
         h.acc[...] = jnp.zeros_like(h.acc)
         for cp in xt_loads(l):
             cp.wait()
+        for cp in xt_sends(l, X_DOWN):
+            cp.wait_recv()
 
         def feed_back(j, carry):
             for cp in act_loads(j):
                 cp.wait()
-            produce(base + 2 * j, X_DOWN, h.act.at[0], h.act.at[1])
+            produce(base + j, X_DOWN, h.b_act.at[0], h.b_act.at[1])
+            slope_load(j).wait()
+
+            def body(k, weight):
+                at = lanes(k, s.PC)
+                h.ug[j, :, at] = (dot(h.gb[...], weight) * h.b_slope[:, at].astype(F32)).astype(BF)
+
+                @pl.when(li == 0)
+                def _():
+                    h.stream[...] += dot(h.b_act[0, :, at], weight, NT)
+
+            u = unit + 4 + s.NJ + j
+            with_unit(h.w_down, l, j, u, body, lambda: pl.when(li == 0)(lambda: tick_weights(u + LAG_READY)))
 
             @pl.when(j + 1 < s.NJ)
             def _():
                 for cp in act_loads(j + 1):
                     cp.start()
 
-            slope_load(j).wait()
-
-            def body(k, weight):
-                at = lanes(k, s.PC)
-                h.ug[j, :, at] = (dot(h.gb[...], weight) * h.slope[:, at].astype(F32)).astype(BF)
-
-            with_unit(h.w_down, l, j, unit + 4 + s.NJ + j, body)
 
             @pl.when(j + 1 < s.NJ)
             def _():
@@ -1007,11 +932,14 @@
                 h.acc[...] += dot(h.ug[j, :, lanes(k, s.PC)], weight, NT)
 
             with_unit(h.w_up, l, j, unit + 4 + j, body_up)
+            return carry
+
+        def produce_up(j):
             g_send(l, h.ug, h.ug_sib, j, j).wait_recv()
-            produce(base + 2 * j + 1, X_LATE, h.ug.at[j], h.ug_sib.at[j])
-            return carry
+            produce(base + s.NJ + j, X_LATE, h.ug.at[j], h.ug_sib.at[j])
 
         lax.fori_loop(0, s.NJ, feed_back, 0)
+        produce_up(0)
         middle = get(h.k_middle.at[l], h.resid, 5)
         middle.start()
         for cp in xt_sends(l, X_DOWN):
@@ -1019,6 +947,8 @@
         middle.wait()
         norm_back(l, 1)
         turn(l, X_MIX)
+        for cp in xt_sends(l, X_MIX):
+            cp.wait_recv()
         stream = get(h.k_stream.at[l], h.resid, 5)
         stream.start()
 
@@ -1028,7 +958,7 @@
         with_unit(h.w_mix, l, 0, unit + 3, body_mix)
         for cp in loads:
             cp.wait()
-        round_one, round_two, round_three, arrive, settle = prefix_rounds(s, h, l, r, z)
+        round_one, round_two, round_three, arrive, settle = prefix_rounds(s, h, l, r, z, 1)
 
         def local_state(k, carry):
             totals = []
@@ -1037,7 +967,7 @@
                 query, wide = h.qkv[0, :, at], h.rg[:, at].astype(F32)
                 den = h.den[:, at]
                 num = (wide / den).astype(BF)
-                product = wide * h.mixed[0, :, at].astype(F32)
+                product = wide * h.b_mixed[0, :, at].astype(F32)
                 high = product.astype(BF)
                 low = (product - high.astype(F32)).astype(BF)
                 slope = -(dot(high, ones) + dot(low, ones)) / den
@@ -1050,9 +980,11 @@
 
         lax.fori_loop(0, s.Z, local_state, 0)
         round_one()
-        produce(base + 2 * s.NJ, X_MIX, h.mixed.at[0], h.mixed.at[1])
+        produce_up(1)
         round_two()
+        produce_up(2)
         round_three()
+        lax.fori_loop(3, s.NJ, lambda j, carry: (produce_up(j), carry)[1], 0)
         arrive()
         causal = (lax.broadcasted_iota(jnp.int32, (s.T, s.T), 1) <= lax.broadcasted_iota(jnp.int32, (s.T, s.T), 0))
         lane = lax.broadcasted_iota(jnp.int32, (1, 128), 1)
@@ -1091,7 +1023,10 @@
             h.pg[2, :, at] = value_grad.astype(BF)
             return carry
 
-        lax.fori_loop(0, s.Z * s.NP, attend_back, 0)
+        half = s.Z * s.NP // 2
+        lax.fori_loop(0, half, attend_back, 0)
+        produce(base + 2 * s.NJ, X_MIX, h.b_mixed.at[0], h.b_mixed.at[1])
+        lax.fori_loop(half, s.Z * s.NP, attend_back, 0)
         settle()
         for kind in range(3):
             g_send(l, h.pg, h.pg_sib, kind, s.NJ + kind).start()
@@ -1115,39 +1050,51 @@
             g_send(l, h.ug, h.ug_sib, j, j).wait_send()
         for kind in range(3):
             g_send(l, h.pg, h.pg_sib, kind, s.NJ + kind).wait_send()
+
+        @pl.when(li + 1 < s.L)
+        def _():
+            turn(l - 1, X_DOWN)
+
         return carry
 
-    lax.fori_loop(0, s.L, one_layer, 0)
-
-    source = h.vec[...]
-    top = lax.broadcasted_iota(jnp.int32, (16, s.D), 0) == 4 * s.L + 1
-    stages = (
-        (h.v_z, s.Z, z, lambda d: (r, (z + d) % s.Z)),
-        (h.v_c, 2, c, lambda d: sibling),
-        (h.v_x, s.NX, x, lambda d: (row_at(s, y, (x + d) % s.NX, c), z)),
-        (h.v_y, s.NY, y, lambda d: (row_at(s, (y + d) % s.NY, x, c), z)),
-    )
-    pending = []
-    for i, (slots, count, me, peer) in enumerate(stages):
-        slots[me] = source
-        for d in range(1, count):
-            at = slots.at[me]
-            cp = remote(at, at, h.v_send.at[i, d], h.v_recv.at[i, count - d], peer(d))
-            cp.start()
-            pending.append(cp)
-        for d in range(1, count):
-            at = slots.at[(me + d) % count]
-            remote(at, at, h.v_send.at[i, d], h.v_recv.at[i, d], (r, z)).wait_recv()
-        total, largest = slots[0], slots[0]
-        for k in range(1, count):
-            total = total + slots[k]
-            largest = jnp.maximum(largest, slots[k])
-        source = jnp.where(top, largest, total)
-    h.vector[...] = source
-    for cp in pending:
-        cp.wait_send()
-    drain()
-    settle_sums()
+    def run():
+        lax.fori_loop(0, s.L, one_layer, 0)
+        finish()
+
+    def finish():
+        h.vec[4 * s.L:4 * s.L + 2, :128] = h.logs[0:2]
+        source = h.vec[...]
+        top = lax.broadcasted_iota(jnp.int32, (16, s.D), 0) == 4 * s.L + 1
+        stages = (
+            (h.v_z, s.Z, z, lambda d: (r, (z + d) % s.Z)),
+            (h.v_c, 2, c, lambda d: sibling),
+            (h.v_x, s.NX, x, lambda d: (row_at(s, y, (x + d) % s.NX, c), z)),
+            (h.v_y, s.NY, y, lambda d: (row_at(s, (y + d) % s.NY, x, c), z)),
+        )
+        pending = []
+        for i, (slots, count, me, peer) in enumerate(stages):
+            slots[me] = source
+            for d in range(1, count):
+                at = slots.at[me]
+                cp = remote(at, at, h.v_send.at[i, d], h.v_recv.at[i, count - d], peer(d))
+                cp.start()
+                pending.append(cp)
+            tick(s.U + i)
+            for d in range(1, count):
+                at = slots.at[(me + d) % count]
+                remote(at, at, h.v_send.at[i, d], h.v_recv.at[i, d], (r, z)).wait_recv()
+            total, largest = slots[0], slots[0]
+            for k in range(1, count):
+                total = total + slots[k]
+                largest = jnp.maximum(largest, slots[k])
+            source = jnp.where(top, largest, total)
+        h.vector[...] = source
+        for cp in pending:
+            cp.wait_send()
+        drain()
+        settle_sums()
+
+    return early, run
 
 
 def unit_reader(s, h):
@@ -1179,40 +1126,85 @@
     return with_unit
 
 
-def backward_call(s, cotangent, kept, gain, coefs, weights):
+def kernel(s, *refs):
+    scratch = forward_scratch(s) | backward_scratch(s)
+    names = Inputs._fields + Outputs._fields + tuple(scratch)
+    h = types.SimpleNamespace(**dict(zip(names, refs, strict=True)))
+    spots = r, z, y, x, c = place(s)
+    pieces = [
+        pltpu.make_async_copy(h.w_in.at[:, :, y, x, c], h.piece.at[:, 0:3], h.piece_sem.at[0]),
+        pltpu.make_async_copy(h.w_mix.at[:, y, x, c], h.piece.at[:, 3], h.piece_sem.at[1]),
+    ]
+    for j in range(s.NJ):
+        cols = pl.ds(j * s.PC, s.PC)
+        pieces.append(pltpu.make_async_copy(h.w_up.at[:, y, x, c, :, cols], h.piece.at[:, 4 + j], h.piece_sem.at[2 + j]))
+        pieces.append(pltpu.make_async_copy(h.w_down.at[:, y, x, c, :, cols], h.piece.at[:, 4 + s.NJ + j],
+                                            h.piece_sem.at[2 + s.NJ + j]))
+    for cp in pieces:
+        cp.start()
+    greet(s, r, z)
+    for cp in pieces:
+        cp.wait()
+    tick_weights, drain_weights = weight_gather(s, h, r, z, y, x, c)
+    with_unit = unit_reader(s, h)
+    sums = gradient_sums(s, h, r, z, y, x, c)
+    early, backward = backward_part(s, h, spots, tick_weights, with_unit, sums)
+
+    def before():
+        h.vec[...] = jnp.zeros_like(h.vec)
+        early()
+
+    forward_part(s, h, spots, tick_weights, with_unit, before)
+    backward()
+    h.output[...] = h.stream[...].astype(BF)
+    drain_weights()
+
+
+def call(s, arrays):
     vmem = pl.BlockSpec(memory_space=pltpu.VMEM)
     smem = pl.BlockSpec(memory_space=pltpu.SMEM)
     hbm = pl.BlockSpec(memory_space=pl.ANY)
     shape = jax.ShapeDtypeStruct
-    outs = [
-        shape((s.T, s.D), F32),
-        shape((16, s.D), F32),
-        shape((s.L, 3, s.PR, s.PC), F32),
-        shape((s.L, s.PR, s.PC), F32),
-        shape((s.L, s.PR, s.NJ * s.PC), F32),
-        shape((s.L, s.PR, s.NJ * s.PC), F32),
-    ]
-    saved = list(kept[2:])
+    outs = Outputs(
+        output=shape((s.T, s.D), BF),
+        grad=shape((s.T, s.D), F32),
+        vector=shape((16, s.D), F32),
+        g_in=shape((s.L, 3, s.PR, s.PC), F32),
+        g_mix=shape((s.L, s.PR, s.PC), F32),
+        g_up=shape((s.L, s.PR, s.NJ * s.PC), F32),
+        g_down=shape((s.L, s.PR, s.NJ * s.PC), F32),
+        whole=shape((s.U, s.Z - 1, s.NY, s.NX, 2, s.PR, s.PC), BF),
+        k_stream=shape((s.L, s.T, s.D), F32),
+        k_middle=shape((s.L, s.T, s.D), F32),
+        k_qkv=shape((s.L, 3, s.T, s.D), BF),
+        k_mixed=shape((s.L, s.T, s.D), BF),
+        k_den=shape((s.L, s.T, s.D), F32),
+        k_state=shape((s.L, s.Z, s.MR, 128), BF),
+        k_act=shape((s.L, s.NJ, s.T, s.D), BF),
+        k_slope=shape((s.L, s.NJ, s.T, s.D), BF),
+        k_normt=shape((s.L, 2, 2, s.NY, s.NX, s.PR, s.T), BF),
+        s_mixed=shape((s.L, s.T, s.D), BF),
+        s_act=shape((s.L, s.NJ, s.T, s.D), BF),
+    )
+    scratch = forward_scratch(s) | backward_scratch(s)
     out = pl.pallas_call(
-        functools.partial(bwd_kernel, s),
-        out_shape=outs,
-        in_specs=[vmem] * 3 + [smem] * 3 + [hbm] * (4 + len(saved)),
-        out_specs=[vmem] * 2 + [hbm] * 4,
-        scratch_shapes=list(bwd_scratch(s).values()),
+        functools.partial(kernel, s),
+        out_shape=list(outs),
+        in_specs=[vmem] * 4 + [smem] * 3 + [hbm] * 4,
+        out_specs=[vmem] * 3 + [hbm] * (len(outs) - 3),
+        scratch_shapes=list(scratch.values()),
         compiler_params=pltpu.CompilerParams(
-            collective_id=1, has_side_effects=True, vmem_limit_bytes=60 * 1024 * 1024),
-    )(cotangent, kept.logs, gain, *coefs, *weights, *saved)
-    return BwdOut(*out)
+            collective_id=0, has_side_effects=True, vmem_limit_bytes=61 * 1024 * 1024),
+    )(*arrays)
+    return Outputs(*out)
 
 
 def local(mesh, tokens, cotangent, image_length, image_start, norm_gain, norm_bias, weight_in, weight_mix, weight_up,
           weight_down):
     s = sizes_of(mesh, tokens, weight_in, weight_up)
-    ahead, behind = coefficients(s, image_length, image_start)
-    gain, bias = norm_gain.reshape(-1, s.D), norm_bias.reshape(-1, s.D)
     weights = split_rows(s, weight_in, weight_mix, weight_up, weight_down)
-    kept = forward_call(s, tokens, gain, bias, ahead, weights)
-    got = backward_call(s, cotangent, kept, gain, behind, weights)
+    *coefs, gain, bias = weigh_units(s, image_length, image_start, norm_gain, norm_bias)
+    got = call(s, Inputs(tokens, cotangent, gain, bias, *coefs, *weights))
     vector = got.vector
     grad_gain = vector[:2 * s.L].reshape(norm_gain.shape)
     grad_bias = vector[2 * s.L:4 * s.L].reshape(norm_bias.shape)
@@ -1220,7 +1212,7 @@
     log_mean = jnp.sum(vector[4 * s.L, :128]) / (HD * s.R * s.Z * s.T * heads * s.L)
     log_max = jnp.max(vector[4 * s.L + 1, :128])
     return (
-        kept.output,
+        got.output,
         got.grad,
         grad_gain,
         grad_bias,

time: 516 us -> 458 us (0.89)
  Pallas kernels: 490 us -> 442 us
  local copies, waits for them, and re-layouts: 16.5 us -> 11 us
    pallas_call x2, Pallas kernels: 490 us -> 442 us  [the longest x1 439 us: call(): pl.pallas_call(functools.partial(kernel, s), out_shape=list(outs), in_spe...]
where the time goes in v3:
time: 458 us; the launch traced here: 457 us
  Pallas kernels  442 us (97%)
  local copies, waits for them, and re-layouts  11 us (2%)
    pallas_call x1, Pallas kernels, call(): pl.pallas_call(functools.partial(kernel, s), out_shape=list(outs), in_spe...  439 us

profile of v3, /device:TPU:0, one launch (start us, length us, event | category | flops | bytes accessed | tf_op | source)
XLA Modules:
  0.0 456.8 jit_solution(7931337567250935535)
XLA Ops:
  0.6 3.0 shard_map.185
  3.7 438.8 %shard_map.186 = (bf16[256,1024]{1,0:T(8,128)(2,1)}, f32[256,1024]{1,0:T(8,128)}, f32[16,1024]{1,0:T(8,128)}, f32[2,3,128,256]{3,2,1,0:T(8,128)}, f32[2,128,256]...) custom-call(bf16[256,1024]{1,0:T(8,128)(2,1)} %refs_0_.1, ...), custom_call_target="tpu_custom_call" | custom-call | tf_op jit(solution)/shard_map/pallas_call | solution.py:1190
  442.5 0.0 copy-start.2
  442.5 0.0 copy-start.1
  442.6 0.0 copy-start
  442.6 1.4 slice_reduce_fusion
  444.7 0.8 fusion
  445.5 0.0 copy-start.3
  445.5 0.6 slice.20
  446.1 0.6 reshape.44
  446.8 1.9 copy.27
  448.6 2.3 copy.28
  450.9 2.1 copy.29
  453.0 0.0 copy-done.2
  453.0 0.7 copy.30
  453.7 0.0 copy-done.1
  453.7 1.0 copy.31
  454.7 0.0 copy-done
  454.7 1.0 copy.32
  455.7 0.0 copy-done.3
  (1 shorter events, 0.0 us)
Async XLA Ops:
  442.5 10.5 %copy-start.2 = (f32[2,128,256]{2,1,0:T(8,128)S(1)}, f32[2,128,256]{2,1,0:T(8,128)}, u32[]{:S(2)}) copy-start(f32[2,128,256]{2,1,0:T(8,128)} %get-tuple-element.56) | copy-start | bytes 786436
  442.5 11.2 %copy-start.1 = (f32[2,128,1024]{2,1,0:T(8,128)S(1)}, f32[2,128,1024]{2,1,0:T(8,128)}, u32[]{:S(2)}) copy-start(f32[2,128,1024]{2,1,0:T(8,128)} %get-tuple-element.57) | copy-start | bytes 3145732
  442.6 12.2 %copy-start = (f32[2,128,1024]{2,1,0:T(8,128)S(1)}, f32[2,128,1024]{2,1,0:T(8,128)}, u32[]{:S(2)}) copy-start(f32[2,128,1024]{2,1,0:T(8,128)} %get-tuple-element.58) | copy-start | bytes 3145732
  445.5 10.2 %copy-start.3 = (f32[2,2,1024]{2,1,0:T(2,128)}, f32[2,2,1024]{2,1,0:T(2,128)S(1)}, u32[]{:S(2)}) copy-start(f32[2,2,1024]{2,1,0:T(2,128)S(1)} %reshape.45) | copy-start | bytes 49156

commit v4 on v3

--- a/solution.py
+++ b/solution.py
@@ -618,7 +618,7 @@
     return (turned,) + tuple(w.reshape((s.L,) + cut + w.shape[2:]) for w in rest)
 
 
-BACK_FIRST, BACK_SECOND, BACK_LAST = 1, 2, 4
+BACK_FIRST, BACK_SECOND, BACK_LAST = 2, 4, 6
 SLOTS = 8
 OUT_RING = 4
 X_EARLY, X_LATE, X_DOWN, X_MIX = 0, 1, 2, 3
@@ -811,7 +811,7 @@
         tick(v)
 
     def drain():
-        @pl.loop(s.U + 4, s.U + max(BACK_LAST + 1, 4))
+        @pl.loop(s.U + 4, s.U + max(BACK_LAST, 4))
         def _(t):
             tick(t)
 
@@ -1199,31 +1199,53 @@
     return Outputs(*out)
 
 
+def finish_kernel(s, count, *refs):
+    sources, vector, results = refs[:count], refs[count], refs[count + 1:2 * count + 1]
+    gain, bias, top, log_max, log_mean, sems = refs[2 * count + 1:2 * count + 7]
+    held = refs[2 * count + 7:]
+    loads = [pltpu.make_async_copy(src, mid, sems.at[0, i]) for i, (src, mid) in enumerate(zip(sources, held))]
+    stores = [pltpu.make_async_copy(mid, dst, sems.at[1, i]) for i, (mid, dst) in enumerate(zip(held, results))]
+    for cp in loads:
+        cp.start()
+    for load, store in zip(loads, stores):
+        load.wait()
+        store.start()
+    for l in range(s.L):
+        gain[l] = vector[2 * l:2 * l + 2]
+        bias[l] = vector[2 * s.L + 2 * l:2 * s.L + 2 * l + 2]
+    top[...] = vector[4 * s.L - 1:4 * s.L]
+    logs = s.R * s.Z * s.T * s.D * s.L
+    log_mean[...] = jnp.sum(vector[4 * s.L:4 * s.L + 1, :128], axis=1, keepdims=True) / logs
+    log_max[...] = jnp.max(vector[4 * s.L + 1:4 * s.L + 2, :128], axis=1, keepdims=True)
+    for cp in stores:
+        cp.wait()
+
+
+def finish(s, got):
+    vmem = pl.BlockSpec(memory_space=pltpu.VMEM)
+    hbm = pl.BlockSpec(memory_space=pl.ANY)
+    shape = jax.ShapeDtypeStruct
+    large = (got.output, got.grad, got.g_in, got.g_mix, got.g_up, got.g_down)
+    return pl.pallas_call(
+        functools.partial(finish_kernel, s, len(large)),
+        out_shape=[shape(a.shape, a.dtype) for a in large] + [
+            shape((s.L, 2, s.D), F32), shape((s.L, 2, s.D), F32), shape((1, s.D), F32), shape((1, 1), F32), shape((1, 1), F32)],
+        in_specs=[hbm] * len(large) + [vmem],
+        out_specs=[hbm] * len(large) + [vmem] * 5,
+        scratch_shapes=[pltpu.SemaphoreType.DMA((2, len(large)))] + [pltpu.VMEM(a.shape, a.dtype) for a in large],
+        compiler_params=pltpu.CompilerParams(vmem_limit_bytes=61 * 1024 * 1024),
+    )(*large, got.vector)
+
+
 def local(mesh, tokens, cotangent, image_length, image_start, norm_gain, norm_bias, weight_in, weight_mix, weight_up,
           weight_down):
     s = sizes_of(mesh, tokens, weight_in, weight_up)
     weights = split_rows(s, weight_in, weight_mix, weight_up, weight_down)
     *coefs, gain, bias = weigh_units(s, image_length, image_start, norm_gain, norm_bias)
     got = call(s, Inputs(tokens, cotangent, gain, bias, *coefs, *weights))
-    vector = got.vector
-    grad_gain = vector[:2 * s.L].reshape(norm_gain.shape)
-    grad_bias = vector[2 * s.L:4 * s.L].reshape(norm_bias.shape)
-    heads = s.D // HD
-    log_mean = jnp.sum(vector[4 * s.L, :128]) / (HD * s.R * s.Z * s.T * heads * s.L)
-    log_max = jnp.max(vector[4 * s.L + 1, :128])
-    return (
-        got.output,
-        got.grad,
-        grad_gain,
-        grad_bias,
-        grad_bias[s.L - 1, 1],
-        jnp.transpose(got.g_in, (0, 2, 1, 3)),
-        got.g_mix,
-        got.g_up,
-        got.g_down,
-        log_max,
-        log_mean,
-    )
+    output, grad, g_in, g_mix, g_up, g_down, grad_gain, grad_bias, top, log_max, log_mean = finish(s, got)
+    return (output, grad, grad_gain, grad_bias, top.reshape(-1), jnp.transpose(g_in, (0, 2, 1, 3)), g_mix, g_up, g_down,
+            log_max.reshape(()), log_mean.reshape(()))
 
 
 def solution(mesh):

time: 458 us -> 441 us (0.963)
  local copies, waits for them, and re-layouts: 11 us -> 0 us
    unnamed x14 -> x0, local copies, waits for them, and re-layouts: 8.93 us -> none
    pallas_call x1, Pallas kernels: 439 us -> 431 us  [call(): pl.pallas_call(functools.partial(kernel, s), out_shape=list(outs), in_spe...]
    pallas_call x0 -> x1, Pallas kernels: none -> 5.56 us  [finish(): pl.pallas_call(functools.partial(finish_kernel, s, len(large)), out_shape...]
where the time goes in v4:
time: 441 us; the launch traced here: 440 us
  Pallas kernels  439 us (100%)
    pallas_call x1, Pallas kernels, call(): pl.pallas_call(functools.partial(kernel, s), out_shape=list(outs), in_spe...  431 us

profile of v4, /device:TPU:0, one launch (start us, length us, event | category | flops | bytes accessed | tf_op | source)
XLA Modules:
  0.0 440.0 jit_solution(17420598114748991302)
XLA Ops:
  0.6 3.0 shard_map.185
  3.7 430.6 %shard_map.186 = (bf16[256,1024]{1,0:T(8,128)(2,1)}, f32[256,1024]{1,0:T(8,128)}, f32[16,1024]{1,0:T(8,128)}, f32[2,3,128,256]{3,2,1,0:T(8,128)}, f32[2,128,256]...) custom-call(bf16[256,1024]{1,0:T(8,128)(2,1)} %refs_0_.1, ...), custom_call_target="tpu_custom_call" | custom-call | tf_op jit(solution)/shard_map/pallas_call | solution.py:1190
  434.3 5.6 %shard_map.187 = (bf16[256,1024]{1,0:T(8,128)(2,1)}, f32[256,1024]{1,0:T(8,128)}, f32[2,3,128,256]{3,2,1,0:T(8,128)}, f32[2,128,256]{2,1,0:T(8,128)}, f32[2,128,...) custom-call(bf16[256,1024]{1,0:T(8,128)(2,1)} %get-tuple-element.39., ...), custom_call_target="tpu_custom_call" | custom-call | tf_op jit(solution)/shard_map/pallas_call | solution.py:1229

commit v5 on v4

--- a/solution.py
+++ b/solution.py
@@ -150,22 +150,51 @@
         at = F.at[u, :, :, :, 1 - c]
         return remote(at, at, h.c_send.at[u % RING], h.c_recv.at[u], (r, z))
 
-    def z_landing(u):
-        return [
-            remote(piece.at[0, 0], F.at[u, k, y, x, c], h.z_send.at[u % RING, 0], h.z_recv.at[u, k], (r, z))
-            for k in range(s.Z - 1)
-        ]
+    reach = s.Z // 2
+
+    def straight(d):
+        return jnp.abs((z + d) % s.Z - z) <= reach
+
+    def z_begin(u):
+        for d, cp in zip(range(1, s.Z), z_copies(u)):
+            pl.when(straight(d))(cp.start)
+
+    def z_sent(u):
+        for d, cp in zip(range(1, s.Z), z_copies(u)):
+            pl.when(straight(d))(cp.wait_send)
+
+    def relays(u):
+        out = []
+        for e in range(1, reach):
+            to = jnp.where(z >= reach, z + e, z - e)
+            slot = jnp.where(z >= reach, reach - e - 1, reach + e - 1)
+            cp = remote(F.at[u, reach - 1, y, x, c], F.at[u, slot, y, x, c], h.relay_send.at[u % RING, e - 1],
+                        h.z_recv.at[u, slot], (r, to))
+            out.append(((to >= 0) & (to < s.Z), cp))
+        return out
+
+    def relay_begin(u):
+        z_landing(u, reach - 1).wait_recv()
+        for inner, cp in relays(u):
+            pl.when(inner)(cp.start)
+
+    def relay_sent(u):
+        for inner, cp in relays(u):
+            pl.when(inner)(cp.wait_send)
+
+    def z_landing(u, k):
+        return remote(piece.at[0, 0], F.at[u, k, y, x, c], h.z_send.at[u % RING, 0], h.z_recv.at[u, k], (r, z))
 
     def inside(u, what):
         pl.when((u >= 0) & (u < s.U))(functools.partial(what, u))
 
     def stage_z(u):
-        for cp in z_copies(u):
-            cp.start()
+        z_begin(u)
 
     def stage_first(u):
-        for cp in z_landing(u):
-            cp.wait_recv()
+        for k in range(s.Z - 1):
+            if k != reach - 1:
+                z_landing(u, k).wait_recv()
         for cp in first(u):
             cp.start()
 
@@ -184,8 +213,10 @@
         share_landing(u).wait_recv()
 
     def tick(t):
-        inside(t - RING, lambda u: [cp.wait_send() for cp in z_copies(u)] and None)
+        inside(t - RING, z_sent)
         inside(t, stage_z)
+        inside(t - 1 - RING, relay_sent)
+        inside(t - 1, relay_begin)
         inside(t - LAG_FIRST - RING, lambda u: [cp.wait_send() for cp in first(u)] and None)
         inside(t - LAG_FIRST, stage_first)
         inside(t - LAG_SECOND - RING, lambda u: [cp.wait_send() for cp in second(u)] and None)
@@ -402,6 +433,7 @@
         w_sem=dma((s.Z,)),
         z_send=dma((RING, s.Z - 1)),
         z_recv=dma((s.U, s.Z - 1)),
+        relay_send=dma((RING, max(s.Z // 2 - 1, 1))),
         x_send=dma((RING, 2, s.NX - 1)),
         x_recv=dma((s.U, 2, s.NX - 1)),
         y_send=dma((RING, 2, s.NY - 1)),
@@ -503,20 +535,11 @@
 
         lax.fori_loop(0, s.Z, local_state, 0)
         round_one()
-        tick(base + 3 + LAG_READY)
-        round_two()
-        tick(base + 4 + LAG_READY)
-        round_three()
-        tick(base + 5 + LAG_READY)
-        arrive()
-        keep_one(l, 7).start()
         causal = (lax.broadcasted_iota(jnp.int32, (s.T, s.T), 1) <= lax.broadcasted_iota(jnp.int32, (s.T, s.T), 0))
 
         def attend(p, carry):
-            k, i = p // s.NP, p % s.NP
             at = lanes(p, 128)
             query, key, value = h.qkv[0, :, at], h.qkv[1, :, at], h.qkv[2, :, at]
-            wide = query.astype(F32)
             value_ones = jnp.concatenate([value, tall], axis=1)
             zero = jnp.zeros_like(query)
             results = []
@@ -525,26 +548,43 @@
                 scores = dot(jnp.where(mine, query, zero), key, NT)
                 weights = jnp.where(causal, scores, 0.0).astype(BF)
                 results.append(dot(weights, value_ones))
+            h.acc[:, at] = jnp.where(first, results[0][:, :128], results[1][:, :128])
+            h.den[:, at] = jnp.where(first, results[0][:, 128:], results[1][:, 128:])
+            return carry
+
+        def look_back(p, carry):
+            k, i = p // s.NP, p % s.NP
+            at = lanes(p, 128)
+            query = h.qkv[0, :, at]
             state = unpack_state(h.r3[k, pl.ds(pl.multiple_of(i * HD, HD), HD), :], first)
             total = pick_row(h.r3[k, s.NP * HD:, :], i)
             square = jnp.zeros((128, 128), BF)
             right = jnp.concatenate(
                 [jnp.concatenate([state, square], axis=1), jnp.concatenate([square, ones], axis=1)], axis=0)
-            left = jnp.concatenate([query, (wide * total).astype(BF)], axis=1)
+            left = jnp.concatenate([query, (query.astype(F32) * total).astype(BF)], axis=1)
             earlier = dot(left, right)
-            num = jnp.where(first, results[0][:, :128], results[1][:, :128]) + earlier[:, :128]
-            den = jnp.where(first, results[0][:, 128:], results[1][:, 128:]) + earlier[:, 128:] + EPS_DEN
-            h.mixed[:, at] = (num / den).astype(BF)
+            den = h.den[:, at] + earlier[:, 128:] + EPS_DEN
+            h.mixed[:, at] = ((h.acc[:, at] + earlier[:, :128]) / den).astype(BF)
             h.den[:, at] = den
             logs = jnp.log(den)
             h.logs[0:1] += jnp.sum(logs, axis=0, keepdims=True)
             h.logs[1:2] = jnp.maximum(h.logs[1:2], jnp.max(logs, axis=0, keepdims=True))
             return carry
 
-        half = s.Z * s.NP // 2
-        lax.fori_loop(0, half, attend, 0)
-        tick(base + 6 + LAG_READY)
-        lax.fori_loop(half, s.Z * s.NP, attend, 0)
+        pairs = s.Z * s.NP
+        cut = [pairs * i // 4 for i in range(5)]
+        lax.fori_loop(cut[0], cut[1], attend, 0)
+        tick(base + 3 + LAG_READY)
+        round_two()
+        lax.fori_loop(cut[1], cut[2], attend, 0)
+        tick(base + 4 + LAG_READY)
+        round_three()
+        lax.fori_loop(cut[2], cut[3], attend, 0)
+        tick(base + 5 + LAG_READY)
+        lax.fori_loop(cut[3], cut[4], attend, 0)
+        arrive()
+        keep_one(l, 7).start()
+        lax.fori_loop(0, pairs, look_back, 0)
         settle()
         keep_one(l, 4).start()
         send_mixed(l).start()
@@ -555,7 +595,7 @@
         def mix(k, weight):
             h.acc[...] += dot(h.mixed[:, lanes(k, s.PC)], weight, NT)
 
-        with_unit(h.w_mix, l, 0, base + 3, mix)
+        with_unit(h.w_mix, l, 0, base + 3, mix, lambda: tick(base + 6 + LAG_READY))
         h.middle[...] = h.stream[...] + h.acc[...]
         keep_one(l, 6).start()
         normalize(l, 1, h.middle[...])
@@ -569,7 +609,8 @@
                 h.act[j, :, lanes(k, s.PC)] = (v * cdf).astype(BF)
                 h.slope[j, :, lanes(k, s.PC)] = (cdf + v * (ROOT_TAU * jnp.exp(-0.5 * v * v))).astype(BF)
 
-            with_unit(h.w_up, l, j, u, body, lambda: pl.when(j >= 3)(lambda: tick(u + LAG_READY)))
+            more = (l + 1 < s.L) | (j + 1 < s.NJ)
+            with_unit(h.w_up, l, j, u, body, lambda: pl.when(more)(lambda: tick(u + s.NJ - 1 + LAG_READY)))
             keep_act(l, j).start()
             keep_slope(l, j).start()
             send_act(l, j).start()
@@ -585,7 +626,7 @@
             def body(k, weight):
                 h.stream[...] += dot(h.act[j, :, lanes(k, s.PC)], weight, NT)
 
-            with_unit(h.w_down, l, j, u, body, lambda: tick(u + LAG_READY))
+            with_unit(h.w_down, l, j, u, body, lambda: pl.when(j == 0)(lambda: tick(u + s.NJ - 1 + LAG_READY)))
             return carry
 
         @pl.when(l + 1 < s.L)
@@ -621,6 +662,7 @@
 BACK_FIRST, BACK_SECOND, BACK_LAST = 2, 4, 6
 SLOTS = 8
 OUT_RING = 4
+UPS_IN_LOOP = 2
 X_EARLY, X_LATE, X_DOWN, X_MIX = 0, 1, 2, 3
 
 def backward_scratch(s):
@@ -676,6 +718,14 @@
     )
 
 
+def down_at(s, j):
+    return j + jnp.maximum(j - (s.NJ - UPS_IN_LOOP), 0) if not isinstance(j, int) else j + max(j - (s.NJ - UPS_IN_LOOP), 0)
+
+
+def up_at(s, j):
+    return s.NJ + j if j >= UPS_IN_LOOP else down_at(s, s.NJ - UPS_IN_LOOP + j) + 1
+
+
 def gradient_sums(s, h, r, z, y, x, c):
     half = s.PR // 2
     rows = (pl.ds(0, half), pl.ds(half, half))
@@ -774,8 +824,9 @@
         h.final[o] = total
         l, q = s.L - 1 - v // s.NU, v % s.NU
         wide = 2 * s.NJ
-        pl.when(q < s.NJ)(lambda: out_copy(h.g_down.at[l, :, lanes(q, s.PC)], o).start())
-        pl.when((q >= s.NJ) & (q < wide))(lambda: out_copy(h.g_up.at[l, :, lanes(q - s.NJ, s.PC)], o).start())
+        for j in range(s.NJ):
+            pl.when(q == down_at(s, j))(functools.partial(lambda to: out_copy(to, o).start(), h.g_down.at[l, :, lanes(j, s.PC)]))
+            pl.when(q == up_at(s, j))(functools.partial(lambda to: out_copy(to, o).start(), h.g_up.at[l, :, lanes(j, s.PC)]))
         pl.when(q == wide)(lambda: out_copy(h.g_mix.at[l], o).start())
         pl.when(q > wide)(lambda: out_copy(h.g_in.at[l, q - wide - 1], o).start())
 
@@ -791,10 +842,10 @@
             for cp in first(v):
                 cp.start()
 
+        inside(t - BACK_LAST, stage_out)
+        inside(t - BACK_SECOND, stage_last)
+        inside(t - BACK_FIRST, stage_second)
         inside(t, start)
-        inside(t - BACK_FIRST, stage_second)
-        inside(t - BACK_SECOND, stage_last)
-        inside(t - BACK_LAST, stage_out)
 
     def produce(v, which, own, sibling):
         b = v % SLOTS
@@ -899,10 +950,14 @@
         for cp in xt_sends(l, X_DOWN):
             cp.wait_recv()
 
+        def produce_up(j):
+            g_send(l, h.ug, h.ug_sib, j, j).wait_recv()
+            produce(base + up_at(s, j), X_LATE, h.ug.at[j], h.ug_sib.at[j])
+
         def feed_back(j, carry):
             for cp in act_loads(j):
                 cp.wait()
-            produce(base + j, X_DOWN, h.b_act.at[0], h.b_act.at[1])
+            produce(base + down_at(s, j), X_DOWN, h.b_act.at[0], h.b_act.at[1])
             slope_load(j).wait()
 
             def body(k, weight):
@@ -914,7 +969,7 @@
                     h.stream[...] += dot(h.b_act[0, :, at], weight, NT)
 
             u = unit + 4 + s.NJ + j
-            with_unit(h.w_down, l, j, u, body, lambda: pl.when(li == 0)(lambda: tick_weights(u + LAG_READY)))
+            with_unit(h.w_down, l, j, u, body, lambda: pl.when((li == 0) & (j < 2))(lambda: tick_weights(u + s.NJ - 2 + LAG_READY)))
 
             @pl.when(j + 1 < s.NJ)
             def _():
@@ -927,6 +982,8 @@
                 slope_load(j + 1).start()
 
             g_send(l, h.ug, h.ug_sib, j, j).start()
+            for i in range(UPS_IN_LOOP):
+                pl.when(j == s.NJ - UPS_IN_LOOP + i)(functools.partial(produce_up, i))
 
             def body_up(k, weight):
                 h.acc[...] += dot(h.ug[j, :, lanes(k, s.PC)], weight, NT)
@@ -934,12 +991,7 @@
             with_unit(h.w_up, l, j, unit + 4 + j, body_up)
             return carry
 
-        def produce_up(j):
-            g_send(l, h.ug, h.ug_sib, j, j).wait_recv()
-            produce(base + s.NJ + j, X_LATE, h.ug.at[j], h.ug_sib.at[j])
-
         lax.fori_loop(0, s.NJ, feed_back, 0)
-        produce_up(0)
         middle = get(h.k_middle.at[l], h.resid, 5)
         middle.start()
         for cp in xt_sends(l, X_DOWN):
@@ -980,12 +1032,6 @@
 
         lax.fori_loop(0, s.Z, local_state, 0)
         round_one()
-        produce_up(1)
-        round_two()
-        produce_up(2)
-        round_three()
-        lax.fori_loop(3, s.NJ, lambda j, carry: (produce_up(j), carry)[1], 0)
-        arrive()
         causal = (lax.broadcasted_iota(jnp.int32, (s.T, s.T), 1) <= lax.broadcasted_iota(jnp.int32, (s.T, s.T), 0))
         lane = lax.broadcasted_iota(jnp.int32, (1, 128), 1)
 
@@ -1000,12 +1046,9 @@
             value_ones = jnp.concatenate([value, tall], axis=1)
             rows = pl.ds(pl.multiple_of(i * HD, HD), HD)
             state = unpack_state(h.state[k, rows, :], first)
-            after = unpack_state(h.r3[k, rows, :], first)
             total = pick_row(h.state[k, s.NP * HD:, :], i)
-            total_after = pick_row(h.r3[k, s.NP * HD:, :], i)
-            value_grad = dot(key, after)
             query_grad = dot(num, state, NT) + slope * total
-            key_grad = dot(value, after, NT) + total_after
+            value_grad = key_grad = jnp.zeros_like(query_grad)
             for head in range(2):
                 mine = first if head == 0 else jnp.logical_not(first)
                 query_mine = jnp.where(mine, query, zero)
@@ -1019,14 +1062,34 @@
                 query_grad = query_grad + dot(score, key_mine)
                 key_grad = key_grad + dot(score, query_mine, TN)
             h.pg[0, :, at] = (query_grad * jnp.minimum(query.astype(F32), 1.0)).astype(BF)
+            h.dg[:, at] = key_grad
+            h.acc[:, at] = value_grad
+            return carry
+
+        def look_ahead(p, carry):
+            k, i = p // s.NP, p % s.NP
+            at = lanes(p, 128)
+            key, value = h.qkv[1, :, at], h.qkv[2, :, at]
+            after = unpack_state(h.r3[k, pl.ds(pl.multiple_of(i * HD, HD), HD), :], first)
+            total_after = pick_row(h.r3[k, s.NP * HD:, :], i)
+            key_grad = h.dg[:, at] + dot(value, after, NT) + total_after
             h.pg[1, :, at] = (key_grad * jnp.minimum(key.astype(F32), 1.0)).astype(BF)
-            h.pg[2, :, at] = value_grad.astype(BF)
-            return carry
-
-        half = s.Z * s.NP // 2
-        lax.fori_loop(0, half, attend_back, 0)
+            h.pg[2, :, at] = (h.acc[:, at] + dot(key, after)).astype(BF)
+            return carry
+
+        pairs = s.Z * s.NP
+        cut = [pairs * i // 4 for i in range(5)]
+        lax.fori_loop(cut[0], cut[1], attend_back, 0)
+        produce_up(2)
+        round_two()
+        lax.fori_loop(cut[1], cut[2], attend_back, 0)
+        produce_up(3)
+        round_three()
+        lax.fori_loop(cut[2], cut[3], attend_back, 0)
+        lax.fori_loop(cut[3], cut[4], attend_back, 0)
         produce(base + 2 * s.NJ, X_MIX, h.b_mixed.at[0], h.b_mixed.at[1])
-        lax.fori_loop(half, s.Z * s.NP, attend_back, 0)
+        arrive()
+        lax.fori_loop(0, pairs, look_ahead, 0)
         settle()
         for kind in range(3):
             g_send(l, h.pg, h.pg_sib, kind, s.NJ + kind).start()

time: 441 us -> 436 us (0.989)
  Pallas kernels: 439 us -> 434 us
    pallas_call x1, Pallas kernels: 431 us -> 425 us  [call(): pl.pallas_call(functools.partial(kernel, s), out_shape=list(outs), in_spe...]
where the time goes in v5:
time: 436 us; the launch traced here: 434 us
  Pallas kernels  434 us (100%)
    pallas_call x1, Pallas kernels, call(): pl.pallas_call(functools.partial(kernel, s), out_shape=list(outs), in_spe...  425 us

profile of v5, /device:TPU:0, one launch (start us, length us, event | category | flops | bytes accessed | tf_op | source)
XLA Modules:
  0.0 434.4 jit_solution(14700421193603939386)
XLA Ops:
  0.6 3.0 shard_map.185
  3.7 425.0 %shard_map.186 = (bf16[256,1024]{1,0:T(8,128)(2,1)}, f32[256,1024]{1,0:T(8,128)}, f32[16,1024]{1,0:T(8,128)}, f32[2,3,128,256]{3,2,1,0:T(8,128)}, f32[2,128,256]...) custom-call(bf16[256,1024]{1,0:T(8,128)(2,1)} %refs_0_.1, ...), custom_call_target="tpu_custom_call" | custom-call | tf_op jit(solution)/shard_map/pallas_call | solution.py:1253
  428.7 5.6 %shard_map.187 = (bf16[256,1024]{1,0:T(8,128)(2,1)}, f32[256,1024]{1,0:T(8,128)}, f32[2,3,128,256]{3,2,1,0:T(8,128)}, f32[2,128,256]{2,1,0:T(8,128)}, f32[2,128,...) custom-call(bf16[256,1024]{1,0:T(8,128)(2,1)} %get-tuple-element.39., ...), custom_call_target="tpu_custom_call" | custom-call | tf_op jit(solution)/shard_map/pallas_call | solution.py:1292

commit v6 on v5

--- a/solution.py
+++ b/solution.py
@@ -1206,14 +1206,15 @@
     for cp in pieces:
         cp.start()
     greet(s, r, z)
-    for cp in pieces:
-        cp.wait()
+    pieces[0].wait()
     tick_weights, drain_weights = weight_gather(s, h, r, z, y, x, c)
     with_unit = unit_reader(s, h)
     sums = gradient_sums(s, h, r, z, y, x, c)
     early, backward = backward_part(s, h, spots, tick_weights, with_unit, sums)
 
     def before():
+        for cp in pieces[1:]:
+            cp.wait()
         h.vec[...] = jnp.zeros_like(h.vec)
         early()
 

time: 436 us -> 436 us (level)
  no operation moved by 1% of the time
where the time goes in v6:
time: 436 us; the launch traced here: 434 us
  Pallas kernels  434 us (100%)
    pallas_call x1, Pallas kernels, call(): pl.pallas_call(functools.partial(kernel, s), out_shape=list(outs), in_spe...  425 us

profile of v6, /device:TPU:0, one launch (start us, length us, event | category | flops | bytes accessed | tf_op | source)
XLA Modules:
  0.0 434.4 jit_solution(17289132730161748410)
XLA Ops:
  0.6 3.0 shard_map.185
  3.7 425.0 %shard_map.186 = (bf16[256,1024]{1,0:T(8,128)(2,1)}, f32[256,1024]{1,0:T(8,128)}, f32[16,1024]{1,0:T(8,128)}, f32[2,3,128,256]{3,2,1,0:T(8,128)}, f32[2,128,256]...) custom-call(bf16[256,1024]{1,0:T(8,128)(2,1)} %refs_0_.1, ...), custom_call_target="tpu_custom_call" | custom-call | tf_op jit(solution)/shard_map/pallas_call | solution.py:1254
  428.7 5.6 %shard_map.187 = (bf16[256,1024]{1,0:T(8,128)(2,1)}, f32[256,1024]{1,0:T(8,128)}, f32[2,3,128,256]{3,2,1,0:T(8,128)}, f32[2,128,256]{2,1,0:T(8,128)}, f32[2,128,...) custom-call(bf16[256,1024]{1,0:T(8,128)(2,1)} %get-tuple-element.39., ...), custom_call_target="tpu_custom_call" | custom-call | tf_op jit(solution)/shard_map/pallas_call | solution.py:1293
